TPU v7x, 32 devices: a whole 2x2x4 slice. The times are simulated.
32 devices in a mesh: sec: 4 (over y, x), term: 8 (over z, core).
Axes of the slice: x: 2, y: 2, z: 4, core: 2. Of those that a mesh axis runs over, the one named last changes fastest.
Arguments:
- psi: bfloat16 [8, 2, 512, 512], P('sec'), may hold values from -6 to 6
- left_ops: bfloat16 [8, 8, 512, 512], P('term', 'sec'), may hold values from -0.25 to 0.25
- right_ops: bfloat16 [8, 8, 512, 512], P('term', 'sec'), may hold values from -0.09375 to 0.09375
- shift: int32 [8], P('term'), may hold values from -2 to 2, as said below
- live: int32 [8], P('term'), may hold values 0 or 1
Outputs:
- sigma: bfloat16 [8, 2, 512, 512], P('sec', None, 'term')
Inputs may be any that keep to these rules, and one draw needn't show every extreme that they name: `shift`: every draw holds both -2 and 2.
All inputs are finite; a program needn't handle non-finite values. No bound on the sum of `live` on one device may be relied on, other than what follows from the above.
Results may differ from a plain program's by a relative error of at most 0.0049.
Values may be sent and summed in bfloat16 or wider, within the bound.
No kernel may reach another device: no remote copies, remote signals or barrier semaphores. Data moves between devices by JAX's collectives and lax.ppermute only.
A program may use at most 64 MiB of HBM per device.

v0:
```python
import jax
import jax.numpy as jnp
from jax import lax
from jax.sharding import PartitionSpec as P

DQ = 2


def padded_2(block, sides, width):
    for axis, dim in sides:
        count = lax.axis_size(axis)
        forward = [(i, i + 1) for i in range(count - 1)]
        backward = [(target, source) for source, target in forward]
        low = lax.ppermute(
            lax.slice_in_dim(block, block.shape[dim] - width, None, axis=dim), axis, forward
        )
        high = lax.ppermute(lax.slice_in_dim(block, 0, width, axis=dim), axis, backward)
        block = jnp.concatenate([low, block, high], axis=dim)
    return block


def local(psi, left_ops, right_ops, shift, live):
    sec_count = psi.shape[0]
    padded = padded_2(psi, (("sec", 0),), DQ)
    left_rows = left_ops[0]
    block = lax.dynamic_slice_in_dim(padded, DQ - shift[0], sec_count, 0)
    inner = jnp.einsum(
        "sab,svbc->asvc", left_rows, block, preferred_element_type=jnp.float32
    ).astype(jnp.bfloat16)
    acc = jnp.einsum(
        "asvc,sdc->asvd", inner, right_ops[0], preferred_element_type=jnp.float32
    ) * live[0].astype(jnp.float32)
    summed = lax.psum_scatter(acc, "term", scatter_dimension=0, tiled=True)
    return jnp.transpose(summed, (1, 2, 0, 3)).astype(jnp.bfloat16)


def solution(mesh):
    in_specs = (
        P("sec", None, None, None),
        P("term", "sec", None, None),
        P("term", "sec", None, None),
        P("term"),
        P("term"),
    )
    out_specs = P("sec", None, "term", None)
    return jax.shard_map(local, mesh=mesh, in_specs=in_specs, out_specs=out_specs, check_vma=False)
```

profile of v0, /device:TPU:1, one launch (start us, length us, event | category | flops | bytes accessed | tf_op | source)
XLA Modules:
  0.0 166.0 jit_solution(151749420642540995)
XLA Ops:
  6.5 0.0 copy-start
  6.5 0.0 reduce-scatter.2.cloned.1.call-start
  6.5 4.2 %collective-permute-start = (bf16[2,2,512,512]{3,2,1,0:T(8,128)(2,1)}, bf16[2,2,512,512]{3,2,1,0:T(8,128)(2,1)S(1)}, u32[]{:S(2)}, u32[]{:S(2)}) collective-permute-start(bf16[2,2,512,512]{3,2,1,0:T(8,128)(2,1)} %param.5), channel_id=1, source_target_pairs={{0,8},{8,16},{16,24},{1,9},{9,17},{17,25},{2,10},{10,18},{18,26},{... | collective-permute-start | bytes 6291464 | tf_op jit(solution)/shard_map/ppermute | solution.py:14
  10.7 1.3 collective-permute-start.1
  13.3 41.9 %collective-permute-done = bf16[2,2,512,512]{3,2,1,0:T(8,128)(2,1)S(1)} collective-permute-done((bf16[2,2,512,512]{3,2,1,0:T(8,128)(2,1)}, bf16[2,2,512,512]{3,2,1,0:T(8,128)(2,1)S(1)}, u32[]{:S(2)}, u32[]{:S(2)}) %collective-permute-start) | collective-permute-done | bytes 2097184 | tf_op jit(solution)/shard_map/ppermute | solution.py:14
  55.2 46.9 %collective-permute-done.1 = bf16[2,2,512,512]{3,2,1,0:T(8,128)(2,1)} collective-permute-done((bf16[2,2,512,512]{3,2,1,0:T(8,128)(2,1)}, bf16[2,2,512,512]{3,2,1,0:T(8,128)(2,1)}, u32[]{:S(2)}, u32[]{:S(2)}) %collective-permute-start.1) | collective-permute-done | bytes 2097184 | tf_op jit(solution)/shard_map/ppermute | solution.py:17
  102.1 0.0 copy-done
  102.1 5.8 %multiply_bitcast_fusion = f32[512,2,2,512]{3,0,2,1:T(8,128)} fusion(f32[]{:T(128)} %bitcast.9, s32[]{:T(128)S(6)} %select_n.3, bf16[2,2,512,512]{3,2,1,0:T(8,128)(2,1)S(1)} %collective-permute-done, bf16[2,2,512,512]{3,2,1,0:T(8,128)(2,1)} %param.5, bf16[2,2,512,512]{3,2,1,0:T(8,128)(2,1)} %collective-permute-done.1, ...), kind=kOutput, calls=%fused_computation.3 | convolution fusion | flops 2155872256 | bytes 12582920 | tf_op jit(solution)/shard_map/asvc,sdc->asvd/dot_general | solution.py:30
  107.9 0.0 reduce-scatter.2.cloned.1.call-update
  107.9 49.5 %reduce-scatter.2.cloned.1.call-done = f32[64,2,2,512]{3,0,2,1:T(8,128)} async-done(((f32[512,2,2,512]{3,0,2,1:T(8,128)}), f32[64,2,2,512]{3,0,2,1:T(8,128)}) %reduce-scatter.2.cloned.1.call-update) | async-done | bytes 524304 | tf_op jit(solution)/shard_map/reduce_scatter | solution.py:33
  157.4 1.8 %convert_bitcast_fusion = bf16[2,2,64,512]{3,2,1,0:T(8,128)(2,1)} fusion(f32[64,2,2,512]{3,0,2,1:T(8,128)} %reduce-scatter.2.cloned.1.call-done), kind=kLoop, calls=%fused_computation.11 | loop fusion | flops 131072 | bytes 786432 | tf_op jit(solution)/shard_map/convert_element_type | solution.py:34
Async XLA Ops:
  6.5 95.6 %copy-start = (bf16[1,2,512,512]{3,2,1,0:T(8,128)(2,1)S(1)}, bf16[1,2,512,512]{3,2,1,0:T(8,128)(2,1)}, u32[]{:S(2)}) copy-start(bf16[1,2,512,512]{3,2,1,0:T(8,128)(2,1)} %param.7) | copy-start | bytes 3145732
  6.5 150.8 %reduce-scatter.2.cloned.1.call-start = ((), (), s32[]{:S(2)}) async-start(), calls=%async_computation.1 | async-start | bytes 4718592 | tf_op jit(solution)/shard_map/reduce_scatter | solution.py:33
  6.5 48.7 %collective-permute-start = (bf16[2,2,512,512]{3,2,1,0:T(8,128)(2,1)}, bf16[2,2,512,512]{3,2,1,0:T(8,128)(2,1)S(1)}, u32[]{:S(2)}, u32[]{:S(2)}) collective-permute-start(bf16[2,2,512,512]{3,2,1,0:T(8,128)(2,1)} %param.5), channel_id=1, source_target_pairs={{0,8},{8,16},{16,24},{1,9},{9,17},{17,25},{2,10},{10,18},{18,26},{... | collective-permute-start | bytes 6291464 | tf_op jit(solution)/shard_map/ppermute | solution.py:14
  10.7 91.3 %collective-permute-start.1 = (bf16[2,2,512,512]{3,2,1,0:T(8,128)(2,1)}, bf16[2,2,512,512]{3,2,1,0:T(8,128)(2,1)}, u32[]{:S(2)}, u32[]{:S(2)}) collective-permute-start(bf16[2,2,512,512]{3,2,1,0:T(8,128)(2,1)} %param.5), channel_id=1, source_target_pairs={{8,0},{16,8},{24,16},{9,1},{17,9},{25,17},{10,2},{18,10},{26,18},{... | collective-permute-start | bytes 6291464 | tf_op jit(solution)/shard_map/ppermute | solution.py:17
Sparse Core Ops, SparseCore 0:
  108.0 49.3 reduce-scatter.1
where the time goes:
time: 169 us; the launch traced here: 166 us
  waiting for transfers between devices  138 us (82%)
  between operations  14.7 us (9%)
  matrix products  5.77 us (3%)
  starting transfers between devices  5.49 us (3%)
  other arithmetic  1.77 us (1%)
    reduce_scatter x1, waiting for transfers between devices, local(): summed = lax.psum_scatter(acc, 'term', scatter_dimension=0, tiled=True)  49.5 us
    ppermute x1, waiting for transfers between devices, padded_2(): lax.ppermute(lax.slice_in_dim(block, 0, width, axis=dim), axis, backward)  46.9 us
    ppermute x1, waiting for transfers between devices, padded_2(): lax.ppermute(lax.slice_in_dim(block, block.shape[dim] - width, None, axis...  41.9 us
    dot_general x1, matrix products, local(): jnp.einsum('asvc,sdc->asvd', inner, right_ops[0], preferred_element_type=...  5.77 us
    ppermute x1, starting transfers between devices, padded_2(): lax.ppermute(lax.slice_in_dim(block, block.shape[dim] - width, None, axis...  4.2 us
  transfers between devices with their start and end apart: 3, of which 3 were waited for; matrix products, arithmetic and copies ran while one was open for 0% of the time, Pallas kernels for 0%

commit v1 on v0

v1 whole, which is shorter than its diff:
```python
import functools

import jax
import jax.numpy as jnp
from jax import lax
from jax.experimental import pallas as pl
from jax.experimental.pallas import tpu as pltpu
from jax.sharding import PartitionSpec as P

DQ = 2
HALVES = 2


def piece_kernel(first_slot, slots, meta, *refs):
    halo = refs[: slots * HALVES]
    psi, left0, right0, left1, right1, keep, send, src, left, right, total, sem = refs[slots * HALVES :]
    rows = src.shape[1] // HALVES
    sector, core, bit = meta[0], meta[1], meta[2]

    def operand_copies(term):
        pair = ((left0, right0), (left1, right1))[term]
        return (
            pltpu.make_async_copy(pair[0].at[0, sector], left.at[term], sem.at[term, HALVES]),
            pltpu.make_async_copy(pair[1].at[0, sector], right.at[term], sem.at[term, HALVES + 1]),
        )

    def source_copy(term, ref, half):
        return pltpu.make_async_copy(ref, src.at[term, pl.ds(half * rows, rows)], sem.at[term, half])

    for term in range(2):
        slot = meta[3 + term]
        for k in range(slots):
            @pl.when(slot == k)
            def _(k=k, term=term):
                for half in range(HALVES):
                    source_copy(term, halo[k * HALVES + half], half).start()
        for own in range(2):
            @pl.when(slot == slots + own)
            def _(own=own, term=term):
                for half in range(HALVES):
                    part = psi.at[own, core, pl.ds(half * rows, rows)]
                    source_copy(term, part, half).start()
        for copy in operand_copies(term):
            copy.start()

    for term in range(2):
        for half in range(HALVES):
            source_copy(term, psi.at[0, 0, pl.ds(0, rows)], half).wait()
        for copy in operand_copies(term):
            copy.wait()
        weight = meta[5 + term].astype(jnp.float32)
        for half in range(2):
            part = pl.ds(half * (left.shape[1] // 2), left.shape[1] // 2)
            inner = jnp.dot(left[term, part], src[term], preferred_element_type=jnp.float32).astype(jnp.bfloat16)
            outer = lax.dot_general(
                inner, right[term], (((1,), (1,)), ((), ())), preferred_element_type=jnp.float32
            ) * weight
            if term == 0:
                total[part] = outer
            else:
                total[part] += outer

    count, height = keep.shape[0], keep.shape[1]
    for k in range(count):
        at = pl.multiple_of((2 * k + bit) * height, height)
        keep[k] = total[pl.ds(at, height)].astype(keep.dtype)
        at = pl.multiple_of((2 * k + 1 - bit) * height, height)
        send[k] = total[pl.ds(at, height)].astype(send.dtype)


def piece(meta, halo, psi, left0, right0, left1, right1, chips):
    size = psi.shape[-1]
    slots = len(halo)
    flat = [part for block in halo for part in block]
    out = (chips // 2, size // chips, size)
    anywhere = pl.BlockSpec(memory_space=pl.ANY)
    return pl.pallas_call(
        functools.partial(piece_kernel, 0, slots),
        out_shape=(jax.ShapeDtypeStruct(out, jnp.float32), jax.ShapeDtypeStruct(out, jnp.bfloat16)),
        in_specs=[pl.BlockSpec(memory_space=pltpu.SMEM)] + [anywhere] * (len(flat) + 5),
        out_specs=(pl.BlockSpec(memory_space=pltpu.VMEM),) * 2,
        scratch_shapes=[
            pltpu.VMEM((2, size, size), jnp.bfloat16),
            pltpu.VMEM((2, size, size), jnp.bfloat16),
            pltpu.VMEM((2, size, size), jnp.bfloat16),
            pltpu.VMEM((size, size), jnp.float32),
            pltpu.SemaphoreType.DMA((2, HALVES + 2)),
        ],
        compiler_params=pltpu.CompilerParams(vmem_limit_bytes=16 * 1024 * 1024),
        cost_estimate=pl.CostEstimate(flops=8 * size**3, bytes_accessed=10 * size * size, transcendentals=0),
        name="piece",
    )(meta, *flat, psi, left0, right0, left1, right1)


def halving(keep, send, z, rounds):
    for step in range(rounds):
        pairs = [(d, d ^ (2 << step)) for d in range(lax.axis_size("term"))]
        got = lax.ppermute(send, "term", pairs)
        total = keep + got.astype(jnp.float32)
        if step == rounds - 1:
            return total[0]
        total = total.reshape(total.shape[0] // 2, 2, *total.shape[1:])
        bit = (z >> (step + 1)) & 1
        keep = lax.dynamic_index_in_dim(total, bit, 1, False)
        send = lax.dynamic_index_in_dim(total, 1 - bit, 1, False).astype(jnp.bfloat16)


def local(psi, left_ops, right_ops, shift, live):
    secs, terms = lax.axis_size("sec"), lax.axis_size("term")
    chips = terms // 2
    rounds = chips.bit_length() - 1
    size = psi.shape[-1]
    i, term = lax.axis_index("sec"), lax.axis_index("term")
    core, z = term % 2, term // 2
    odd = i % 2
    cores = [(d, d ^ 1) for d in range(terms)]
    xswap = [(d, d ^ 1) for d in range(secs)]

    mine = lax.dynamic_index_in_dim(psi, core, 1, False)
    order = (lax.dynamic_index_in_dim(mine, odd, 0, False), lax.dynamic_index_in_dim(mine, 1 - odd, 0, False))
    parts = [jnp.split(block, HALVES, axis=0) for block in order]
    near = [[lax.ppermute(p, "sec", xswap) for p in block] for block in parts]
    left1 = lax.ppermute(left_ops, "term", cores)
    right1 = lax.ppermute(right_ops, "term", cores)
    other = lax.ppermute(jnp.concatenate([shift, live]), "term", cores)
    if secs == 4:
        yswap = [(d, d ^ 2) for d in range(secs)]
        far = [[lax.ppermute(p, "sec", yswap) for p in block] for block in near]
    else:
        nexts = [(d, d + 1) for d in range(1, secs - 1, 2)]
        nexts = nexts + [(b, a) for a, b in nexts]
        far = [[lax.ppermute(p, "sec", nexts) for p in block] for block in parts]

    shifts = jnp.stack([shift[0], other[0]])
    lives = jnp.stack([live[0], other[1]])
    sign = 2 * odd - 1
    outs = []
    for s in range(2):
        sector = jnp.where(odd == 1, s, 1 - s)
        rel = sector - shifts
        there = ((rel >= 0) | (i > 0)) & ((rel <= 1) | (i < secs - 1))
        place = s - sign * shifts
        if s == 0:
            halo = (near[0], near[1], far[0])
            slot = jnp.where(place == 2, 2, place + 2)
        else:
            halo = (near[1], far[0], far[1])
            slot = jnp.where(place >= 2, place - 1, place + 1)
        slot = jnp.where((rel == 0) | (rel == 1), 3 + rel, slot)
        weight = jnp.where(there, lives, 0)
        meta = jnp.concatenate([jnp.stack([sector, core, z % 2]), slot, weight]).astype(jnp.int32)
        keep, send = piece(meta, halo, psi, left_ops, right_ops, left1, right1, chips)
        total = halving(keep, send, z, rounds).reshape(2, size // terms, size)
        own = lax.dynamic_index_in_dim(total, core, 0, False).astype(jnp.bfloat16)
        off = lax.dynamic_index_in_dim(total, 1 - core, 0, False).astype(jnp.bfloat16)
        got = lax.ppermute(off, "term", cores)
        outs.append(jnp.where(core == 0, jnp.stack([own, got]), jnp.stack([got, own])))
    return jnp.where(odd == 1, jnp.stack(outs), jnp.stack(outs[::-1]))


def solution(mesh):
    in_specs = (
        P("sec", None, None, None),
        P("term", "sec", None, None),
        P("term", "sec", None, None),
        P("term"),
        P("term"),
    )
    out_specs = P("sec", None, "term", None)
    return jax.shard_map(local, mesh=mesh, in_specs=in_specs, out_specs=out_specs, check_vma=False)
```

time: 169 us -> 68.5 us (0.41); the launches traced: 166 us -> 67.8 us
  waiting for transfers between devices: 138 us -> 18.5 us
  starting transfers between devices: 5.49 us -> 25.3 us
  between operations: 14.7 us -> 1.42 us
  local copies, waits for them, and re-layouts: 0.01 us -> 11 us
  Pallas kernels: 0 us -> 7.61 us
  matrix products: 5.77 us -> 0 us
  other arithmetic: 1.77 us -> 3.95 us
    ppermute x2 -> x17, waiting for transfers between devices: 88.8 us -> 18.5 us  [the longest x4 12.5 us: local(): near = [[lax.ppermute(p, 'sec', xswap) for p in block] for block in parts]]
    reduce_scatter x1 -> x0, waiting for transfers between devices: 49.5 us -> none  [local(): summed = lax.psum_scatter(acc, 'term', scatter_dimension=0, tiled=True)]
    ppermute x2 -> x17, starting transfers between devices: 5.49 us -> 25.3 us  [the longest x2 8.36 us: local(): got = lax.ppermute(off, 'term', cores)]
    unnamed x2 -> x20, local copies, waits for them, and re-layouts: 0.01 us -> 7.89 us
    pallas_call x0 -> x2, Pallas kernels: none -> 7.61 us  [piece(): pl.pallas_call(functools.partial(piece_kernel, 0, slots), out_shape=(jax....]
    dot_general x1 -> x0, matrix products: 5.77 us -> none  [local(): jnp.einsum('asvc,sdc->asvd', inner, right_ops[0], preferred_element_type=...]
    select_n x0 -> x5, other arithmetic: none -> 2.71 us  [the longest x1 1.31 us: local(): weight = jnp.where(there, lives, 0)]
    split x0 -> x1, local copies, waits for them, and re-layouts: none -> 2.28 us  [local(): parts = [jnp.split(block, HALVES, axis=0) for block in order]]
  transfers between devices with their start and end apart: 3 -> 17, of which waited for: 3 -> 9; matrix products, arithmetic and copies ran while one was open for 0% -> 9% of each run, Pallas kernels for 0% -> 11%
where the time goes in v1:
time: 68.5 us; the launch traced here: 67.8 us
  starting transfers between devices  25.3 us (37%)
  waiting for transfers between devices  18.5 us (27%)
  local copies, waits for them, and re-layouts  11 us (16%)
  Pallas kernels  7.61 us (11%)
  other arithmetic  3.95 us (6%)
  between operations  1.42 us (2%)
    ppermute x4, waiting for transfers between devices, local(): near = [[lax.ppermute(p, 'sec', xswap) for p in block] for block in parts]  12.5 us
    ppermute x2, starting transfers between devices, local(): got = lax.ppermute(off, 'term', cores)  8.36 us
    unnamed x20, local copies, waits for them, and re-layouts  7.89 us
    pallas_call x2, Pallas kernels, piece(): pl.pallas_call(functools.partial(piece_kernel, 0, slots), out_shape=(jax....  7.61 us
    ppermute x4, starting transfers between devices, halving(): got = lax.ppermute(send, 'term', pairs)  6.84 us
    ppermute x4, starting transfers between devices, local(): near = [[lax.ppermute(p, 'sec', xswap) for p in block] for block in parts]  5.05 us
    ppermute x4, starting transfers between devices, local(): far = [[lax.ppermute(p, 'sec', yswap) for p in block] for block in near]  3.71 us
    ppermute x4, waiting for transfers between devices, halving(): got = lax.ppermute(send, 'term', pairs)  3.18 us
  transfers between devices with their start and end apart: 17, of which 9 were waited for; matrix products, arithmetic and copies ran while one was open for 9% of the time, Pallas kernels for 11%

profile of v1, /device:TPU:1, one launch (start us, length us, event | category | flops | bytes accessed | tf_op | source)
XLA Modules:
  0.0 67.8 jit_solution(2860710573183281662)
XLA Ops:
  0.5 2.3 %dynamic-slice_bitcast_fusion.2 = (bf16[256,512]{1,0:T(8,128)(2,1)}, bf16[256,512]{1,0:T(8,128)(2,1)}, bf16[256,512]{1,0:T(8,128)(2,1)}, bf16[256,512]{1,0:T(8,128)(2,1)}) fusion(bf16[2,2,512,512]{3,2,1,0:T(8,128)(2,1)} %refs_6_.3, s32[]{:T(128)S(6)} %select_n.127, s32[]{:T(128)S(6)} %select_n.129, s32[]{:T(128)S(6)} %add.96, s32[]{:T(128)S(6)} %select_n.131), kind=kLoop, calls=%fused_computation.4 | loop fusion | bytes 2097168 | tf_op jit(solution)/shard_map/split | solution.py:121
  2.8 2.2 %collective-permute-start.1 = (bf16[256,512]{1,0:T(8,128)(2,1)}, bf16[256,512]{1,0:T(8,128)(2,1)}, u32[]{:S(2)}, u32[]{:S(2)}) collective-permute-start(bf16[256,512]{1,0:T(8,128)(2,1)} %get-tuple-element.17), channel_id=1, source_target_pairs={{0,8},{8,0},{16,24},{24,16},{1,9},{9,1},{17,25},{25,17},{2,10},{10... | collective-permute-start | bytes 786440 | tf_op jit(solution)/shard_map/ppermute | solution.py:122
  8.0 1.7 %collective-permute-start.3 = (bf16[256,512]{1,0:T(8,128)(2,1)}, bf16[256,512]{1,0:T(8,128)(2,1)S(1)}, u32[]{:S(2)}, u32[]{:S(2)}) collective-permute-start(bf16[256,512]{1,0:T(8,128)(2,1)} %get-tuple-element.16), channel_id=1, source_target_pairs={{0,8},{8,0},{16,24},{24,16},{1,9},{9,1},{17,25},{25,17},{2,10},{10... | collective-permute-start | bytes 786440 | tf_op jit(solution)/shard_map/ppermute | solution.py:122
  10.3 1.1 %collective-permute-done.1.refs_0_ = bf16[256,512]{1,0:T(8,128)(2,1)} collective-permute-done((bf16[256,512]{1,0:T(8,128)(2,1)}, bf16[256,512]{1,0:T(8,128)(2,1)}, u32[]{:S(2)}, u32[]{:S(2)}) %collective-permute-start.1) | collective-permute-done | bytes 262176 | tf_op jit(solution)/shard_map/ppermute | solution.py:122
  11.4 1.1 %collective-permute-start.4 = (bf16[256,512]{1,0:T(8,128)(2,1)}, bf16[256,512]{1,0:T(8,128)(2,1)}, u32[]{:S(2)}, u32[]{:S(2)}) collective-permute-start(bf16[256,512]{1,0:T(8,128)(2,1)} %get-tuple-element.18), channel_id=1, source_target_pairs={{0,8},{8,0},{16,24},{24,16},{1,9},{9,1},{17,25},{25,17},{2,10},{10... | collective-permute-start | bytes 786440 | tf_op jit(solution)/shard_map/ppermute | solution.py:122
  12.6 4.5 %collective-permute-done.2.refs_1_ = bf16[256,512]{1,0:T(8,128)(2,1)} collective-permute-done((bf16[256,512]{1,0:T(8,128)(2,1)}, bf16[256,512]{1,0:T(8,128)(2,1)}, u32[]{:S(2)}, u32[]{:S(2)}) %collective-permute-start.2) | collective-permute-done | bytes 262176 | tf_op jit(solution)/shard_map/ppermute | solution.py:122
  17.0 1.2 %collective-permute-start.5 = (bf16[256,512]{1,0:T(8,128)(2,1)}, bf16[256,512]{1,0:T(8,128)(2,1)}, u32[]{:S(2)}, u32[]{:S(2)}) collective-permute-start(bf16[256,512]{1,0:T(8,128)(2,1)} %collective-permute-done.1.refs_0_), channel_id=1, source_target_pairs={{0,16},{8,24},{16,0},{24,8},{1,17},{9,25},{17,1},{25,9},{2,18},{10... | collective-permute-start | bytes 786440 | tf_op jit(solution)/shard_map/ppermute | solution.py:128
  18.2 4.4 %collective-permute-done.3.refs_2_.refs_0_ = bf16[256,512]{1,0:T(8,128)(2,1)S(1)} collective-permute-done((bf16[256,512]{1,0:T(8,128)(2,1)}, bf16[256,512]{1,0:T(8,128)(2,1)S(1)}, u32[]{:S(2)}, u32[]{:S(2)}) %collective-permute-start.3) | collective-permute-done | bytes 262176 | tf_op jit(solution)/shard_map/ppermute | solution.py:122
  23.7 1.3 %and_select_fusion.1 = (s32[2]{0:T(128)S(1)}, s32[2]{0:T(128)S(1)}) fusion(pred[]{:T(512)S(6)} %lt.50, pred[]{:T(512)S(6)} %gt.4, s32[]{:T(128)} %select_n.120, s32[1]{0:T(128)} %get-tuple-element.27, s32[1]{0:T(128)S(6)} %copy.7, s32[1]{0:T(128)} %get-tuple-element.26, s32[1]{0:T(128)S(6)} %copy.6), kind=kLoop, calls=%fused_computation.24 | loop fusion | flops 18 | bytes 38 | tf_op jit(solution)/shard_map/jit(_where)/select_n | solution.py:150
  25.7 2.5 %collective-permute-done.4.refs_3_.refs_1_ = bf16[256,512]{1,0:T(8,128)(2,1)} collective-permute-done((bf16[256,512]{1,0:T(8,128)(2,1)}, bf16[256,512]{1,0:T(8,128)(2,1)}, u32[]{:S(2)}, u32[]{:S(2)}) %collective-permute-start.4) | collective-permute-done | bytes 262176 | tf_op jit(solution)/shard_map/ppermute | solution.py:122
  28.3 1.2 %collective-permute-start.12 = (bf16[256,512]{1,0:T(8,128)(2,1)S(1)}, bf16[256,512]{1,0:T(8,128)(2,1)}, u32[]{:S(2)}, u32[]{:S(2)}) collective-permute-start(bf16[256,512]{1,0:T(8,128)(2,1)S(1)} %collective-permute-done.3.refs_2_.refs_0_), channel_id=1, source_target_pairs={{0,16},{8,24},{16,0},{24,8},{1,17},{9,25},{17,1},{25,9},{2,18},{10... | collective-permute-start | bytes 786440 | tf_op jit(solution)/shard_map/ppermute | solution.py:128
  30.7 1.2 %copy-done.1 = bf16[1,2,512,512]{3,2,1,0:T(8,128)(2,1)S(1)} copy-done((bf16[1,2,512,512]{3,2,1,0:T(8,128)(2,1)S(1)}, bf16[1,2,512,512]{3,2,1,0:T(8,128)(2,1)}, u32[]{:S(2)}) %copy-start.1) | copy-done | bytes 1048600
  31.9 1.2 %copy-done.3 = bf16[1,2,512,512]{3,2,1,0:T(8,128)(2,1)S(1)} copy-done((bf16[1,2,512,512]{3,2,1,0:T(8,128)(2,1)S(1)}, bf16[1,2,512,512]{3,2,1,0:T(8,128)(2,1)}, u32[]{:S(2)}) %copy-start.3) | copy-done | bytes 1048600
  33.2 1.2 %copy-done.6 = bf16[1,2,512,512]{3,2,1,0:T(8,128)(2,1)S(1)} copy-done((bf16[1,2,512,512]{3,2,1,0:T(8,128)(2,1)S(1)}, bf16[1,2,512,512]{3,2,1,0:T(8,128)(2,1)}, u32[]{:S(2)}) %copy-start.6) | copy-done | bytes 1048600
  34.4 4.2 %piece.2 = (f32[2,128,512]{2,1,0:T(8,128)S(1)}, bf16[2,128,512]{2,1,0:T(8,128)(2,1)}) custom-call(s32[7]{0:T(128)S(1)} %concatenate.38.meta, bf16[256,512]{1,0:T(8,128)(2,1)} %collective-permute-done.1.refs_0_, bf16[256,512]{1,0:T(8,128)(2,1)} %collective-permute-done.2.refs_1_, bf16[256,512]{1,0:T(8,128)(2,1)S(1)} %collective-permute-done.3.refs_2_.refs_0_, ...), custom_call_target="tpu_custom_call" | custom-call | flops 1073741824 | bytes 2621440 | tf_op jit(solution)/shard_map/piece/pallas_call | solution.py:77
  41.1 1.2 %copy-done.4 = bf16[1,2,512,512]{3,2,1,0:T(8,128)(2,1)S(1)} copy-done((bf16[1,2,512,512]{3,2,1,0:T(8,128)(2,1)S(1)}, bf16[1,2,512,512]{3,2,1,0:T(8,128)(2,1)}, u32[]{:S(2)}) %copy-start.4) | copy-done | bytes 1048600
  42.3 1.2 %copy-done.7 = bf16[1,2,512,512]{3,2,1,0:T(8,128)(2,1)S(1)} copy-done((bf16[1,2,512,512]{3,2,1,0:T(8,128)(2,1)S(1)}, bf16[1,2,512,512]{3,2,1,0:T(8,128)(2,1)}, u32[]{:S(2)}) %copy-start.7) | copy-done | bytes 1048600
  43.6 3.5 %piece.3 = (f32[2,128,512]{2,1,0:T(8,128)S(1)}, bf16[2,128,512]{2,1,0:T(8,128)(2,1)S(1)}) custom-call(s32[7]{0:T(128)S(1)} %concatenate.39.meta, bf16[256,512]{1,0:T(8,128)(2,1)S(1)} %collective-permute-done.3.refs_2_.refs_0_, bf16[256,512]{1,0:T(8,128)(2,1)} %collective-permute-done.4.refs_3_.refs_1_, ...), custom_call_target="tpu_custom_call" | custom-call | flops 1073741824 | bytes 2621440 | tf_op jit(solution)/shard_map/piece/pallas_call | solution.py:77
  48.6 3.0 %collective-permute-start.10 = (bf16[1,128,512]{2,1,0:T(8,128)(2,1)S(1)}, bf16[1,128,512]{2,1,0:T(8,128)(2,1)S(1)}, u32[]{:S(2)}, u32[]{:S(2)}) collective-permute-start(bf16[1,128,512]{2,1,0:T(8,128)(2,1)S(1)} %dynamic-slice_convert_fusion.1), channel_id=1, source_target_pairs={{0,4},{1,5},{2,6},{3,7},{4,0},{5,1},{6,2},{7,3},{8,12},{9,13},{10,... | collective-permute-start | bytes 393224 | tf_op jit(solution)/shard_map/ppermute | solution.py:98
  51.6 1.2 %collective-permute-done.14 = bf16[2,128,512]{2,1,0:T(8,128)(2,1)S(1)} collective-permute-done((bf16[2,128,512]{2,1,0:T(8,128)(2,1)S(1)}, bf16[2,128,512]{2,1,0:T(8,128)(2,1)S(1)}, u32[]{:S(2)}, u32[]{:S(2)}) %collective-permute-start.14) | collective-permute-done | bytes 262176 | tf_op jit(solution)/shard_map/ppermute | solution.py:98
  53.0 2.7 %collective-permute-start.15 = (bf16[1,128,512]{2,1,0:T(8,128)(2,1)S(1)}, bf16[1,128,512]{2,1,0:T(8,128)(2,1)S(1)}, u32[]{:S(2)}, u32[]{:S(2)}) collective-permute-start(bf16[1,128,512]{2,1,0:T(8,128)(2,1)S(1)} %dynamic-slice_convert_fusion), channel_id=1, source_target_pairs={{0,4},{1,5},{2,6},{3,7},{4,0},{5,1},{6,2},{7,3},{8,12},{9,13},{10,... | collective-permute-start | bytes 393224 | tf_op jit(solution)/shard_map/ppermute | solution.py:98
  55.8 4.2 %collective-permute-start.11 = (bf16[64,512]{1,0:T(8,128)(2,1)S(1)}, bf16[64,512]{1,0:T(8,128)(2,1)S(1)}, u32[]{:S(2)}, u32[]{:S(2)}) collective-permute-start(bf16[64,512]{1,0:T(8,128)(2,1)S(1)} %get-tuple-element.20), channel_id=1, source_target_pairs={{0,1},{1,0},{2,3},{3,2},{4,5},{5,4},{6,7},{7,6},{8,9},{9,8},{10,11... | collective-permute-start | bytes 196616 | tf_op jit(solution)/shard_map/ppermute | solution.py:156
  59.9 1.9 %collective-permute-done.15 = bf16[1,128,512]{2,1,0:T(8,128)(2,1)S(1)} collective-permute-done((bf16[1,128,512]{2,1,0:T(8,128)(2,1)S(1)}, bf16[1,128,512]{2,1,0:T(8,128)(2,1)S(1)}, u32[]{:S(2)}, u32[]{:S(2)}) %collective-permute-start.15) | collective-permute-done | bytes 131104 | tf_op jit(solution)/shard_map/ppermute | solution.py:98
  61.9 4.2 %collective-permute-start.16 = (bf16[64,512]{1,0:T(8,128)(2,1)S(1)}, bf16[64,512]{1,0:T(8,128)(2,1)S(1)}, u32[]{:S(2)}, u32[]{:S(2)}) collective-permute-start(bf16[64,512]{1,0:T(8,128)(2,1)S(1)} %get-tuple-element.22), channel_id=1, source_target_pairs={{0,1},{1,0},{2,3},{3,2},{4,5},{5,4},{6,7},{7,6},{8,9},{9,8},{10,11... | collective-permute-start | bytes 196616 | tf_op jit(solution)/shard_map/ppermute | solution.py:156
  (50 shorter events, 11.9 us)
Async XLA Ops:
  0.0 30.7 %copy-start = (bf16[2,2,512,512]{3,2,1,0:T(8,128)(2,1)S(1)}, bf16[2,2,512,512]{3,2,1,0:T(8,128)(2,1)}, u32[]{:S(2)}) copy-start(bf16[2,2,512,512]{3,2,1,0:T(8,128)(2,1)} %refs_6_.3) | copy-start | bytes 6291460
  0.0 29.7 %collective-permute-start.7 = (bf16[1,2,512,512]{3,2,1,0:T(8,128)(2,1)}, bf16[1,2,512,512]{3,2,1,0:T(8,128)(2,1)S(1)}, u32[]{:S(2)}, u32[]{:S(2)}) collective-permute-start(bf16[1,2,512,512]{3,2,1,0:T(8,128)(2,1)} %refs_7_.3), channel_id=1, source_target_pairs={{0,1},{1,0},{2,3},{3,2},{4,5},{5,4},{6,7},{7,6},{8,9},{9,8},{10,11... | collective-permute-start | bytes 3145736 | tf_op jit(solution)/shard_map/ppermute | solution.py:123
  0.1 30.7 %collective-permute-start.8 = (bf16[1,2,512,512]{3,2,1,0:T(8,128)(2,1)}, bf16[1,2,512,512]{3,2,1,0:T(8,128)(2,1)}, u32[]{:S(2)}, u32[]{:S(2)}) collective-permute-start(bf16[1,2,512,512]{3,2,1,0:T(8,128)(2,1)} %refs_8_.3), channel_id=1, source_target_pairs={{0,1},{1,0},{2,3},{3,2},{4,5},{5,4},{6,7},{7,6},{8,9},{9,8},{10,11... | collective-permute-start | bytes 3145736 | tf_op jit(solution)/shard_map/ppermute | solution.py:124
  2.8 8.6 %collective-permute-start.1 = (bf16[256,512]{1,0:T(8,128)(2,1)}, bf16[256,512]{1,0:T(8,128)(2,1)}, u32[]{:S(2)}, u32[]{:S(2)}) collective-permute-start(bf16[256,512]{1,0:T(8,128)(2,1)} %get-tuple-element.17), channel_id=1, source_target_pairs={{0,8},{8,0},{16,24},{24,16},{1,9},{9,1},{17,25},{25,17},{2,10},{10... | collective-permute-start | bytes 786440 | tf_op jit(solution)/shard_map/ppermute | solution.py:122
  4.9 12.1 %collective-permute-start.2 = (bf16[256,512]{1,0:T(8,128)(2,1)}, bf16[256,512]{1,0:T(8,128)(2,1)}, u32[]{:S(2)}, u32[]{:S(2)}) collective-permute-start(bf16[256,512]{1,0:T(8,128)(2,1)} %get-tuple-element.15), channel_id=1, source_target_pairs={{0,8},{8,0},{16,24},{24,16},{1,9},{9,1},{17,25},{25,17},{2,10},{10... | collective-permute-start | bytes 786440 | tf_op jit(solution)/shard_map/ppermute | solution.py:122
  6.4 1.7 %collective-permute-start = (s32[2]{0:T(128)S(1)}, s32[2]{0:T(128)S(1)}, u32[]{:S(2)}, u32[]{:S(2)}) collective-permute-start(s32[2]{0:T(128)S(1)} %pad_add_fusion), channel_id=1, source_target_pairs={{0,1},{1,0},{2,3},{3,2},{4,5},{5,4},{6,7},{7,6},{8,9},{9,8},{10,11... | collective-permute-start | bytes 32 | tf_op jit(solution)/shard_map/ppermute | solution.py:125
  8.0 14.6 %collective-permute-start.3 = (bf16[256,512]{1,0:T(8,128)(2,1)}, bf16[256,512]{1,0:T(8,128)(2,1)S(1)}, u32[]{:S(2)}, u32[]{:S(2)}) collective-permute-start(bf16[256,512]{1,0:T(8,128)(2,1)} %get-tuple-element.16), channel_id=1, source_target_pairs={{0,8},{8,0},{16,24},{24,16},{1,9},{9,1},{17,25},{25,17},{2,10},{10... | collective-permute-start | bytes 786440 | tf_op jit(solution)/shard_map/ppermute | solution.py:122
  11.4 16.9 %collective-permute-start.4 = (bf16[256,512]{1,0:T(8,128)(2,1)}, bf16[256,512]{1,0:T(8,128)(2,1)}, u32[]{:S(2)}, u32[]{:S(2)}) collective-permute-start(bf16[256,512]{1,0:T(8,128)(2,1)} %get-tuple-element.18), channel_id=1, source_target_pairs={{0,8},{8,0},{16,24},{24,16},{1,9},{9,1},{17,25},{25,17},{2,10},{10... | collective-permute-start | bytes 786440 | tf_op jit(solution)/shard_map/ppermute | solution.py:122
  17.0 12.4 %collective-permute-start.5 = (bf16[256,512]{1,0:T(8,128)(2,1)}, bf16[256,512]{1,0:T(8,128)(2,1)}, u32[]{:S(2)}, u32[]{:S(2)}) collective-permute-start(bf16[256,512]{1,0:T(8,128)(2,1)} %collective-permute-done.1.refs_0_), channel_id=1, source_target_pairs={{0,16},{8,24},{16,0},{24,8},{1,17},{9,25},{17,1},{25,9},{2,18},{10... | collective-permute-start | bytes 786440 | tf_op jit(solution)/shard_map/ppermute | solution.py:128
  22.7 7.1 %collective-permute-start.6 = (bf16[256,512]{1,0:T(8,128)(2,1)}, bf16[256,512]{1,0:T(8,128)(2,1)}, u32[]{:S(2)}, u32[]{:S(2)}) collective-permute-start(bf16[256,512]{1,0:T(8,128)(2,1)} %collective-permute-done.2.refs_1_), channel_id=1, source_target_pairs={{0,16},{8,24},{16,0},{24,8},{1,17},{9,25},{17,1},{25,9},{2,18},{10... | collective-permute-start | bytes 786440 | tf_op jit(solution)/shard_map/ppermute | solution.py:128
  28.3 11.8 %collective-permute-start.12 = (bf16[256,512]{1,0:T(8,128)(2,1)S(1)}, bf16[256,512]{1,0:T(8,128)(2,1)}, u32[]{:S(2)}, u32[]{:S(2)}) collective-permute-start(bf16[256,512]{1,0:T(8,128)(2,1)S(1)} %collective-permute-done.3.refs_2_.refs_0_), channel_id=1, source_target_pairs={{0,16},{8,24},{16,0},{24,8},{1,17},{9,25},{17,1},{25,9},{2,18},{10... | collective-permute-start | bytes 786440 | tf_op jit(solution)/shard_map/ppermute | solution.py:128
  29.4 11.7 %collective-permute-start.13 = (bf16[256,512]{1,0:T(8,128)(2,1)}, bf16[256,512]{1,0:T(8,128)(2,1)}, u32[]{:S(2)}, u32[]{:S(2)}) collective-permute-start(bf16[256,512]{1,0:T(8,128)(2,1)} %collective-permute-done.4.refs_3_.refs_1_), channel_id=1, source_target_pairs={{0,16},{8,24},{16,0},{24,8},{1,17},{9,25},{17,1},{25,9},{2,18},{10... | collective-permute-start | bytes 786440 | tf_op jit(solution)/shard_map/ppermute | solution.py:128
  30.7 1.2 %copy-start.1 = (bf16[1,2,512,512]{3,2,1,0:T(8,128)(2,1)S(1)}, bf16[1,2,512,512]{3,2,1,0:T(8,128)(2,1)}, u32[]{:S(2)}) copy-start(bf16[1,2,512,512]{3,2,1,0:T(8,128)(2,1)} %refs_7_.3) | copy-start | bytes 3145732
  33.2 1.2 %copy-start.6 = (bf16[1,2,512,512]{3,2,1,0:T(8,128)(2,1)S(1)}, bf16[1,2,512,512]{3,2,1,0:T(8,128)(2,1)}, u32[]{:S(2)}) copy-start(bf16[1,2,512,512]{3,2,1,0:T(8,128)(2,1)} %copy-done.5) | copy-start | bytes 3145732
  34.4 6.7 %copy-start.2 = (bf16[1,2,512,512]{3,2,1,0:T(8,128)(2,1)S(1)}, bf16[1,2,512,512]{3,2,1,0:T(8,128)(2,1)}, u32[]{:S(2)}) copy-start(bf16[1,2,512,512]{3,2,1,0:T(8,128)(2,1)} %refs_7_.3) | copy-start | bytes 3145732
  39.4 8.2 %collective-permute-start.9 = (bf16[2,128,512]{2,1,0:T(8,128)(2,1)}, bf16[2,128,512]{2,1,0:T(8,128)(2,1)}, u32[]{:S(2)}, u32[]{:S(2)}) collective-permute-start(bf16[2,128,512]{2,1,0:T(8,128)(2,1)} %get-tuple-element.10), channel_id=1, source_target_pairs={{0,2},{1,3},{2,0},{3,1},{4,6},{5,7},{6,4},{7,5},{8,10},{9,11},{10,... | collective-permute-start | bytes 786440 | tf_op jit(solution)/shard_map/ppermute | solution.py:98
  41.1 1.2 %copy-start.4 = (bf16[1,2,512,512]{3,2,1,0:T(8,128)(2,1)S(1)}, bf16[1,2,512,512]{3,2,1,0:T(8,128)(2,1)}, u32[]{:S(2)}) copy-start(bf16[1,2,512,512]{3,2,1,0:T(8,128)(2,1)} %refs_8_.3) | copy-start | bytes 3145732
  42.3 1.2 %copy-start.7 = (bf16[1,2,512,512]{3,2,1,0:T(8,128)(2,1)S(1)}, bf16[1,2,512,512]{3,2,1,0:T(8,128)(2,1)}, u32[]{:S(2)}) copy-start(bf16[1,2,512,512]{3,2,1,0:T(8,128)(2,1)} %copy-done.5) | copy-start | bytes 3145732
  43.6 4.0 %copy-start.9 = (f32[2,128,512]{2,1,0:T(8,128)S(1)}, f32[2,128,512]{2,1,0:T(8,128)}, u32[]{:S(2)}) copy-start(f32[2,128,512]{2,1,0:T(8,128)} %copy-done.8) | copy-start | bytes 1572868
  47.0 5.9 %collective-permute-start.14 = (bf16[2,128,512]{2,1,0:T(8,128)(2,1)S(1)}, bf16[2,128,512]{2,1,0:T(8,128)(2,1)S(1)}, u32[]{:S(2)}, u32[]{:S(2)}) collective-permute-start(bf16[2,128,512]{2,1,0:T(8,128)(2,1)S(1)} %get-tuple-element.12), channel_id=1, source_target_pairs={{0,2},{1,3},{2,0},{3,1},{4,6},{5,7},{6,4},{7,5},{8,10},{9,11},{10,... | collective-permute-start | bytes 786440 | tf_op jit(solution)/shard_map/ppermute | solution.py:98
  48.6 7.1 %collective-permute-start.10 = (bf16[1,128,512]{2,1,0:T(8,128)(2,1)S(1)}, bf16[1,128,512]{2,1,0:T(8,128)(2,1)S(1)}, u32[]{:S(2)}, u32[]{:S(2)}) collective-permute-start(bf16[1,128,512]{2,1,0:T(8,128)(2,1)S(1)} %dynamic-slice_convert_fusion.1), channel_id=1, source_target_pairs={{0,4},{1,5},{2,6},{3,7},{4,0},{5,1},{6,2},{7,3},{8,12},{9,13},{10,... | collective-permute-start | bytes 393224 | tf_op jit(solution)/shard_map/ppermute | solution.py:98
  53.0 8.9 %collective-permute-start.15 = (bf16[1,128,512]{2,1,0:T(8,128)(2,1)S(1)}, bf16[1,128,512]{2,1,0:T(8,128)(2,1)S(1)}, u32[]{:S(2)}, u32[]{:S(2)}) collective-permute-start(bf16[1,128,512]{2,1,0:T(8,128)(2,1)S(1)} %dynamic-slice_convert_fusion), channel_id=1, source_target_pairs={{0,4},{1,5},{2,6},{3,7},{4,0},{5,1},{6,2},{7,3},{8,12},{9,13},{10,... | collective-permute-start | bytes 393224 | tf_op jit(solution)/shard_map/ppermute | solution.py:98
  55.8 10.4 %collective-permute-start.11 = (bf16[64,512]{1,0:T(8,128)(2,1)S(1)}, bf16[64,512]{1,0:T(8,128)(2,1)S(1)}, u32[]{:S(2)}, u32[]{:S(2)}) collective-permute-start(bf16[64,512]{1,0:T(8,128)(2,1)S(1)} %get-tuple-element.20), channel_id=1, source_target_pairs={{0,1},{1,0},{2,3},{3,2},{4,5},{5,4},{6,7},{7,6},{8,9},{9,8},{10,11... | collective-permute-start | bytes 196616 | tf_op jit(solution)/shard_map/ppermute | solution.py:156
  61.9 5.1 %collective-permute-start.16 = (bf16[64,512]{1,0:T(8,128)(2,1)S(1)}, bf16[64,512]{1,0:T(8,128)(2,1)S(1)}, u32[]{:S(2)}, u32[]{:S(2)}) collective-permute-start(bf16[64,512]{1,0:T(8,128)(2,1)S(1)} %get-tuple-element.22), channel_id=1, source_target_pairs={{0,1},{1,0},{2,3},{3,2},{4,5},{5,4},{6,7},{7,6},{8,9},{9,8},{10,11... | collective-permute-start | bytes 196616 | tf_op jit(solution)/shard_map/ppermute | solution.py:156
  (3 other events, 3.0 us)

commit v2 on v0

v2 whole, which is shorter than its diff:
```python
import jax
import jax.numpy as jnp
from jax import lax
from jax.experimental import pallas as pl
from jax.experimental.pallas import tpu as pltpu
from jax.sharding import PartitionSpec as P

DQ = 2
VMEM_LIMIT = 12 * 1024 * 1024
SMEM_SPEC = pl.BlockSpec(memory_space=pltpu.SMEM)
VMEM_SPEC = pl.BlockSpec(memory_space=pltpu.VMEM)
ANY_SPEC = pl.BlockSpec(memory_space=pl.ANY)


def in_vmem(array):
    return pltpu.with_memory_space_constraint(array, pltpu.VMEM)


def in_hbm(array):
    return pltpu.with_memory_space_constraint(array, pltpu.HBM)


def call(body, name, **kwargs):
    return pl.pallas_call(
        body,
        compiler_params=pltpu.CompilerParams(vmem_limit_bytes=VMEM_LIMIT),
        cost_estimate=pl.CostEstimate(flops=1000, bytes_accessed=1000, transcendentals=0),
        name=name,
        **kwargs,
    )


def cut(place, psi, left, right):
    size = psi.shape[-1]
    rows = size // 2

    def body(place_ref, psi_ref, left_ref, right_ref, *refs):
        parts, pack, sem = refs[:3], refs[3], refs[4]
        core, odd, half = place_ref[0], place_ref[1], place_ref[3] % 2
        copies = [
            pltpu.make_async_copy(psi_ref.at[sector, core, pl.ds(start * rows, rows)], part, sem.at[n])
            for n, (part, sector, start) in enumerate(zip(parts, (odd, 1 - odd, 1 - odd), (half, 0, 1), strict=True))
        ]
        copies.append(pltpu.make_async_copy(left_ref.at[0], pack.at[pl.ds(0, 2)], sem.at[3]))
        copies.append(pltpu.make_async_copy(right_ref.at[0], pack.at[pl.ds(2, 2)], sem.at[4]))
        for copy in copies:
            copy.start()
        for copy in copies:
            copy.wait()

    out = [pltpu.VMEM((rows, size), psi.dtype)] * 3 + [pltpu.VMEM((4, size, size), psi.dtype)]
    *parts, pack = call(
        body,
        "cut",
        out_shape=out,
        in_specs=[SMEM_SPEC] + [ANY_SPEC] * 3,
        out_specs=[VMEM_SPEC] * len(out),
        scratch_shapes=[pltpu.SemaphoreType.DMA((5,))],
    )(place, in_hbm(psi), in_hbm(left), in_hbm(right))
    return parts, pack


def copy_after(part, *after):
    def body(part_ref, *refs):
        out, sem = refs[-2:]
        copy = pltpu.make_async_copy(part_ref, out, sem)
        copy.start()
        copy.wait()

    return call(
        body,
        "copy_after",
        out_shape=pltpu.VMEM(part.shape, part.dtype),
        in_specs=[VMEM_SPEC] + [ANY_SPEC] * len(after),
        out_specs=VMEM_SPEC,
        scratch_shapes=[pltpu.SemaphoreType.DMA],
    )(in_vmem(part), *after)


def piece(step, secs, chips, scalars, halo, swapped, pack1, psi, left0, right0):
    size = psi.shape[-1]
    slots, height, count = len(halo), size // chips, chips // 2
    rows = size // 2
    near = [part for block in halo for part in block] + [pack1]
    far = [psi, left0, right0]

    def body(place, shift0, live0, other, *refs):
        halves, pack, refs = refs[: 2 * slots], refs[2 * slots], refs[2 * slots + 1 :]
        psi_ref, left_ref, right_ref, stay, first, final, own, left, right, inner, sem = refs
        core, odd, i, z = place[0], place[1], place[2], place[3]
        sector = step * odd + (1 - step) * (1 - odd)
        slot_of, weight_of = [], []
        for shift, live in zip((shift0[0], other[0]), (live0[0], other[1])):
            rel = sector - shift
            at = step - (2 * odd - 1) * shift
            if step == 0:
                slot = jnp.where(at == 2, 2, at + 2)
            else:
                slot = jnp.where(at >= 2, at - 1, at + 1)
            slot_of.append(jnp.where((rel == 0) | (rel == 1), slots + rel, slot))
            there = ((rel >= 0) | (i > 0)) & ((rel <= 1) | (i < secs - 1))
            weight_of.append(jnp.where(there, live, 0).astype(jnp.float32))

        def own_copy(term, index):
            return pltpu.make_async_copy(psi_ref.at[index, core], own.at[term], sem.at[term])

        for term in (1, 0):
            @pl.when(slot_of[term] >= slots)
            def _(term=term):
                own_copy(term, slot_of[term] - slots).start()
        left_copy = pltpu.make_async_copy(left_ref.at[0, sector], left, sem.at[2])
        right_copy = pltpu.make_async_copy(right_ref.at[0, sector], right, sem.at[3])
        left_copy.start()
        right_copy.start()

        order = [*range(1, chips, 2), *range(0, chips, 2)]
        for term in (1, 0):
            if term == 0:
                left_copy.wait()

            def left_rows(group, column, term=term):
                def at(r, k):
                    block = pl.ds(pl.multiple_of((z ^ r) * height + (core ^ k) * (height // 2), height // 2), height // 2)
                    columns = pl.ds(pl.multiple_of(column * rows, 128), rows)
                    return left[block, columns] if term == 0 else pack[sector, block, columns]

                return jnp.concatenate([at(r, k) for r in order[group * count : (group + 1) * count] for k in range(2)])

            def first_product(sources, columns, term=term, left_rows=left_rows):
                for group in range(2):
                    product = sum(
                        jnp.dot(left_rows(group, column), source(), preferred_element_type=jnp.float32)
                        for source, column in zip(sources, columns)
                    )
                    inner[term, pl.ds(group * rows, rows)] = product.astype(jnp.bfloat16)

            for k in range(slots):
                @pl.when(slot_of[term] == k)
                def _(k=k):
                    parity = z % 2 if swapped[k] else 0
                    sources = [lambda n=n: halves[2 * k + n][...] for n in range(2)]
                    first_product(sources, [parity, 1 - parity])

            @pl.when(slot_of[term] >= slots)
            def _(term=term):
                own_copy(term, 0).wait()
                first_product([lambda n=n: own[term, pl.ds(n * rows, rows)] for n in range(2)], [0, 1])

        right_copy.wait()
        for group in range(2):
            total = sum(
                lax.dot_general(
                    inner[term, pl.ds(group * rows, rows)],
                    right[...] if term == 0 else pack[2 + sector],
                    (((1,), (1,)), ((), ())),
                    preferred_element_type=jnp.float32,
                )
                * weight_of[term]
                for term in (1, 0)
            )
            for n in range(count):
                block = total[n * height : (n + 1) * height]
                if group == 1:
                    stay[n] = block
                elif n == 0:
                    final[...] = block.astype(final.dtype)
                else:
                    first[n - 1] = block.astype(first.dtype)

    return call(
        body,
        "piece",
        out_shape=(
            pltpu.VMEM((count, height, size), jnp.float32),
            pltpu.VMEM((count - 1, height, size), jnp.bfloat16),
            pltpu.VMEM((height, size), jnp.bfloat16),
        ),
        in_specs=[SMEM_SPEC] * 4 + [VMEM_SPEC] * len(near) + [ANY_SPEC] * len(far),
        out_specs=(VMEM_SPEC,) * 3,
        scratch_shapes=[
            pltpu.VMEM((2, size, size), jnp.bfloat16),
            pltpu.VMEM((size, size), jnp.bfloat16),
            pltpu.VMEM((size, size), jnp.bfloat16),
            pltpu.VMEM((2, size, size), jnp.bfloat16),
            pltpu.SemaphoreType.DMA((4,)),
        ],
    )(*scalars, *[in_vmem(x) for x in near], *[in_hbm(x) for x in far])


def sum_over_chips(stay, first, final, terms):
    pairs = [(d, d ^ 2) for d in range(terms)]
    got = lax.ppermute(first, "term", pairs)
    last = lax.ppermute(final, "term", pairs)
    mid = stay[1:] + got.astype(jnp.float32)
    keep = stay[0] + last.astype(jnp.float32)
    step = 4
    while step < terms:
        pairs = [(d, d ^ step) for d in range(terms)]
        last = lax.ppermute(mid[0].astype(jnp.bfloat16), "term", pairs)
        keep = keep + last.astype(jnp.float32)
        if mid.shape[0] > 1:
            got = lax.ppermute(mid[2::2].astype(jnp.bfloat16), "term", pairs)
            mid = mid[1::2] + got.astype(jnp.float32)
        step *= 2
    return keep


def local(psi, left_ops, right_ops, shift, live):
    secs, terms = lax.axis_size("sec"), lax.axis_size("term")
    size = psi.shape[-1]
    i, term = lax.axis_index("sec"), lax.axis_index("term")
    core, odd, z = term % 2, i % 2, term // 2
    cores = [(d, d ^ 1) for d in range(terms)]
    pairs = [(d, d ^ 1) for d in range(secs)]

    place = jnp.stack([core, odd, i, z]).astype(jnp.int32)
    parts, pack0 = cut(place, psi, left_ops, right_ops)
    near = [lax.ppermute(part, "sec", pairs) for part in parts]
    pack1 = lax.ppermute(pack0, "term", cores)
    other = lax.ppermute(jnp.concatenate([shift, live]), "term", cores)
    if secs == 4:
        turn = [(d, d ^ 2) for d in range(secs)]
        far = [lax.ppermute(part, "sec", turn) for part in near[:2]]
        far.append(lax.ppermute(copy_after(near[2], far[0]), "sec", turn))
    else:
        nexts = [(d, d + 1) for d in range(1, secs - 1, 2)]
        nexts = nexts + [(b, a) for a, b in nexts]
        far = [lax.ppermute(part, "sec", nexts) for part in parts]
    planes = [(d, d ^ 2) for d in range(terms)]
    near_first, near_second = (near[0], lax.ppermute(near[0], "term", planes)), near[1:]
    far_first, far_second = (far[0], lax.ppermute(far[0], "term", planes)), far[1:]

    scalars = (place, shift, live, other)
    outs = []
    for step in range(2):
        halo = (near_first, near_second, far_first) if step == 0 else (near_second, far_first, far_second)
        swapped = (True, False, True) if step == 0 else (False, True, False)
        blocks = piece(step, secs, terms // 2, scalars, halo, swapped, pack1, psi, left_ops, right_ops)
        total = sum_over_chips(*blocks, terms).astype(jnp.bfloat16)
        mine, others = total[: size // terms], total[size // terms :]
        got = lax.ppermute(others, "term", cores)
        outs.append(jnp.where(core == 0, jnp.stack([mine, got]), jnp.stack([got, mine])))
    return jnp.where(odd == 1, jnp.stack(outs), jnp.stack(outs[::-1]))


def solution(mesh):
    in_specs = (
        P("sec", None, None, None),
        P("term", "sec", None, None),
        P("term", "sec", None, None),
        P("term"),
        P("term"),
    )
    out_specs = P("sec", None, "term", None)
    return jax.shard_map(local, mesh=mesh, in_specs=in_specs, out_specs=out_specs, check_vma=False)
```

time: 169 us -> 60.8 us (0.36); the launches traced: 166 us -> 60.1 us
  waiting for transfers between devices: 138 us -> 18.5 us
  starting transfers between devices: 5.49 us -> 27.9 us
  between operations: 14.7 us -> 1.41 us
  Pallas kernels: 0 us -> 9.59 us
  matrix products: 5.77 us -> 0 us
    ppermute x2 -> x18, waiting for transfers between devices: 88.8 us -> 18.5 us  [the longest x3 8.43 us: local(): near = [lax.ppermute(part, 'sec', pairs) for part in parts]]
    reduce_scatter x1 -> x0, waiting for transfers between devices: 49.5 us -> none  [local(): summed = lax.psum_scatter(acc, 'term', scatter_dimension=0, tiled=True)]
    ppermute x2 -> x18, starting transfers between devices: 5.49 us -> 27.9 us  [the longest x2 9.49 us: local(): got = lax.ppermute(others, 'term', cores)]
    pallas_call x0 -> x4, Pallas kernels: none -> 9.59 us  [the longest x2 6.48 us: piece(): call(body, 'piece', out_shape=(pltpu.VMEM((count, height, size), jnp.floa...]
    dot_general x1 -> x0, matrix products: 5.77 us -> none  [local(): jnp.einsum('asvc,sdc->asvd', inner, right_ops[0], preferred_element_type=...]
  transfers between devices with their start and end apart: 3 -> 18, of which waited for: 3 -> 6; matrix products, arithmetic and copies ran while one was open for 0% -> 2% of each run, Pallas kernels for 0% -> 12%
where the time goes in v2:
time: 60.8 us; the launch traced here: 60.1 us
  starting transfers between devices  27.9 us (46%)
  waiting for transfers between devices  18.5 us (30%)
  Pallas kernels  9.59 us (16%)
  other arithmetic  1.98 us (3%)
  between operations  1.41 us (2%)
  local copies, waits for them, and re-layouts  0.83 us (1%)
    ppermute x2, starting transfers between devices, local(): got = lax.ppermute(others, 'term', cores)  9.49 us
    ppermute x3, waiting for transfers between devices, local(): near = [lax.ppermute(part, 'sec', pairs) for part in parts]  8.43 us
    pallas_call x2, Pallas kernels, piece(): call(body, 'piece', out_shape=(pltpu.VMEM((count, height, size), jnp.floa...  6.48 us
    ppermute x3, starting transfers between devices, local(): near = [lax.ppermute(part, 'sec', pairs) for part in parts]  4.14 us
    ppermute x1, waiting for transfers between devices, local(): far.append(lax.ppermute(copy_after(near[2], far[0]), 'sec', turn))  3.66 us
    ppermute x2, starting transfers between devices, sum_over_chips(): last = lax.ppermute(mid[0].astype(jnp.bfloat16), 'term', pairs)  3.44 us
    ppermute x2, waiting for transfers between devices, local(): far = [lax.ppermute(part, 'sec', turn) for part in near[:2]]  3.12 us
    ppermute x2, starting transfers between devices, sum_over_chips(): got = lax.ppermute(first, 'term', pairs)  3.11 us
  transfers between devices with their start and end apart: 18, of which 6 were waited for; matrix products, arithmetic and copies ran while one was open for 2% of the time, Pallas kernels for 12%

profile of v2, /device:TPU:1, one launch (start us, length us, event | category | flops | bytes accessed | tf_op | source)
XLA Modules:
  0.0 60.1 jit_solution(14021153999782207552)
XLA Ops:
  0.1 2.4 %cut.1 = (bf16[256,512]{1,0:T(8,128)(2,1)S(1)}, bf16[256,512]{1,0:T(8,128)(2,1)S(1)}, bf16[256,512]{1,0:T(8,128)(2,1)S(1)}, bf16[4,512,512]{2,1,0:T(8,128)(2,1)S(1)}) custom-call(s32[4]{0:T(128)S(1)} %pad_add_fusion.place_ref.place, bf16[2,2,512,512]{3,2,1,0:T(8,128)(2,1)} %refs_7_.3, bf16[1,2,512,512]{3,2,1,0:T(8,128)(2,1)} %refs_8_.3, ...), custom_call_target="tpu_custom_call" | custom-call | flops 1000 | bytes 1000 | tf_op jit(solution)/shard_map/cut/pallas_call | solution.py:52
  2.6 2.7 %collective-permute-start.1 = (bf16[256,512]{1,0:T(8,128)(2,1)S(1)}, bf16[256,512]{1,0:T(8,128)(2,1)S(1)}, u32[]{:S(2)}, u32[]{:S(2)}) collective-permute-start(bf16[256,512]{1,0:T(8,128)(2,1)S(1)} %get-tuple-element.15), channel_id=1, source_target_pairs={{0,8},{8,0},{16,24},{24,16},{1,9},{9,1},{17,25},{25,17},{2,10},{10... | collective-permute-start | bytes 786440 | tf_op jit(solution)/shard_map/ppermute | solution.py:218
  5.3 6.6 %collective-permute-done.1.refs_0_ = bf16[256,512]{1,0:T(8,128)(2,1)S(1)} collective-permute-done((bf16[256,512]{1,0:T(8,128)(2,1)S(1)}, bf16[256,512]{1,0:T(8,128)(2,1)S(1)}, u32[]{:S(2)}, u32[]{:S(2)}) %collective-permute-start.1) | collective-permute-done | bytes 262176 | tf_op jit(solution)/shard_map/ppermute | solution.py:218
  11.8 1.3 %collective-permute-start.5 = (bf16[256,512]{1,0:T(8,128)(2,1)S(1)}, bf16[256,512]{1,0:T(8,128)(2,1)S(1)}, u32[]{:S(2)}, u32[]{:S(2)}) collective-permute-start(bf16[256,512]{1,0:T(8,128)(2,1)S(1)} %collective-permute-done.1.refs_0_), channel_id=1, source_target_pairs={{0,16},{8,24},{16,0},{24,8},{1,17},{9,25},{17,1},{25,9},{2,18},{10... | collective-permute-start | bytes 786440 | tf_op jit(solution)/shard_map/ppermute | solution.py:223
  13.2 1.2 %collective-permute-start.3 = (bf16[256,512]{1,0:T(8,128)(2,1)S(1)}, bf16[256,512]{1,0:T(8,128)(2,1)S(1)}, u32[]{:S(2)}, u32[]{:S(2)}) collective-permute-start(bf16[256,512]{1,0:T(8,128)(2,1)S(1)} %get-tuple-element.16), channel_id=1, source_target_pairs={{0,8},{8,0},{16,24},{24,16},{1,9},{9,1},{17,25},{25,17},{2,10},{10... | collective-permute-start | bytes 786440 | tf_op jit(solution)/shard_map/ppermute | solution.py:218
  14.6 1.3 %collective-permute-start.2 = (bf16[256,512]{1,0:T(8,128)(2,1)S(1)}, bf16[256,512]{1,0:T(8,128)(2,1)S(1)}, u32[]{:S(2)}, u32[]{:S(2)}) collective-permute-start(bf16[256,512]{1,0:T(8,128)(2,1)S(1)} %collective-permute-done.1.refs_0_), channel_id=1, source_target_pairs={{0,2},{1,3},{2,0},{3,1},{4,6},{5,7},{6,4},{7,5},{8,10},{9,11},{10,... | collective-permute-start | bytes 786440 | tf_op jit(solution)/shard_map/ppermute | solution.py:230
  15.9 3.1 %collective-permute-done.5.refs_4_.refs_0_.refs_2_ = bf16[256,512]{1,0:T(8,128)(2,1)S(1)} collective-permute-done((bf16[256,512]{1,0:T(8,128)(2,1)S(1)}, bf16[256,512]{1,0:T(8,128)(2,1)S(1)}, u32[]{:S(2)}, u32[]{:S(2)}) %collective-permute-start.5) | collective-permute-done | bytes 262176 | tf_op jit(solution)/shard_map/ppermute | solution.py:223
  19.0 1.2 %collective-permute-start.6 = (bf16[256,512]{1,0:T(8,128)(2,1)S(1)}, bf16[256,512]{1,0:T(8,128)(2,1)S(1)}, u32[]{:S(2)}, u32[]{:S(2)}) collective-permute-start(bf16[256,512]{1,0:T(8,128)(2,1)S(1)} %collective-permute-done.5.refs_4_.refs_0_.refs_2_), channel_id=1, source_target_pairs={{0,2},{1,3},{2,0},{3,1},{4,6},{5,7},{6,4},{7,5},{8,10},{9,11},{10,... | collective-permute-start | bytes 786440 | tf_op jit(solution)/shard_map/ppermute | solution.py:231
  21.6 2.0 %collective-permute-start = (s32[2]{0:T(128)S(1)}, s32[2]{0:T(128)S(1)}, u32[]{:S(2)}, u32[]{:S(2)}) collective-permute-start(s32[2]{0:T(128)S(1)} %pad_add_fusion.1), channel_id=1, source_target_pairs={{0,1},{1,0},{2,3},{3,2},{4,5},{5,4},{6,7},{7,6},{8,9},{9,8},{10,11... | collective-permute-start | bytes 32 | tf_op jit(solution)/shard_map/ppermute | solution.py:220
  23.6 1.8 %collective-permute-done.4.refs_3_.part_ref.refs_1_ = bf16[256,512]{1,0:T(8,128)(2,1)S(1)} collective-permute-done((bf16[256,512]{1,0:T(8,128)(2,1)S(1)}, bf16[256,512]{1,0:T(8,128)(2,1)S(1)}, u32[]{:S(2)}, u32[]{:S(2)}) %collective-permute-start.4) | collective-permute-done | bytes 262176 | tf_op jit(solution)/shard_map/ppermute | solution.py:218
  26.6 1.2 %collective-permute-start.13 = (bf16[256,512]{1,0:T(8,128)(2,1)}, bf16[256,512]{1,0:T(8,128)(2,1)}, u32[]{:S(2)}, u32[]{:S(2)}) collective-permute-start(bf16[256,512]{1,0:T(8,128)(2,1)} %copy_after.1), channel_id=1, source_target_pairs={{0,16},{8,24},{16,0},{24,8},{1,17},{9,25},{17,1},{25,9},{2,18},{10... | collective-permute-start | bytes 786440 | tf_op jit(solution)/shard_map/ppermute | solution.py:224
  27.7 3.2 %piece.2 = (f32[2,128,512]{2,1,0:T(8,128)S(1)}, bf16[1,128,512]{2,1,0:T(8,128)(2,1)}, bf16[128,512]{1,0:T(8,128)(2,1)S(1)}) custom-call(s32[4]{0:T(128)S(1)} %pad_add_fusion.place_ref.place, s32[1]{0:T(128)S(6)} %copy.6.shift0, s32[1]{0:T(128)S(6)} %copy.7.live0, s32[2]{0:T(128)S(1)} %collective-permute-done.other, ...), custom_call_target="tpu_custom_call" | custom-call | flops 1000 | bytes 1000 | tf_op jit(solution)/shard_map/piece/pallas_call | solution.py:170
  31.0 0.8 %copy-done = f32[2,128,512]{2,1,0:T(8,128)} copy-done((f32[2,128,512]{2,1,0:T(8,128)}, f32[2,128,512]{2,1,0:T(8,128)S(1)}, u32[]{:S(2)}) %copy-start) | copy-done | bytes 524312
  31.8 1.3 %collective-permute-start.9 = (bf16[1,128,512]{2,1,0:T(8,128)(2,1)}, bf16[1,128,512]{2,1,0:T(8,128)(2,1)}, u32[]{:S(2)}, u32[]{:S(2)}) collective-permute-start(bf16[1,128,512]{2,1,0:T(8,128)(2,1)} %get-tuple-element.21), channel_id=1, source_target_pairs={{0,2},{1,3},{2,0},{3,1},{4,6},{5,7},{6,4},{7,5},{8,10},{9,11},{10,... | collective-permute-start | bytes 393224 | tf_op jit(solution)/shard_map/ppermute | solution.py:192
  33.3 3.7 %collective-permute-done.13.refs_5_ = bf16[256,512]{1,0:T(8,128)(2,1)} collective-permute-done((bf16[256,512]{1,0:T(8,128)(2,1)}, bf16[256,512]{1,0:T(8,128)(2,1)}, u32[]{:S(2)}, u32[]{:S(2)}) %collective-permute-start.13) | collective-permute-done | bytes 262176 | tf_op jit(solution)/shard_map/ppermute | solution.py:224
  36.9 3.2 %piece.3 = (f32[2,128,512]{2,1,0:T(8,128)S(1)}, bf16[1,128,512]{2,1,0:T(8,128)(2,1)S(1)}, bf16[128,512]{1,0:T(8,128)(2,1)S(1)}) custom-call(s32[4]{0:T(128)S(1)} %pad_add_fusion.place_ref.place, s32[1]{0:T(128)S(6)} %copy.6.shift0, s32[1]{0:T(128)S(6)} %copy.7.live0, s32[2]{0:T(128)S(1)} %collective-permute-done.other, ...), custom_call_target="tpu_custom_call" | custom-call | flops 1000 | bytes 1000 | tf_op jit(solution)/shard_map/piece/pallas_call | solution.py:170
  40.2 1.8 %collective-permute-start.15 = (bf16[1,128,512]{2,1,0:T(8,128)(2,1)S(1)}, bf16[1,128,512]{2,1,0:T(8,128)(2,1)S(1)}, u32[]{:S(2)}, u32[]{:S(2)}) collective-permute-start(bf16[1,128,512]{2,1,0:T(8,128)(2,1)S(1)} %get-tuple-element.24), channel_id=1, source_target_pairs={{0,2},{1,3},{2,0},{3,1},{4,6},{5,7},{6,4},{7,5},{8,10},{9,11},{10,... | collective-permute-start | bytes 393224 | tf_op jit(solution)/shard_map/ppermute | solution.py:192
  42.1 0.9 %fusion.4 = bf16[128,512]{1,0:T(8,128)(2,1)S(1)} fusion(bf16[1,128,512]{2,1,0:T(8,128)(2,1)} %collective-permute-done.9, f32[2,128,512]{2,1,0:T(8,128)S(1)} %copy-done.1), kind=kLoop, calls=%fused_computation.9 | loop fusion | flops 196608 | bytes 524288 | tf_op jit(solution)/shard_map/convert_element_type | solution.py:199
  43.0 2.0 %collective-permute-start.10 = (bf16[128,512]{1,0:T(8,128)(2,1)S(1)}, bf16[128,512]{1,0:T(8,128)(2,1)S(1)}, u32[]{:S(2)}, u32[]{:S(2)}) collective-permute-start(bf16[128,512]{1,0:T(8,128)(2,1)S(1)} %fusion.4), channel_id=1, source_target_pairs={{0,4},{1,5},{2,6},{3,7},{4,0},{5,1},{6,2},{7,3},{8,12},{9,13},{10,... | collective-permute-start | bytes 393224 | tf_op jit(solution)/shard_map/ppermute | solution.py:199
  45.1 1.4 %collective-permute-start.16 = (bf16[128,512]{1,0:T(8,128)(2,1)S(1)}, bf16[128,512]{1,0:T(8,128)(2,1)S(1)}, u32[]{:S(2)}, u32[]{:S(2)}) collective-permute-start(bf16[128,512]{1,0:T(8,128)(2,1)S(1)} %fusion.5), channel_id=1, source_target_pairs={{0,4},{1,5},{2,6},{3,7},{4,0},{5,1},{6,2},{7,3},{8,12},{9,13},{10,... | collective-permute-start | bytes 393224 | tf_op jit(solution)/shard_map/ppermute | solution.py:199
  46.5 2.4 %collective-permute-done.10 = bf16[128,512]{1,0:T(8,128)(2,1)S(1)} collective-permute-done((bf16[128,512]{1,0:T(8,128)(2,1)S(1)}, bf16[128,512]{1,0:T(8,128)(2,1)S(1)}, u32[]{:S(2)}, u32[]{:S(2)}) %collective-permute-start.10) | collective-permute-done | bytes 131104 | tf_op jit(solution)/shard_map/ppermute | solution.py:199
  48.9 8.2 %collective-permute-start.11 = (bf16[64,512]{1,0:T(8,128)(2,1)S(1)}, bf16[64,512]{1,0:T(8,128)(2,1)S(1)}, u32[]{:S(2)}, u32[]{:S(2)}) collective-permute-start(bf16[64,512]{1,0:T(8,128)(2,1)S(1)} %get-tuple-element.26), channel_id=1, source_target_pairs={{0,1},{1,0},{2,3},{3,2},{4,5},{5,4},{6,7},{7,6},{8,9},{9,8},{10,11... | collective-permute-start | bytes 196616 | tf_op jit(solution)/shard_map/ppermute | solution.py:241
  57.2 1.3 %collective-permute-start.17 = (bf16[64,512]{1,0:T(8,128)(2,1)S(1)}, bf16[64,512]{1,0:T(8,128)(2,1)S(1)}, u32[]{:S(2)}, u32[]{:S(2)}) collective-permute-start(bf16[64,512]{1,0:T(8,128)(2,1)S(1)} %get-tuple-element.28), channel_id=1, source_target_pairs={{0,1},{1,0},{2,3},{3,2},{4,5},{5,4},{6,7},{7,6},{8,9},{9,8},{10,11... | collective-permute-start | bytes 196616 | tf_op jit(solution)/shard_map/ppermute | solution.py:241
  58.5 0.9 %collective-permute-done.17 = bf16[64,512]{1,0:T(8,128)(2,1)S(1)} collective-permute-done((bf16[64,512]{1,0:T(8,128)(2,1)S(1)}, bf16[64,512]{1,0:T(8,128)(2,1)S(1)}, u32[]{:S(2)}, u32[]{:S(2)}) %collective-permute-start.17) | collective-permute-done | bytes 65568 | tf_op jit(solution)/shard_map/ppermute | solution.py:241
  (31 shorter events, 2.8 us)
Async XLA Ops:
  2.5 25.3 %collective-permute-start.7 = (bf16[4,512,512]{2,1,0:T(8,128)(2,1)S(1)}, bf16[4,512,512]{2,1,0:T(8,128)(2,1)S(1)}, u32[]{:S(2)}, u32[]{:S(2)}) collective-permute-start(bf16[4,512,512]{2,1,0:T(8,128)(2,1)S(1)} %get-tuple-element.18), channel_id=1, source_target_pairs={{0,1},{1,0},{2,3},{3,2},{4,5},{5,4},{6,7},{7,6},{8,9},{9,8},{10,11... | collective-permute-start | bytes 6291464 | tf_op jit(solution)/shard_map/ppermute | solution.py:219
  2.6 9.3 %collective-permute-start.1 = (bf16[256,512]{1,0:T(8,128)(2,1)S(1)}, bf16[256,512]{1,0:T(8,128)(2,1)S(1)}, u32[]{:S(2)}, u32[]{:S(2)}) collective-permute-start(bf16[256,512]{1,0:T(8,128)(2,1)S(1)} %get-tuple-element.15), channel_id=1, source_target_pairs={{0,8},{8,0},{16,24},{24,16},{1,9},{9,1},{17,25},{25,17},{2,10},{10... | collective-permute-start | bytes 786440 | tf_op jit(solution)/shard_map/ppermute | solution.py:218
  11.8 7.2 %collective-permute-start.5 = (bf16[256,512]{1,0:T(8,128)(2,1)S(1)}, bf16[256,512]{1,0:T(8,128)(2,1)S(1)}, u32[]{:S(2)}, u32[]{:S(2)}) collective-permute-start(bf16[256,512]{1,0:T(8,128)(2,1)S(1)} %collective-permute-done.1.refs_0_), channel_id=1, source_target_pairs={{0,16},{8,24},{16,0},{24,8},{1,17},{9,25},{17,1},{25,9},{2,18},{10... | collective-permute-start | bytes 786440 | tf_op jit(solution)/shard_map/ppermute | solution.py:223
  13.2 8.4 %collective-permute-start.3 = (bf16[256,512]{1,0:T(8,128)(2,1)S(1)}, bf16[256,512]{1,0:T(8,128)(2,1)S(1)}, u32[]{:S(2)}, u32[]{:S(2)}) collective-permute-start(bf16[256,512]{1,0:T(8,128)(2,1)S(1)} %get-tuple-element.16), channel_id=1, source_target_pairs={{0,8},{8,0},{16,24},{24,16},{1,9},{9,1},{17,25},{25,17},{2,10},{10... | collective-permute-start | bytes 786440 | tf_op jit(solution)/shard_map/ppermute | solution.py:218
  14.4 11.1 %collective-permute-start.4 = (bf16[256,512]{1,0:T(8,128)(2,1)S(1)}, bf16[256,512]{1,0:T(8,128)(2,1)S(1)}, u32[]{:S(2)}, u32[]{:S(2)}) collective-permute-start(bf16[256,512]{1,0:T(8,128)(2,1)S(1)} %get-tuple-element.17), channel_id=1, source_target_pairs={{0,8},{8,0},{16,24},{24,16},{1,9},{9,1},{17,25},{25,17},{2,10},{10... | collective-permute-start | bytes 786440 | tf_op jit(solution)/shard_map/ppermute | solution.py:218
  14.6 13.1 %collective-permute-start.2 = (bf16[256,512]{1,0:T(8,128)(2,1)S(1)}, bf16[256,512]{1,0:T(8,128)(2,1)S(1)}, u32[]{:S(2)}, u32[]{:S(2)}) collective-permute-start(bf16[256,512]{1,0:T(8,128)(2,1)S(1)} %collective-permute-done.1.refs_0_), channel_id=1, source_target_pairs={{0,2},{1,3},{2,0},{3,1},{4,6},{5,7},{6,4},{7,5},{8,10},{9,11},{10,... | collective-permute-start | bytes 786440 | tf_op jit(solution)/shard_map/ppermute | solution.py:230
  19.0 8.7 %collective-permute-start.6 = (bf16[256,512]{1,0:T(8,128)(2,1)S(1)}, bf16[256,512]{1,0:T(8,128)(2,1)S(1)}, u32[]{:S(2)}, u32[]{:S(2)}) collective-permute-start(bf16[256,512]{1,0:T(8,128)(2,1)S(1)} %collective-permute-done.5.refs_4_.refs_0_.refs_2_), channel_id=1, source_target_pairs={{0,2},{1,3},{2,0},{3,1},{4,6},{5,7},{6,4},{7,5},{8,10},{9,11},{10,... | collective-permute-start | bytes 786440 | tf_op jit(solution)/shard_map/ppermute | solution.py:231
  21.6 5.0 %collective-permute-start = (s32[2]{0:T(128)S(1)}, s32[2]{0:T(128)S(1)}, u32[]{:S(2)}, u32[]{:S(2)}) collective-permute-start(s32[2]{0:T(128)S(1)} %pad_add_fusion.1), channel_id=1, source_target_pairs={{0,1},{1,0},{2,3},{3,2},{4,5},{5,4},{6,7},{7,6},{8,9},{9,8},{10,11... | collective-permute-start | bytes 32 | tf_op jit(solution)/shard_map/ppermute | solution.py:220
  25.4 7.8 %collective-permute-start.12 = (bf16[256,512]{1,0:T(8,128)(2,1)S(1)}, bf16[256,512]{1,0:T(8,128)(2,1)S(1)}, u32[]{:S(2)}, u32[]{:S(2)}) collective-permute-start(bf16[256,512]{1,0:T(8,128)(2,1)S(1)} %collective-permute-done.3.refs_2_.refs_0_), channel_id=1, source_target_pairs={{0,16},{8,24},{16,0},{24,8},{1,17},{9,25},{17,1},{25,9},{2,18},{10... | collective-permute-start | bytes 786440 | tf_op jit(solution)/shard_map/ppermute | solution.py:223
  26.6 10.4 %collective-permute-start.13 = (bf16[256,512]{1,0:T(8,128)(2,1)}, bf16[256,512]{1,0:T(8,128)(2,1)}, u32[]{:S(2)}, u32[]{:S(2)}) collective-permute-start(bf16[256,512]{1,0:T(8,128)(2,1)} %copy_after.1), channel_id=1, source_target_pairs={{0,16},{8,24},{16,0},{24,8},{1,17},{9,25},{17,1},{25,9},{2,18},{10... | collective-permute-start | bytes 786440 | tf_op jit(solution)/shard_map/ppermute | solution.py:224
  31.0 0.8 %copy-start = (f32[2,128,512]{2,1,0:T(8,128)}, f32[2,128,512]{2,1,0:T(8,128)S(1)}, u32[]{:S(2)}) copy-start(f32[2,128,512]{2,1,0:T(8,128)S(1)} %get-tuple-element.19) | copy-start | bytes 1572868
  31.8 10.3 %collective-permute-start.9 = (bf16[1,128,512]{2,1,0:T(8,128)(2,1)}, bf16[1,128,512]{2,1,0:T(8,128)(2,1)}, u32[]{:S(2)}, u32[]{:S(2)}) collective-permute-start(bf16[1,128,512]{2,1,0:T(8,128)(2,1)} %get-tuple-element.21), channel_id=1, source_target_pairs={{0,2},{1,3},{2,0},{3,1},{4,6},{5,7},{6,4},{7,5},{8,10},{9,11},{10,... | collective-permute-start | bytes 393224 | tf_op jit(solution)/shard_map/ppermute | solution.py:192
  33.1 9.0 %copy-start.1 = (f32[2,128,512]{2,1,0:T(8,128)S(1)}, f32[2,128,512]{2,1,0:T(8,128)}, u32[]{:S(2)}) copy-start(f32[2,128,512]{2,1,0:T(8,128)} %copy-done) | copy-start | bytes 1572868
  33.1 13.4 %collective-permute-start.8 = (bf16[128,512]{1,0:T(8,128)(2,1)S(1)}, bf16[128,512]{1,0:T(8,128)(2,1)S(1)}, u32[]{:S(2)}, u32[]{:S(2)}) collective-permute-start(bf16[128,512]{1,0:T(8,128)(2,1)S(1)} %get-tuple-element.20), channel_id=1, source_target_pairs={{0,2},{1,3},{2,0},{3,1},{4,6},{5,7},{6,4},{7,5},{8,10},{9,11},{10,... | collective-permute-start | bytes 393224 | tf_op jit(solution)/shard_map/ppermute | solution.py:193
  40.2 4.9 %collective-permute-start.15 = (bf16[1,128,512]{2,1,0:T(8,128)(2,1)S(1)}, bf16[1,128,512]{2,1,0:T(8,128)(2,1)S(1)}, u32[]{:S(2)}, u32[]{:S(2)}) collective-permute-start(bf16[1,128,512]{2,1,0:T(8,128)(2,1)S(1)} %get-tuple-element.24), channel_id=1, source_target_pairs={{0,2},{1,3},{2,0},{3,1},{4,6},{5,7},{6,4},{7,5},{8,10},{9,11},{10,... | collective-permute-start | bytes 393224 | tf_op jit(solution)/shard_map/ppermute | solution.py:192
  42.0 15.1 %collective-permute-start.14 = (bf16[128,512]{1,0:T(8,128)(2,1)S(1)}, bf16[128,512]{1,0:T(8,128)(2,1)S(1)}, u32[]{:S(2)}, u32[]{:S(2)}) collective-permute-start(bf16[128,512]{1,0:T(8,128)(2,1)S(1)} %get-tuple-element.23), channel_id=1, source_target_pairs={{0,2},{1,3},{2,0},{3,1},{4,6},{5,7},{6,4},{7,5},{8,10},{9,11},{10,... | collective-permute-start | bytes 393224 | tf_op jit(solution)/shard_map/ppermute | solution.py:193
  43.0 5.8 %collective-permute-start.10 = (bf16[128,512]{1,0:T(8,128)(2,1)S(1)}, bf16[128,512]{1,0:T(8,128)(2,1)S(1)}, u32[]{:S(2)}, u32[]{:S(2)}) collective-permute-start(bf16[128,512]{1,0:T(8,128)(2,1)S(1)} %fusion.4), channel_id=1, source_target_pairs={{0,4},{1,5},{2,6},{3,7},{4,0},{5,1},{6,2},{7,3},{8,12},{9,13},{10,... | collective-permute-start | bytes 393224 | tf_op jit(solution)/shard_map/ppermute | solution.py:199
  45.1 12.0 %collective-permute-start.16 = (bf16[128,512]{1,0:T(8,128)(2,1)S(1)}, bf16[128,512]{1,0:T(8,128)(2,1)S(1)}, u32[]{:S(2)}, u32[]{:S(2)}) collective-permute-start(bf16[128,512]{1,0:T(8,128)(2,1)S(1)} %fusion.5), channel_id=1, source_target_pairs={{0,4},{1,5},{2,6},{3,7},{4,0},{5,1},{6,2},{7,3},{8,12},{9,13},{10,... | collective-permute-start | bytes 393224 | tf_op jit(solution)/shard_map/ppermute | solution.py:199
  48.9 9.6 %collective-permute-start.11 = (bf16[64,512]{1,0:T(8,128)(2,1)S(1)}, bf16[64,512]{1,0:T(8,128)(2,1)S(1)}, u32[]{:S(2)}, u32[]{:S(2)}) collective-permute-start(bf16[64,512]{1,0:T(8,128)(2,1)S(1)} %get-tuple-element.26), channel_id=1, source_target_pairs={{0,1},{1,0},{2,3},{3,2},{4,5},{5,4},{6,7},{7,6},{8,9},{9,8},{10,11... | collective-permute-start | bytes 196616 | tf_op jit(solution)/shard_map/ppermute | solution.py:241
  57.2 2.2 %collective-permute-start.17 = (bf16[64,512]{1,0:T(8,128)(2,1)S(1)}, bf16[64,512]{1,0:T(8,128)(2,1)S(1)}, u32[]{:S(2)}, u32[]{:S(2)}) collective-permute-start(bf16[64,512]{1,0:T(8,128)(2,1)S(1)} %get-tuple-element.28), channel_id=1, source_target_pairs={{0,1},{1,0},{2,3},{3,2},{4,5},{5,4},{6,7},{7,6},{8,9},{9,8},{10,11... | collective-permute-start | bytes 196616 | tf_op jit(solution)/shard_map/ppermute | solution.py:241

commit v3 on v2

--- a/solution.py
+++ b/solution.py
@@ -41,21 +41,26 @@
             pltpu.make_async_copy(psi_ref.at[sector, core, pl.ds(start * rows, rows)], part, sem.at[n])
             for n, (part, sector, start) in enumerate(zip(parts, (odd, 1 - odd, 1 - odd), (half, 0, 1), strict=True))
         ]
-        copies.append(pltpu.make_async_copy(left_ref.at[0], pack.at[pl.ds(0, 2)], sem.at[3]))
-        copies.append(pltpu.make_async_copy(right_ref.at[0], pack.at[pl.ds(2, 2)], sem.at[4]))
+        for k, ref in enumerate((left_ref, right_ref)):
+            for s in range(2):
+                at = pl.ds((2 * k + s) * size, size)
+                copies.append(pltpu.make_async_copy(ref.at[0, s], pack.at[at], sem.at[3 + 2 * k + s]))
         for copy in copies:
             copy.start()
+        number = lax.broadcasted_iota(jnp.int32, (16, size), 0)
+        flags = jnp.where(number < 8, place_ref[4], place_ref[5])
+        pack[pl.ds(4 * size, 16)] = flags.astype(jnp.float32).astype(pack.dtype)
         for copy in copies:
             copy.wait()
 
-    out = [pltpu.VMEM((rows, size), psi.dtype)] * 3 + [pltpu.VMEM((4, size, size), psi.dtype)]
+    out = [pltpu.VMEM((rows, size), psi.dtype)] * 3 + [pltpu.VMEM((4 * size + 16, size), psi.dtype)]
     *parts, pack = call(
         body,
         "cut",
         out_shape=out,
         in_specs=[SMEM_SPEC] + [ANY_SPEC] * 3,
-        out_specs=[VMEM_SPEC] * len(out),
-        scratch_shapes=[pltpu.SemaphoreType.DMA((5,))],
+        out_specs=[VMEM_SPEC] * 4,
+        scratch_shapes=[pltpu.SemaphoreType.DMA((7,))],
     )(place, in_hbm(psi), in_hbm(left), in_hbm(right))
     return parts, pack
 
@@ -77,20 +82,26 @@
     )(in_vmem(part), *after)
 
 
-def piece(step, secs, chips, scalars, halo, swapped, pack1, psi, left0, right0):
+def piece(step, secs, chips, bits, scalars, halo, swapped, pack1, psi, left0, right0):
+    def relative(q):
+        return sum((q >> k & 1) << bit for k, bit in enumerate(bits))
+
     size = psi.shape[-1]
+    parked = step == 0
     slots, height, count = len(halo), size // chips, chips // 2
     rows = size // 2
     near = [part for block in halo for part in block] + [pack1]
     far = [psi, left0, right0]
 
-    def body(place, shift0, live0, other, *refs):
+    def body(place, *refs):
         halves, pack, refs = refs[: 2 * slots], refs[2 * slots], refs[2 * slots + 1 :]
-        psi_ref, left_ref, right_ref, stay, first, final, own, left, right, inner, sem = refs
+        psi_ref, left_ref, right_ref, stay, gone, own, left, right, inner, kept, sem = refs
         core, odd, i, z = place[0], place[1], place[2], place[3]
         sector = step * odd + (1 - step) * (1 - odd)
+        flags = pack[pl.ds(4 * size, 16), pl.ds(0, 128)].astype(jnp.float32)
+        shift1, live1 = (jnp.max(part).astype(jnp.int32) for part in (flags[:8], flags[8:]))
         slot_of, weight_of = [], []
-        for shift, live in zip((shift0[0], other[0]), (live0[0], other[1])):
+        for shift, live in ((place[4], place[5]), (shift1, live1)):
             rel = sector - shift
             at = step - (2 * odd - 1) * shift
             if step == 0:
@@ -113,16 +124,18 @@
         left_copy.start()
         right_copy.start()
 
-        order = [*range(1, chips, 2), *range(0, chips, 2)]
+        order = [relative(q) for q in [*range(1, chips, 2), *range(0, chips, 2)]]
         for term in (1, 0):
             if term == 0:
                 left_copy.wait()
 
             def left_rows(group, column, term=term):
                 def at(r, k):
-                    block = pl.ds(pl.multiple_of((z ^ r) * height + (core ^ k) * (height // 2), height // 2), height // 2)
+                    start = (z ^ r) * height + (core ^ k) * (height // 2)
+                    start = start if term == 0 else start + sector * size
+                    block = pl.ds(pl.multiple_of(start, height // 2), height // 2)
                     columns = pl.ds(pl.multiple_of(column * rows, 128), rows)
-                    return left[block, columns] if term == 0 else pack[sector, block, columns]
+                    return left[block, columns] if term == 0 else pack[block, columns]
 
                 return jnp.concatenate([at(r, k) for r in order[group * count : (group + 1) * count] for k in range(2)])
 
@@ -147,11 +160,12 @@
                 first_product([lambda n=n: own[term, pl.ds(n * rows, rows)] for n in range(2)], [0, 1])
 
         right_copy.wait()
-        for group in range(2):
+        stay_copy = pltpu.make_async_copy(kept, stay, sem.at[4]) if parked else None
+        for group in (1, 0):
             total = sum(
                 lax.dot_general(
                     inner[term, pl.ds(group * rows, rows)],
-                    right[...] if term == 0 else pack[2 + sector],
+                    right[...] if term == 0 else pack[pl.ds(pl.multiple_of((2 + sector) * size, size), size)],
                     (((1,), (1,)), ((), ())),
                     preferred_element_type=jnp.float32,
                 )
@@ -160,49 +174,41 @@
             )
             for n in range(count):
                 block = total[n * height : (n + 1) * height]
-                if group == 1:
-                    stay[n] = block
-                elif n == 0:
-                    final[...] = block.astype(final.dtype)
+                if group == 0:
+                    gone[n] = block.astype(gone.dtype)
                 else:
-                    first[n - 1] = block.astype(first.dtype)
-
+                    (kept if parked else stay)[n] = block
+            if group == 1 and parked:
+                stay_copy.start()
+        if parked:
+            stay_copy.wait()
+
+    stay_shape = (count, height, size)
+    outs = [pltpu.HBM(stay_shape, jnp.float32) if parked else pltpu.VMEM(stay_shape, jnp.float32)]
+    outs.append(pltpu.VMEM(stay_shape, jnp.bfloat16))
     return call(
         body,
         "piece",
-        out_shape=(
-            pltpu.VMEM((count, height, size), jnp.float32),
-            pltpu.VMEM((count - 1, height, size), jnp.bfloat16),
-            pltpu.VMEM((height, size), jnp.bfloat16),
-        ),
-        in_specs=[SMEM_SPEC] * 4 + [VMEM_SPEC] * len(near) + [ANY_SPEC] * len(far),
-        out_specs=(VMEM_SPEC,) * 3,
+        out_shape=outs,
+        in_specs=[SMEM_SPEC] + [VMEM_SPEC] * len(near) + [ANY_SPEC] * len(far),
+        out_specs=[ANY_SPEC if parked else VMEM_SPEC] + [VMEM_SPEC] * (len(outs) - 1),
         scratch_shapes=[
             pltpu.VMEM((2, size, size), jnp.bfloat16),
             pltpu.VMEM((size, size), jnp.bfloat16),
             pltpu.VMEM((size, size), jnp.bfloat16),
             pltpu.VMEM((2, size, size), jnp.bfloat16),
-            pltpu.SemaphoreType.DMA((4,)),
+            pltpu.VMEM((count, height, size), jnp.float32),
+            pltpu.SemaphoreType.DMA((5,)),
         ],
     )(*scalars, *[in_vmem(x) for x in near], *[in_hbm(x) for x in far])
 
 
-def sum_over_chips(stay, first, final, terms):
-    pairs = [(d, d ^ 2) for d in range(terms)]
-    got = lax.ppermute(first, "term", pairs)
-    last = lax.ppermute(final, "term", pairs)
-    mid = stay[1:] + got.astype(jnp.float32)
-    keep = stay[0] + last.astype(jnp.float32)
-    step = 4
-    while step < terms:
-        pairs = [(d, d ^ step) for d in range(terms)]
-        last = lax.ppermute(mid[0].astype(jnp.bfloat16), "term", pairs)
-        keep = keep + last.astype(jnp.float32)
-        if mid.shape[0] > 1:
-            got = lax.ppermute(mid[2::2].astype(jnp.bfloat16), "term", pairs)
-            mid = mid[1::2] + got.astype(jnp.float32)
-        step *= 2
-    return keep
+def sum_over_chips(stay, gone, bits, terms):
+    for bit in bits:
+        pairs = [(d, d ^ (2 << bit)) for d in range(terms)]
+        total = stay + lax.ppermute(gone, "term", pairs).astype(jnp.float32)
+        stay, gone = total[::2], total[1::2].astype(jnp.bfloat16)
+    return stay[0]
 
 
 def local(psi, left_ops, right_ops, shift, live):
@@ -213,11 +219,10 @@
     cores = [(d, d ^ 1) for d in range(terms)]
     pairs = [(d, d ^ 1) for d in range(secs)]
 
-    place = jnp.stack([core, odd, i, z]).astype(jnp.int32)
+    place = jnp.stack([core, odd, i, z, shift[0], live[0]]).astype(jnp.int32)
     parts, pack0 = cut(place, psi, left_ops, right_ops)
     near = [lax.ppermute(part, "sec", pairs) for part in parts]
     pack1 = lax.ppermute(pack0, "term", cores)
-    other = lax.ppermute(jnp.concatenate([shift, live]), "term", cores)
     if secs == 4:
         turn = [(d, d ^ 2) for d in range(secs)]
         far = [lax.ppermute(part, "sec", turn) for part in near[:2]]
@@ -228,15 +233,16 @@
         far = [lax.ppermute(part, "sec", nexts) for part in parts]
     planes = [(d, d ^ 2) for d in range(terms)]
     near_first, near_second = (near[0], lax.ppermute(near[0], "term", planes)), near[1:]
-    far_first, far_second = (far[0], lax.ppermute(far[0], "term", planes)), far[1:]
-
-    scalars = (place, shift, live, other)
+    far_first, far_second = (far[0], lax.ppermute(copy_after(far[0], near[1]), "term", planes)), far[1:]
+
+    scalars = (place,)
     outs = []
     for step in range(2):
         halo = (near_first, near_second, far_first) if step == 0 else (near_second, far_first, far_second)
         swapped = (True, False, True) if step == 0 else (False, True, False)
-        blocks = piece(step, secs, terms // 2, scalars, halo, swapped, pack1, psi, left_ops, right_ops)
-        total = sum_over_chips(*blocks, terms).astype(jnp.bfloat16)
+        bits = list(range((terms // 2).bit_length() - 1))
+        blocks = piece(step, secs, terms // 2, bits, scalars, halo, swapped, pack1, psi, left_ops, right_ops)
+        total = sum_over_chips(*blocks, bits, terms).astype(jnp.bfloat16)
         mine, others = total[: size // terms], total[size // terms :]
         got = lax.ppermute(others, "term", cores)
         outs.append(jnp.where(core == 0, jnp.stack([mine, got]), jnp.stack([got, mine])))

time: 60.8 us -> 59 us (0.970)
  waiting for transfers between devices: 18.5 us -> 26.1 us
  starting transfers between devices: 27.9 us -> 21 us
  other arithmetic: 1.98 us -> 0.97 us
  Pallas kernels: 9.59 us -> 8.83 us
  local copies, waits for them, and re-layouts: 0.83 us -> 0.15 us
    ppermute x8 -> x5, waiting for transfers between devices: 2.38 us -> 13.5 us  [the longest x4 10.9 us: sum_over_chips(): total = stay + lax.ppermute(gone, 'term', pairs).astype(jnp.float32)]
    ppermute x2, starting transfers between devices: 9.49 us -> 4.52 us  [local(): got = lax.ppermute(others, 'term', cores)]
    ppermute x1, waiting for transfers between devices: 3.66 us -> 0.01 us  [local(): far.append(lax.ppermute(copy_after(near[2], far[0]), 'sec', turn))]
    ppermute x8 -> x5, starting transfers between devices: 9.98 us -> 7.25 us  [the longest x4 6.21 us: sum_over_chips(): total = stay + lax.ppermute(gone, 'term', pairs).astype(jnp.float32)]
    ppermute x3, waiting for transfers between devices: 8.43 us -> 10.4 us  [local(): near = [lax.ppermute(part, 'sec', pairs) for part in parts]]
    ppermute x2, waiting for transfers between devices: 3.12 us -> 1.29 us  [local(): far = [lax.ppermute(part, 'sec', turn) for part in near[:2]]]
    convert_element_type x4 -> x2, other arithmetic: 1.07 us -> 0.06 us  [local(): total = sum_over_chips(*blocks, bits, terms).astype(jnp.bfloat16)]
    ppermute x2, starting transfers between devices: 1.67 us -> 2.55 us  [local(): far = [lax.ppermute(part, 'sec', turn) for part in near[:2]]]
  transfers between devices with their start and end apart: 18 -> 15, of which waited for: 6 -> 9; matrix products, arithmetic and copies ran while one was open for 2% -> 0% of each run, Pallas kernels for 12% -> 11%
where the time goes in v3:
time: 59 us; the launch traced here: 58.5 us
  waiting for transfers between devices  26.1 us (44%)
  starting transfers between devices  21 us (36%)
  Pallas kernels  8.83 us (15%)
  between operations  1.43 us (2%)
  other arithmetic  0.97 us (2%)
    ppermute x4, waiting for transfers between devices, sum_over_chips(): total = stay + lax.ppermute(gone, 'term', pairs).astype(jnp.float32)  10.9 us
    ppermute x3, waiting for transfers between devices, local(): near = [lax.ppermute(part, 'sec', pairs) for part in parts]  10.4 us
    pallas_call x2, Pallas kernels, piece(): call(body, 'piece', out_shape=outs, in_specs=[SMEM_SPEC] + [VMEM_SPEC] *...  6.41 us
    ppermute x4, starting transfers between devices, sum_over_chips(): total = stay + lax.ppermute(gone, 'term', pairs).astype(jnp.float32)  6.21 us
    ppermute x2, starting transfers between devices, local(): got = lax.ppermute(others, 'term', cores)  4.52 us
    ppermute x3, starting transfers between devices, local(): near = [lax.ppermute(part, 'sec', pairs) for part in parts]  3.9 us
    ppermute x1, waiting for transfers between devices, local(): lax.ppermute(copy_after(far[0], near[1]), 'term', planes)  2.61 us
    ppermute x2, starting transfers between devices, local(): far = [lax.ppermute(part, 'sec', turn) for part in near[:2]]  2.55 us
  transfers between devices with their start and end apart: 15, of which 9 were waited for; matrix products, arithmetic and copies ran while one was open for 0% of the time, Pallas kernels for 11%

profile of v3, /device:TPU:1, one launch (start us, length us, event | category | flops | bytes accessed | tf_op | source)
XLA Modules:
  0.0 58.5 jit_solution(4639525600673075606)
XLA Ops:
  1.4 2.4 %cut.1 = (bf16[256,512]{1,0:T(8,128)(2,1)S(1)}, bf16[256,512]{1,0:T(8,128)(2,1)S(1)}, bf16[256,512]{1,0:T(8,128)(2,1)S(1)}, bf16[2064,512]{1,0:T(8,128)(2,1)S(1)}) custom-call(s32[6]{0:T(128)S(1)} %stack.57.place_ref.place, bf16[2,2,512,512]{3,2,1,0:T(8,128)(2,1)} %refs_7_.3, bf16[1,2,512,512]{3,2,1,0:T(8,128)(2,1)} %refs_8_.3, bf16[1,2,512,512]{3,2,1,0:T(8,128)(2,1)} %refs_9_.3), custom_call_target="tpu_custom_call" | custom-call | flops 1000 | bytes 1000 | tf_op jit(solution)/shard_map/cut/pallas_call | solution.py:57
  3.9 2.7 %collective-permute-start = (bf16[256,512]{1,0:T(8,128)(2,1)S(1)}, bf16[256,512]{1,0:T(8,128)(2,1)S(1)}, u32[]{:S(2)}, u32[]{:S(2)}) collective-permute-start(bf16[256,512]{1,0:T(8,128)(2,1)S(1)} %get-tuple-element.13), channel_id=1, source_target_pairs={{0,8},{8,0},{16,24},{24,16},{1,9},{9,1},{17,25},{25,17},{2,10},{10... | collective-permute-start | bytes 786440 | tf_op jit(solution)/shard_map/ppermute | solution.py:224
  6.6 6.6 %collective-permute-done.refs_0_ = bf16[256,512]{1,0:T(8,128)(2,1)S(1)} collective-permute-done((bf16[256,512]{1,0:T(8,128)(2,1)S(1)}, bf16[256,512]{1,0:T(8,128)(2,1)S(1)}, u32[]{:S(2)}, u32[]{:S(2)}) %collective-permute-start) | collective-permute-done | bytes 262176 | tf_op jit(solution)/shard_map/ppermute | solution.py:224
  13.2 1.3 %collective-permute-start.4 = (bf16[256,512]{1,0:T(8,128)(2,1)S(1)}, bf16[256,512]{1,0:T(8,128)(2,1)S(1)}, u32[]{:S(2)}, u32[]{:S(2)}) collective-permute-start(bf16[256,512]{1,0:T(8,128)(2,1)S(1)} %collective-permute-done.refs_0_), channel_id=1, source_target_pairs={{0,16},{8,24},{16,0},{24,8},{1,17},{9,25},{17,1},{25,9},{2,18},{10... | collective-permute-start | bytes 786440 | tf_op jit(solution)/shard_map/ppermute | solution.py:228
  14.5 1.2 %collective-permute-start.3 = (bf16[256,512]{1,0:T(8,128)(2,1)S(1)}, bf16[256,512]{1,0:T(8,128)(2,1)S(1)}, u32[]{:S(2)}, u32[]{:S(2)}) collective-permute-start(bf16[256,512]{1,0:T(8,128)(2,1)S(1)} %get-tuple-element.15), channel_id=1, source_target_pairs={{0,8},{8,0},{16,24},{24,16},{1,9},{9,1},{17,25},{25,17},{2,10},{10... | collective-permute-start | bytes 786440 | tf_op jit(solution)/shard_map/ppermute | solution.py:224
  15.7 1.3 %collective-permute-start.1 = (bf16[256,512]{1,0:T(8,128)(2,1)S(1)}, bf16[256,512]{1,0:T(8,128)(2,1)S(1)}, u32[]{:S(2)}, u32[]{:S(2)}) collective-permute-start(bf16[256,512]{1,0:T(8,128)(2,1)S(1)} %collective-permute-done.refs_0_), channel_id=1, source_target_pairs={{0,2},{1,3},{2,0},{3,1},{4,6},{5,7},{6,4},{7,5},{8,10},{9,11},{10,... | collective-permute-start | bytes 786440 | tf_op jit(solution)/shard_map/ppermute | solution.py:235
  17.0 1.8 %collective-permute-done.2.refs_0_.refs_2_ = bf16[256,512]{1,0:T(8,128)(2,1)S(1)} collective-permute-done((bf16[256,512]{1,0:T(8,128)(2,1)S(1)}, bf16[256,512]{1,0:T(8,128)(2,1)S(1)}, u32[]{:S(2)}, u32[]{:S(2)}) %collective-permute-start.2) | collective-permute-done | bytes 262176 | tf_op jit(solution)/shard_map/ppermute | solution.py:224
  18.8 1.3 %collective-permute-done.4.part_ref.refs_4_.refs_0_.refs_2_ = bf16[256,512]{1,0:T(8,128)(2,1)S(1)} collective-permute-done((bf16[256,512]{1,0:T(8,128)(2,1)S(1)}, bf16[256,512]{1,0:T(8,128)(2,1)S(1)}, u32[]{:S(2)}, u32[]{:S(2)}) %collective-permute-start.4) | collective-permute-done | bytes 262176 | tf_op jit(solution)/shard_map/ppermute | solution.py:228
  20.1 1.0 %collective-permute-start.5 = (bf16[256,512]{1,0:T(8,128)(2,1)S(1)}, bf16[256,512]{1,0:T(8,128)(2,1)S(1)}, u32[]{:S(2)}, u32[]{:S(2)}) collective-permute-start(bf16[256,512]{1,0:T(8,128)(2,1)S(1)} %copy_after.2), channel_id=1, source_target_pairs={{0,2},{1,3},{2,0},{3,1},{4,6},{5,7},{6,4},{7,5},{8,10},{9,11},{10,... | collective-permute-start | bytes 786440 | tf_op jit(solution)/shard_map/ppermute | solution.py:236
  21.1 1.2 %collective-permute-start.10 = (bf16[256,512]{1,0:T(8,128)(2,1)S(1)}, bf16[256,512]{1,0:T(8,128)(2,1)S(1)}, u32[]{:S(2)}, u32[]{:S(2)}) collective-permute-start(bf16[256,512]{1,0:T(8,128)(2,1)S(1)} %collective-permute-done.2.refs_0_.refs_2_), channel_id=1, source_target_pairs={{0,16},{8,24},{16,0},{24,8},{1,17},{9,25},{17,1},{25,9},{2,18},{10... | collective-permute-start | bytes 786440 | tf_op jit(solution)/shard_map/ppermute | solution.py:228
  22.4 2.0 %collective-permute-done.3.refs_3_.part_ref.refs_1_ = bf16[256,512]{1,0:T(8,128)(2,1)S(1)} collective-permute-done((bf16[256,512]{1,0:T(8,128)(2,1)S(1)}, bf16[256,512]{1,0:T(8,128)(2,1)S(1)}, u32[]{:S(2)}, u32[]{:S(2)}) %collective-permute-start.3) | collective-permute-done | bytes 262176 | tf_op jit(solution)/shard_map/ppermute | solution.py:224
  24.4 1.4 %collective-permute-start.11 = (bf16[256,512]{1,0:T(8,128)(2,1)S(1)}, bf16[256,512]{1,0:T(8,128)(2,1)S(1)}, u32[]{:S(2)}, u32[]{:S(2)}) collective-permute-start(bf16[256,512]{1,0:T(8,128)(2,1)S(1)} %copy_after.3), channel_id=1, source_target_pairs={{0,16},{8,24},{16,0},{24,8},{1,17},{9,25},{17,1},{25,9},{2,18},{10... | collective-permute-start | bytes 786440 | tf_op jit(solution)/shard_map/ppermute | solution.py:229
  25.8 2.6 %collective-permute-done.5.refs_5_.refs_3_ = bf16[256,512]{1,0:T(8,128)(2,1)S(1)} collective-permute-done((bf16[256,512]{1,0:T(8,128)(2,1)S(1)}, bf16[256,512]{1,0:T(8,128)(2,1)S(1)}, u32[]{:S(2)}, u32[]{:S(2)}) %collective-permute-start.5) | collective-permute-done | bytes 262176 | tf_op jit(solution)/shard_map/ppermute | solution.py:236
  28.4 3.5 %piece.2 = (f32[2,128,512]{2,1,0:T(8,128)}, bf16[2,128,512]{2,1,0:T(8,128)(2,1)S(1)}) custom-call(s32[6]{0:T(128)S(1)} %stack.57.place_ref.place, bf16[256,512]{1,0:T(8,128)(2,1)S(1)} %collective-permute-done.refs_0_, bf16[256,512]{1,0:T(8,128)(2,1)S(1)} %collective-permute-done.1.refs_1_, bf16[256,512]{1,0:T(8,128)(2,1)S(1)} %collective-permute-done.2.refs_0_.refs_2_, ...), custom_call_target="tpu_custom_call" | custom-call | flops 1000 | bytes 1000 | tf_op jit(solution)/shard_map/piece/pallas_call | solution.py:189
  31.9 1.3 %collective-permute-start.7 = (bf16[2,128,512]{2,1,0:T(8,128)(2,1)S(1)}, bf16[2,128,512]{2,1,0:T(8,128)(2,1)S(1)}, u32[]{:S(2)}, u32[]{:S(2)}) collective-permute-start(bf16[2,128,512]{2,1,0:T(8,128)(2,1)S(1)} %get-tuple-element.18), channel_id=1, source_target_pairs={{0,2},{1,3},{2,0},{3,1},{4,6},{5,7},{6,4},{7,5},{8,10},{9,11},{10,... | collective-permute-start | bytes 786440 | tf_op jit(solution)/shard_map/ppermute | solution.py:209
  33.2 2.9 %piece.3 = (f32[2,128,512]{2,1,0:T(8,128)S(1)}, bf16[2,128,512]{2,1,0:T(8,128)(2,1)S(1)}) custom-call(s32[6]{0:T(128)S(1)} %stack.57.place_ref.place, bf16[256,512]{1,0:T(8,128)(2,1)S(1)} %collective-permute-done.2.refs_0_.refs_2_, bf16[256,512]{1,0:T(8,128)(2,1)S(1)} %collective-permute-done.3.refs_3_.part_ref.refs_1_, ...), custom_call_target="tpu_custom_call" | custom-call | flops 1000 | bytes 1000 | tf_op jit(solution)/shard_map/piece/pallas_call | solution.py:189
  36.2 1.5 %collective-permute-start.12 = (bf16[2,128,512]{2,1,0:T(8,128)(2,1)S(1)}, bf16[2,128,512]{2,1,0:T(8,128)(2,1)S(1)}, u32[]{:S(2)}, u32[]{:S(2)}) collective-permute-start(bf16[2,128,512]{2,1,0:T(8,128)(2,1)S(1)} %get-tuple-element.20), channel_id=1, source_target_pairs={{0,2},{1,3},{2,0},{3,1},{4,6},{5,7},{6,4},{7,5},{8,10},{9,11},{10,... | collective-permute-start | bytes 786440 | tf_op jit(solution)/shard_map/ppermute | solution.py:209
  38.3 1.9 %collective-permute-start.8 = (bf16[1,128,512]{2,1,0:T(8,128)(2,1)S(1)}, bf16[1,128,512]{2,1,0:T(8,128)(2,1)S(1)}, u32[]{:S(2)}, u32[]{:S(2)}) collective-permute-start(bf16[1,128,512]{2,1,0:T(8,128)(2,1)S(1)} %slice.69), channel_id=1, source_target_pairs={{0,4},{1,5},{2,6},{3,7},{4,0},{5,1},{6,2},{7,3},{8,12},{9,13},{10,... | collective-permute-start | bytes 393224 | tf_op jit(solution)/shard_map/ppermute | solution.py:209
  40.1 5.6 %collective-permute-done.12 = bf16[2,128,512]{2,1,0:T(8,128)(2,1)S(1)} collective-permute-done((bf16[2,128,512]{2,1,0:T(8,128)(2,1)S(1)}, bf16[2,128,512]{2,1,0:T(8,128)(2,1)S(1)}, u32[]{:S(2)}, u32[]{:S(2)}) %collective-permute-start.12) | collective-permute-done | bytes 262176 | tf_op jit(solution)/shard_map/ppermute | solution.py:209
  45.8 1.5 %collective-permute-start.13 = (bf16[1,128,512]{2,1,0:T(8,128)(2,1)S(1)}, bf16[1,128,512]{2,1,0:T(8,128)(2,1)S(1)}, u32[]{:S(2)}, u32[]{:S(2)}) collective-permute-start(bf16[1,128,512]{2,1,0:T(8,128)(2,1)S(1)} %slice.68), channel_id=1, source_target_pairs={{0,4},{1,5},{2,6},{3,7},{4,0},{5,1},{6,2},{7,3},{8,12},{9,13},{10,... | collective-permute-start | bytes 393224 | tf_op jit(solution)/shard_map/ppermute | solution.py:209
  47.4 3.1 %collective-permute-start.9 = (bf16[64,512]{1,0:T(8,128)(2,1)S(1)}, bf16[64,512]{1,0:T(8,128)(2,1)S(1)}, u32[]{:S(2)}, u32[]{:S(2)}) collective-permute-start(bf16[64,512]{1,0:T(8,128)(2,1)S(1)} %get-tuple-element.22), channel_id=1, source_target_pairs={{0,1},{1,0},{2,3},{3,2},{4,5},{5,4},{6,7},{7,6},{8,9},{9,8},{10,11... | collective-permute-start | bytes 196616 | tf_op jit(solution)/shard_map/ppermute | solution.py:247
  50.6 4.9 %collective-permute-done.13 = bf16[1,128,512]{2,1,0:T(8,128)(2,1)S(1)} collective-permute-done((bf16[1,128,512]{2,1,0:T(8,128)(2,1)S(1)}, bf16[1,128,512]{2,1,0:T(8,128)(2,1)S(1)}, u32[]{:S(2)}, u32[]{:S(2)}) %collective-permute-start.13) | collective-permute-done | bytes 131104 | tf_op jit(solution)/shard_map/ppermute | solution.py:209
  55.5 1.4 %collective-permute-start.14 = (bf16[64,512]{1,0:T(8,128)(2,1)S(1)}, bf16[64,512]{1,0:T(8,128)(2,1)S(1)}, u32[]{:S(2)}, u32[]{:S(2)}) collective-permute-start(bf16[64,512]{1,0:T(8,128)(2,1)S(1)} %get-tuple-element.24), channel_id=1, source_target_pairs={{0,1},{1,0},{2,3},{3,2},{4,5},{5,4},{6,7},{7,6},{8,9},{9,8},{10,11... | collective-permute-start | bytes 196616 | tf_op jit(solution)/shard_map/ppermute | solution.py:247
  56.9 0.9 %collective-permute-done.14 = bf16[64,512]{1,0:T(8,128)(2,1)S(1)} collective-permute-done((bf16[64,512]{1,0:T(8,128)(2,1)S(1)}, bf16[64,512]{1,0:T(8,128)(2,1)S(1)}, u32[]{:S(2)}, u32[]{:S(2)}) %collective-permute-start.14) | collective-permute-done | bytes 65568 | tf_op jit(solution)/shard_map/ppermute | solution.py:247
  (25 shorter events, 1.8 us)
Async XLA Ops:
  3.8 24.6 %collective-permute-start.6 = (bf16[2064,512]{1,0:T(8,128)(2,1)S(1)}, bf16[2064,512]{1,0:T(8,128)(2,1)S(1)}, u32[]{:S(2)}, u32[]{:S(2)}) collective-permute-start(bf16[2064,512]{1,0:T(8,128)(2,1)S(1)} %get-tuple-element.16), channel_id=1, source_target_pairs={{0,1},{1,0},{2,3},{3,2},{4,5},{5,4},{6,7},{7,6},{8,9},{9,8},{10,11... | collective-permute-start | bytes 6340616 | tf_op jit(solution)/shard_map/ppermute | solution.py:225
  3.9 9.3 %collective-permute-start = (bf16[256,512]{1,0:T(8,128)(2,1)S(1)}, bf16[256,512]{1,0:T(8,128)(2,1)S(1)}, u32[]{:S(2)}, u32[]{:S(2)}) collective-permute-start(bf16[256,512]{1,0:T(8,128)(2,1)S(1)} %get-tuple-element.13), channel_id=1, source_target_pairs={{0,8},{8,0},{16,24},{24,16},{1,9},{9,1},{17,25},{25,17},{2,10},{10... | collective-permute-start | bytes 786440 | tf_op jit(solution)/shard_map/ppermute | solution.py:224
  6.6 12.2 %collective-permute-start.2 = (bf16[256,512]{1,0:T(8,128)(2,1)S(1)}, bf16[256,512]{1,0:T(8,128)(2,1)S(1)}, u32[]{:S(2)}, u32[]{:S(2)}) collective-permute-start(bf16[256,512]{1,0:T(8,128)(2,1)S(1)} %get-tuple-element.14), channel_id=1, source_target_pairs={{0,8},{8,0},{16,24},{24,16},{1,9},{9,1},{17,25},{25,17},{2,10},{10... | collective-permute-start | bytes 786440 | tf_op jit(solution)/shard_map/ppermute | solution.py:224
  13.2 6.9 %collective-permute-start.4 = (bf16[256,512]{1,0:T(8,128)(2,1)S(1)}, bf16[256,512]{1,0:T(8,128)(2,1)S(1)}, u32[]{:S(2)}, u32[]{:S(2)}) collective-permute-start(bf16[256,512]{1,0:T(8,128)(2,1)S(1)} %collective-permute-done.refs_0_), channel_id=1, source_target_pairs={{0,16},{8,24},{16,0},{24,8},{1,17},{9,25},{17,1},{25,9},{2,18},{10... | collective-permute-start | bytes 786440 | tf_op jit(solution)/shard_map/ppermute | solution.py:228
  14.5 9.9 %collective-permute-start.3 = (bf16[256,512]{1,0:T(8,128)(2,1)S(1)}, bf16[256,512]{1,0:T(8,128)(2,1)S(1)}, u32[]{:S(2)}, u32[]{:S(2)}) collective-permute-start(bf16[256,512]{1,0:T(8,128)(2,1)S(1)} %get-tuple-element.15), channel_id=1, source_target_pairs={{0,8},{8,0},{16,24},{24,16},{1,9},{9,1},{17,25},{25,17},{2,10},{10... | collective-permute-start | bytes 786440 | tf_op jit(solution)/shard_map/ppermute | solution.py:224
  15.7 10.1 %collective-permute-start.1 = (bf16[256,512]{1,0:T(8,128)(2,1)S(1)}, bf16[256,512]{1,0:T(8,128)(2,1)S(1)}, u32[]{:S(2)}, u32[]{:S(2)}) collective-permute-start(bf16[256,512]{1,0:T(8,128)(2,1)S(1)} %collective-permute-done.refs_0_), channel_id=1, source_target_pairs={{0,2},{1,3},{2,0},{3,1},{4,6},{5,7},{6,4},{7,5},{8,10},{9,11},{10,... | collective-permute-start | bytes 786440 | tf_op jit(solution)/shard_map/ppermute | solution.py:235
  20.1 8.3 %collective-permute-start.5 = (bf16[256,512]{1,0:T(8,128)(2,1)S(1)}, bf16[256,512]{1,0:T(8,128)(2,1)S(1)}, u32[]{:S(2)}, u32[]{:S(2)}) collective-permute-start(bf16[256,512]{1,0:T(8,128)(2,1)S(1)} %copy_after.2), channel_id=1, source_target_pairs={{0,2},{1,3},{2,0},{3,1},{4,6},{5,7},{6,4},{7,5},{8,10},{9,11},{10,... | collective-permute-start | bytes 786440 | tf_op jit(solution)/shard_map/ppermute | solution.py:236
  21.1 12.1 %collective-permute-start.10 = (bf16[256,512]{1,0:T(8,128)(2,1)S(1)}, bf16[256,512]{1,0:T(8,128)(2,1)S(1)}, u32[]{:S(2)}, u32[]{:S(2)}) collective-permute-start(bf16[256,512]{1,0:T(8,128)(2,1)S(1)} %collective-permute-done.2.refs_0_.refs_2_), channel_id=1, source_target_pairs={{0,16},{8,24},{16,0},{24,8},{1,17},{9,25},{17,1},{25,9},{2,18},{10... | collective-permute-start | bytes 786440 | tf_op jit(solution)/shard_map/ppermute | solution.py:228
  24.4 8.8 %collective-permute-start.11 = (bf16[256,512]{1,0:T(8,128)(2,1)S(1)}, bf16[256,512]{1,0:T(8,128)(2,1)S(1)}, u32[]{:S(2)}, u32[]{:S(2)}) collective-permute-start(bf16[256,512]{1,0:T(8,128)(2,1)S(1)} %copy_after.3), channel_id=1, source_target_pairs={{0,16},{8,24},{16,0},{24,8},{1,17},{9,25},{17,1},{25,9},{2,18},{10... | collective-permute-start | bytes 786440 | tf_op jit(solution)/shard_map/ppermute | solution.py:229
  31.9 6.3 %copy-start = (f32[2,128,512]{2,1,0:T(8,128)S(1)}, f32[2,128,512]{2,1,0:T(8,128)}, u32[]{:S(2)}) copy-start(f32[2,128,512]{2,1,0:T(8,128)} %get-tuple-element.17) | copy-start | bytes 1572868
  31.9 6.3 %collective-permute-start.7 = (bf16[2,128,512]{2,1,0:T(8,128)(2,1)S(1)}, bf16[2,128,512]{2,1,0:T(8,128)(2,1)S(1)}, u32[]{:S(2)}, u32[]{:S(2)}) collective-permute-start(bf16[2,128,512]{2,1,0:T(8,128)(2,1)S(1)} %get-tuple-element.18), channel_id=1, source_target_pairs={{0,2},{1,3},{2,0},{3,1},{4,6},{5,7},{6,4},{7,5},{8,10},{9,11},{10,... | collective-permute-start | bytes 786440 | tf_op jit(solution)/shard_map/ppermute | solution.py:209
  36.2 9.6 %collective-permute-start.12 = (bf16[2,128,512]{2,1,0:T(8,128)(2,1)S(1)}, bf16[2,128,512]{2,1,0:T(8,128)(2,1)S(1)}, u32[]{:S(2)}, u32[]{:S(2)}) collective-permute-start(bf16[2,128,512]{2,1,0:T(8,128)(2,1)S(1)} %get-tuple-element.20), channel_id=1, source_target_pairs={{0,2},{1,3},{2,0},{3,1},{4,6},{5,7},{6,4},{7,5},{8,10},{9,11},{10,... | collective-permute-start | bytes 786440 | tf_op jit(solution)/shard_map/ppermute | solution.py:209
  38.3 9.1 %collective-permute-start.8 = (bf16[1,128,512]{2,1,0:T(8,128)(2,1)S(1)}, bf16[1,128,512]{2,1,0:T(8,128)(2,1)S(1)}, u32[]{:S(2)}, u32[]{:S(2)}) collective-permute-start(bf16[1,128,512]{2,1,0:T(8,128)(2,1)S(1)} %slice.69), channel_id=1, source_target_pairs={{0,4},{1,5},{2,6},{3,7},{4,0},{5,1},{6,2},{7,3},{8,12},{9,13},{10,... | collective-permute-start | bytes 393224 | tf_op jit(solution)/shard_map/ppermute | solution.py:209
  45.8 9.6 %collective-permute-start.13 = (bf16[1,128,512]{2,1,0:T(8,128)(2,1)S(1)}, bf16[1,128,512]{2,1,0:T(8,128)(2,1)S(1)}, u32[]{:S(2)}, u32[]{:S(2)}) collective-permute-start(bf16[1,128,512]{2,1,0:T(8,128)(2,1)S(1)} %slice.68), channel_id=1, source_target_pairs={{0,4},{1,5},{2,6},{3,7},{4,0},{5,1},{6,2},{7,3},{8,12},{9,13},{10,... | collective-permute-start | bytes 393224 | tf_op jit(solution)/shard_map/ppermute | solution.py:209
  47.4 9.4 %collective-permute-start.9 = (bf16[64,512]{1,0:T(8,128)(2,1)S(1)}, bf16[64,512]{1,0:T(8,128)(2,1)S(1)}, u32[]{:S(2)}, u32[]{:S(2)}) collective-permute-start(bf16[64,512]{1,0:T(8,128)(2,1)S(1)} %get-tuple-element.22), channel_id=1, source_target_pairs={{0,1},{1,0},{2,3},{3,2},{4,5},{5,4},{6,7},{7,6},{8,9},{9,8},{10,11... | collective-permute-start | bytes 196616 | tf_op jit(solution)/shard_map/ppermute | solution.py:247
  55.5 2.3 %collective-permute-start.14 = (bf16[64,512]{1,0:T(8,128)(2,1)S(1)}, bf16[64,512]{1,0:T(8,128)(2,1)S(1)}, u32[]{:S(2)}, u32[]{:S(2)}) collective-permute-start(bf16[64,512]{1,0:T(8,128)(2,1)S(1)} %get-tuple-element.24), channel_id=1, source_target_pairs={{0,1},{1,0},{2,3},{3,2},{4,5},{5,4},{6,7},{7,6},{8,9},{9,8},{10,11... | collective-permute-start | bytes 196616 | tf_op jit(solution)/shard_map/ppermute | solution.py:247

commit v4 on v3

--- a/solution.py
+++ b/solution.py
@@ -203,12 +203,21 @@
     )(*scalars, *[in_vmem(x) for x in near], *[in_hbm(x) for x in far])
 
 
-def sum_over_chips(stay, gone, bits, terms):
-    for bit in bits:
+def sum_over_chips(stay, gone, bits, terms, direct):
+    half = stay.shape[1] // 2
+    cores = [(d, d ^ 1) for d in range(terms)]
+    for n, bit in enumerate(bits):
         pairs = [(d, d ^ (2 << bit)) for d in range(terms)]
+        if direct and n == len(bits) - 1:
+            across = [(d, d ^ (2 << bit) ^ 1) for d in range(terms)]
+            swapped = lax.ppermute(stay[0], "term", cores)[half:]
+            mine = stay[0, :half] + lax.ppermute(gone[0, :half], "term", pairs).astype(jnp.float32)
+            others = swapped + lax.ppermute(gone[0, half:], "term", across).astype(jnp.float32)
+            return mine.astype(jnp.bfloat16), others.astype(jnp.bfloat16)
         total = stay + lax.ppermute(gone, "term", pairs).astype(jnp.float32)
         stay, gone = total[::2], total[1::2].astype(jnp.bfloat16)
-    return stay[0]
+    total = stay[0].astype(jnp.bfloat16)
+    return total[:half], lax.ppermute(total[half:], "term", cores)
 
 
 def local(psi, left_ops, right_ops, shift, live):
@@ -233,7 +242,7 @@
         far = [lax.ppermute(part, "sec", nexts) for part in parts]
     planes = [(d, d ^ 2) for d in range(terms)]
     near_first, near_second = (near[0], lax.ppermute(near[0], "term", planes)), near[1:]
-    far_first, far_second = (far[0], lax.ppermute(copy_after(far[0], near[1]), "term", planes)), far[1:]
+    far_first, far_second = (far[0], lax.ppermute(copy_after(far[0], near[1], near_first[1]), "term", planes)), far[1:]
 
     scalars = (place,)
     outs = []
@@ -242,9 +251,7 @@
         swapped = (True, False, True) if step == 0 else (False, True, False)
         bits = list(range((terms // 2).bit_length() - 1))
         blocks = piece(step, secs, terms // 2, bits, scalars, halo, swapped, pack1, psi, left_ops, right_ops)
-        total = sum_over_chips(*blocks, bits, terms).astype(jnp.bfloat16)
-        mine, others = total[: size // terms], total[size // terms :]
-        got = lax.ppermute(others, "term", cores)
+        mine, got = sum_over_chips(*blocks, bits, terms, step == 1)
         outs.append(jnp.where(core == 0, jnp.stack([mine, got]), jnp.stack([got, mine])))
     return jnp.where(odd == 1, jnp.stack(outs), jnp.stack(outs[::-1]))
 

time: 59 us -> 56.9 us (0.964); the launches traced: 58.5 us -> 57.4 us
  waiting for transfers between devices: 26.1 us -> 22.4 us
  starting transfers between devices: 21 us -> 23.6 us
    ppermute x4 -> x3, waiting for transfers between devices: 10.9 us -> 4.14 us  [sum_over_chips(): total = stay + lax.ppermute(gone, 'term', pairs).astype(jnp.float32)]
    ppermute x3 -> x5, waiting for transfers between devices: 3.49 us -> 5.68 us  [the longest x1 4.44 us: sum_over_chips(): lax.ppermute(gone[0, half:], 'term', across).astype(jnp.float32)]
    ppermute x3 -> x5, starting transfers between devices: 5.55 us -> 7.63 us  [the longest x1 4.95 us: sum_over_chips(): swapped = lax.ppermute(stay[0], 'term', cores)[half:]]
    ppermute x1, waiting for transfers between devices: 0.01 us -> 1.74 us  [local(): far.append(lax.ppermute(copy_after(near[2], far[0]), 'sec', turn))]
    ppermute x3, waiting for transfers between devices: 10.4 us -> 8.81 us  [local(): near = [lax.ppermute(part, 'sec', pairs) for part in parts]]
    ppermute x1, starting transfers between devices: 1.38 us -> 2.85 us  [local(): far.append(lax.ppermute(copy_after(near[2], far[0]), 'sec', turn))]
    ppermute x1, waiting for transfers between devices: 0.01 us -> 1.27 us  [local(): lax.ppermute(near[0], 'term', planes)]
    ppermute x4 -> x3, starting transfers between devices: 6.21 us -> 5.46 us  [sum_over_chips(): total = stay + lax.ppermute(gone, 'term', pairs).astype(jnp.float32)]
  transfers between devices with their start and end apart: 15 -> 16, of which waited for: 9 -> 10; matrix products, arithmetic and copies ran while one was open for 0% -> 0% of each run, Pallas kernels for 11% -> 11%
where the time goes in v4:
time: 56.9 us; the launch traced here: 57.4 us
  starting transfers between devices  23.6 us (41%)
  waiting for transfers between devices  22.4 us (39%)
  Pallas kernels  8.85 us (16%)
  between operations  1.44 us (3%)
  other arithmetic  0.98 us (2%)
    ppermute x3, waiting for transfers between devices, local(): near = [lax.ppermute(part, 'sec', pairs) for part in parts]  8.81 us
    pallas_call x2, Pallas kernels, piece(): call(body, 'piece', out_shape=outs, in_specs=[SMEM_SPEC] + [VMEM_SPEC] *...  6.43 us
    ppermute x3, starting transfers between devices, sum_over_chips(): total = stay + lax.ppermute(gone, 'term', pairs).astype(jnp.float32)  5.46 us
    ppermute x1, starting transfers between devices, sum_over_chips(): swapped = lax.ppermute(stay[0], 'term', cores)[half:]  4.95 us
    ppermute x1, waiting for transfers between devices, sum_over_chips(): lax.ppermute(gone[0, half:], 'term', across).astype(jnp.float32)  4.44 us
    ppermute x3, waiting for transfers between devices, sum_over_chips(): total = stay + lax.ppermute(gone, 'term', pairs).astype(jnp.float32)  4.14 us
    ppermute x3, starting transfers between devices, local(): near = [lax.ppermute(part, 'sec', pairs) for part in parts]  3.9 us
    ppermute x1, starting transfers between devices, local(): far.append(lax.ppermute(copy_after(near[2], far[0]), 'sec', turn))  2.85 us
  transfers between devices with their start and end apart: 16, of which 10 were waited for; matrix products, arithmetic and copies ran while one was open for 0% of the time, Pallas kernels for 11%

profile of v4, /device:TPU:1, one launch (start us, length us, event | category | flops | bytes accessed | tf_op | source)
XLA Modules:
  0.0 57.4 jit_solution(6349471308136619476)
XLA Ops:
  1.4 2.4 %cut.1 = (bf16[256,512]{1,0:T(8,128)(2,1)S(1)}, bf16[256,512]{1,0:T(8,128)(2,1)S(1)}, bf16[256,512]{1,0:T(8,128)(2,1)S(1)}, bf16[2064,512]{1,0:T(8,128)(2,1)S(1)}) custom-call(s32[6]{0:T(128)S(1)} %stack.57.place_ref.place, bf16[2,2,512,512]{3,2,1,0:T(8,128)(2,1)} %refs_7_.3, bf16[1,2,512,512]{3,2,1,0:T(8,128)(2,1)} %refs_8_.3, bf16[1,2,512,512]{3,2,1,0:T(8,128)(2,1)} %refs_9_.3), custom_call_target="tpu_custom_call" | custom-call | flops 1000 | bytes 1000 | tf_op jit(solution)/shard_map/cut/pallas_call | solution.py:57
  3.9 2.7 %collective-permute-start = (bf16[256,512]{1,0:T(8,128)(2,1)S(1)}, bf16[256,512]{1,0:T(8,128)(2,1)S(1)}, u32[]{:S(2)}, u32[]{:S(2)}) collective-permute-start(bf16[256,512]{1,0:T(8,128)(2,1)S(1)} %get-tuple-element.13), channel_id=1, source_target_pairs={{0,8},{8,0},{16,24},{24,16},{1,9},{9,1},{17,25},{25,17},{2,10},{10... | collective-permute-start | bytes 786440 | tf_op jit(solution)/shard_map/ppermute | solution.py:233
  6.6 6.6 %collective-permute-done.refs_0_ = bf16[256,512]{1,0:T(8,128)(2,1)S(1)} collective-permute-done((bf16[256,512]{1,0:T(8,128)(2,1)S(1)}, bf16[256,512]{1,0:T(8,128)(2,1)S(1)}, u32[]{:S(2)}, u32[]{:S(2)}) %collective-permute-start) | collective-permute-done | bytes 262176 | tf_op jit(solution)/shard_map/ppermute | solution.py:233
  13.2 1.4 %collective-permute-start.1 = (bf16[256,512]{1,0:T(8,128)(2,1)S(1)}, bf16[256,512]{1,0:T(8,128)(2,1)S(1)}, u32[]{:S(2)}, u32[]{:S(2)}) collective-permute-start(bf16[256,512]{1,0:T(8,128)(2,1)S(1)} %collective-permute-done.refs_0_), channel_id=1, source_target_pairs={{0,2},{1,3},{2,0},{3,1},{4,6},{5,7},{6,4},{7,5},{8,10},{9,11},{10,... | collective-permute-start | bytes 786440 | tf_op jit(solution)/shard_map/ppermute | solution.py:244
  14.5 1.2 %collective-permute-start.4 = (bf16[256,512]{1,0:T(8,128)(2,1)S(1)}, bf16[256,512]{1,0:T(8,128)(2,1)S(1)}, u32[]{:S(2)}, u32[]{:S(2)}) collective-permute-start(bf16[256,512]{1,0:T(8,128)(2,1)S(1)} %collective-permute-done.refs_0_), channel_id=1, source_target_pairs={{0,16},{8,24},{16,0},{24,8},{1,17},{9,25},{17,1},{25,9},{2,18},{10... | collective-permute-start | bytes 786440 | tf_op jit(solution)/shard_map/ppermute | solution.py:237
  15.8 1.2 %collective-permute-start.3 = (bf16[256,512]{1,0:T(8,128)(2,1)S(1)}, bf16[256,512]{1,0:T(8,128)(2,1)S(1)}, u32[]{:S(2)}, u32[]{:S(2)}) collective-permute-start(bf16[256,512]{1,0:T(8,128)(2,1)S(1)} %get-tuple-element.15), channel_id=1, source_target_pairs={{0,8},{8,0},{16,24},{24,16},{1,9},{9,1},{17,25},{25,17},{2,10},{10... | collective-permute-start | bytes 786440 | tf_op jit(solution)/shard_map/ppermute | solution.py:233
  17.0 1.8 %collective-permute-done.2.refs_0_.refs_2_ = bf16[256,512]{1,0:T(8,128)(2,1)S(1)} collective-permute-done((bf16[256,512]{1,0:T(8,128)(2,1)S(1)}, bf16[256,512]{1,0:T(8,128)(2,1)S(1)}, u32[]{:S(2)}, u32[]{:S(2)}) %collective-permute-start.2) | collective-permute-done | bytes 262176 | tf_op jit(solution)/shard_map/ppermute | solution.py:233
  18.8 1.3 %collective-permute-done.1.refs_1_ = bf16[256,512]{1,0:T(8,128)(2,1)S(1)} collective-permute-done((bf16[256,512]{1,0:T(8,128)(2,1)S(1)}, bf16[256,512]{1,0:T(8,128)(2,1)S(1)}, u32[]{:S(2)}, u32[]{:S(2)}) %collective-permute-start.1) | collective-permute-done | bytes 262176 | tf_op jit(solution)/shard_map/ppermute | solution.py:244
  20.0 0.7 %collective-permute-done.4.part_ref.refs_4_.refs_0_.refs_2_ = bf16[256,512]{1,0:T(8,128)(2,1)S(1)} collective-permute-done((bf16[256,512]{1,0:T(8,128)(2,1)S(1)}, bf16[256,512]{1,0:T(8,128)(2,1)S(1)}, u32[]{:S(2)}, u32[]{:S(2)}) %collective-permute-start.4) | collective-permute-done | bytes 262176 | tf_op jit(solution)/shard_map/ppermute | solution.py:237
  20.8 0.5 collective-permute-start.5
  21.3 1.1 %collective-permute-start.10 = (bf16[256,512]{1,0:T(8,128)(2,1)S(1)}, bf16[256,512]{1,0:T(8,128)(2,1)S(1)}, u32[]{:S(2)}, u32[]{:S(2)}) collective-permute-start(bf16[256,512]{1,0:T(8,128)(2,1)S(1)} %collective-permute-done.2.refs_0_.refs_2_), channel_id=1, source_target_pairs={{0,16},{8,24},{16,0},{24,8},{1,17},{9,25},{17,1},{25,9},{2,18},{10... | collective-permute-start | bytes 786440 | tf_op jit(solution)/shard_map/ppermute | solution.py:237
  22.9 2.8 %collective-permute-start.11 = (bf16[256,512]{1,0:T(8,128)(2,1)S(1)}, bf16[256,512]{1,0:T(8,128)(2,1)S(1)}, u32[]{:S(2)}, u32[]{:S(2)}) collective-permute-start(bf16[256,512]{1,0:T(8,128)(2,1)S(1)} %copy_after.3), channel_id=1, source_target_pairs={{0,16},{8,24},{16,0},{24,8},{1,17},{9,25},{17,1},{25,9},{2,18},{10... | collective-permute-start | bytes 786440 | tf_op jit(solution)/shard_map/ppermute | solution.py:238
  26.1 3.5 %piece.2 = (f32[2,128,512]{2,1,0:T(8,128)}, bf16[2,128,512]{2,1,0:T(8,128)(2,1)S(1)}) custom-call(s32[6]{0:T(128)S(1)} %stack.57.place_ref.place, bf16[256,512]{1,0:T(8,128)(2,1)S(1)} %collective-permute-done.refs_0_, bf16[256,512]{1,0:T(8,128)(2,1)S(1)} %collective-permute-done.1.refs_1_, bf16[256,512]{1,0:T(8,128)(2,1)S(1)} %collective-permute-done.2.refs_0_.refs_2_, ...), custom_call_target="tpu_custom_call" | custom-call | flops 1000 | bytes 1000 | tf_op jit(solution)/shard_map/piece/pallas_call | solution.py:189
  29.6 1.3 %collective-permute-start.7 = (bf16[2,128,512]{2,1,0:T(8,128)(2,1)S(1)}, bf16[2,128,512]{2,1,0:T(8,128)(2,1)S(1)}, u32[]{:S(2)}, u32[]{:S(2)}) collective-permute-start(bf16[2,128,512]{2,1,0:T(8,128)(2,1)S(1)} %get-tuple-element.18), channel_id=1, source_target_pairs={{0,2},{1,3},{2,0},{3,1},{4,6},{5,7},{6,4},{7,5},{8,10},{9,11},{10,... | collective-permute-start | bytes 786440 | tf_op jit(solution)/shard_map/ppermute | solution.py:217
  30.8 1.7 %collective-permute-done.11.refs_5_ = bf16[256,512]{1,0:T(8,128)(2,1)S(1)} collective-permute-done((bf16[256,512]{1,0:T(8,128)(2,1)S(1)}, bf16[256,512]{1,0:T(8,128)(2,1)S(1)}, u32[]{:S(2)}, u32[]{:S(2)}) %collective-permute-start.11) | collective-permute-done | bytes 262176 | tf_op jit(solution)/shard_map/ppermute | solution.py:238
  32.6 2.9 %piece.3 = (f32[2,128,512]{2,1,0:T(8,128)S(1)}, bf16[2,128,512]{2,1,0:T(8,128)(2,1)S(1)}) custom-call(s32[6]{0:T(128)S(1)} %stack.57.place_ref.place, bf16[256,512]{1,0:T(8,128)(2,1)S(1)} %collective-permute-done.2.refs_0_.refs_2_, bf16[256,512]{1,0:T(8,128)(2,1)S(1)} %collective-permute-done.3.refs_3_.part_ref.refs_1_, ...), custom_call_target="tpu_custom_call" | custom-call | flops 1000 | bytes 1000 | tf_op jit(solution)/shard_map/piece/pallas_call | solution.py:189
  35.5 2.1 %collective-permute-start.12 = (bf16[2,128,512]{2,1,0:T(8,128)(2,1)S(1)}, bf16[2,128,512]{2,1,0:T(8,128)(2,1)S(1)}, u32[]{:S(2)}, u32[]{:S(2)}) collective-permute-start(bf16[2,128,512]{2,1,0:T(8,128)(2,1)S(1)} %get-tuple-element.20), channel_id=1, source_target_pairs={{0,2},{1,3},{2,0},{3,1},{4,6},{5,7},{6,4},{7,5},{8,10},{9,11},{10,... | collective-permute-start | bytes 786440 | tf_op jit(solution)/shard_map/ppermute | solution.py:217
  37.8 2.1 %collective-permute-start.8 = (bf16[1,128,512]{2,1,0:T(8,128)(2,1)S(1)}, bf16[1,128,512]{2,1,0:T(8,128)(2,1)S(1)}, u32[]{:S(2)}, u32[]{:S(2)}) collective-permute-start(bf16[1,128,512]{2,1,0:T(8,128)(2,1)S(1)} %slice.81), channel_id=1, source_target_pairs={{0,4},{1,5},{2,6},{3,7},{4,0},{5,1},{6,2},{7,3},{8,12},{9,13},{10,... | collective-permute-start | bytes 393224 | tf_op jit(solution)/shard_map/ppermute | solution.py:217
  39.8 4.1 %collective-permute-done.12 = bf16[2,128,512]{2,1,0:T(8,128)(2,1)S(1)} collective-permute-done((bf16[2,128,512]{2,1,0:T(8,128)(2,1)S(1)}, bf16[2,128,512]{2,1,0:T(8,128)(2,1)S(1)}, u32[]{:S(2)}, u32[]{:S(2)}) %collective-permute-start.12) | collective-permute-done | bytes 262176 | tf_op jit(solution)/shard_map/ppermute | solution.py:217
  44.1 1.5 %collective-permute-start.13 = (bf16[64,512]{1,0:T(8,128)(2,1)S(1)}, bf16[64,512]{1,0:T(8,128)(2,1)S(1)}, u32[]{:S(2)}, u32[]{:S(2)}) collective-permute-start(bf16[64,512]{1,0:T(8,128)(2,1)S(1)} %get-tuple-element.23), channel_id=1, source_target_pairs={{0,4},{1,5},{2,6},{3,7},{4,0},{5,1},{6,2},{7,3},{8,12},{9,13},{10,... | collective-permute-start | bytes 196616 | tf_op jit(solution)/shard_map/ppermute | solution.py:214
  45.6 4.9 %collective-permute-start.14 = (f32[128,512]{1,0:T(8,128)S(1)}, f32[128,512]{1,0:T(8,128)S(1)}, u32[]{:S(2)}, u32[]{:S(2)}) collective-permute-start(f32[128,512]{1,0:T(8,128)S(1)} %slice_bitcast_fusion), channel_id=1, source_target_pairs={{0,1},{1,0},{2,3},{3,2},{4,5},{5,4},{6,7},{7,6},{8,9},{9,8},{10,11... | collective-permute-start | bytes 786440 | tf_op jit(solution)/shard_map/ppermute | solution.py:213
  51.3 0.9 %collective-permute-done.9 = bf16[64,512]{1,0:T(8,128)(2,1)S(1)} collective-permute-done((bf16[64,512]{1,0:T(8,128)(2,1)S(1)}, bf16[64,512]{1,0:T(8,128)(2,1)S(1)}, u32[]{:S(2)}, u32[]{:S(2)}) %collective-permute-start.9) | collective-permute-done | bytes 65568 | tf_op jit(solution)/shard_map/ppermute | solution.py:220
  52.2 4.4 %collective-permute-done.15 = bf16[64,512]{1,0:T(8,128)(2,1)S(1)} collective-permute-done((bf16[64,512]{1,0:T(8,128)(2,1)S(1)}, bf16[64,512]{1,0:T(8,128)(2,1)S(1)}, u32[]{:S(2)}, u32[]{:S(2)}) %collective-permute-start.15) | collective-permute-done | bytes 65568 | tf_op jit(solution)/shard_map/ppermute | solution.py:215
  56.7 0.7 %maximum_select_fusion = bf16[2,2,64,512]{3,2,1,0:T(8,128)(2,1)} fusion(bf16[1,2,64,512]{3,2,1,0:T(8,128)(2,1)S(1)} %maximum_select_fusion.2, bf16[1,2,64,512]{3,2,1,0:T(8,128)(2,1)S(1)} %maximum_select_fusion.1, pred[]{:T(512)S(6)} %eq.10), kind=kLoop, calls=%fused_computation.6 | loop fusion | flops 393216 | bytes 524289 | tf_op jit(solution)/shard_map/jit(_where)/select_n | solution.py:256
  (28 shorter events, 2.1 us)
Async XLA Ops:
  3.8 22.3 %collective-permute-start.6 = (bf16[2064,512]{1,0:T(8,128)(2,1)S(1)}, bf16[2064,512]{1,0:T(8,128)(2,1)S(1)}, u32[]{:S(2)}, u32[]{:S(2)}) collective-permute-start(bf16[2064,512]{1,0:T(8,128)(2,1)S(1)} %get-tuple-element.16), channel_id=1, source_target_pairs={{0,1},{1,0},{2,3},{3,2},{4,5},{5,4},{6,7},{7,6},{8,9},{9,8},{10,11... | collective-permute-start | bytes 6340616 | tf_op jit(solution)/shard_map/ppermute | solution.py:234
  3.9 9.3 %collective-permute-start = (bf16[256,512]{1,0:T(8,128)(2,1)S(1)}, bf16[256,512]{1,0:T(8,128)(2,1)S(1)}, u32[]{:S(2)}, u32[]{:S(2)}) collective-permute-start(bf16[256,512]{1,0:T(8,128)(2,1)S(1)} %get-tuple-element.13), channel_id=1, source_target_pairs={{0,8},{8,0},{16,24},{24,16},{1,9},{9,1},{17,25},{25,17},{2,10},{10... | collective-permute-start | bytes 786440 | tf_op jit(solution)/shard_map/ppermute | solution.py:233
  6.6 12.2 %collective-permute-start.2 = (bf16[256,512]{1,0:T(8,128)(2,1)S(1)}, bf16[256,512]{1,0:T(8,128)(2,1)S(1)}, u32[]{:S(2)}, u32[]{:S(2)}) collective-permute-start(bf16[256,512]{1,0:T(8,128)(2,1)S(1)} %get-tuple-element.14), channel_id=1, source_target_pairs={{0,8},{8,0},{16,24},{24,16},{1,9},{9,1},{17,25},{25,17},{2,10},{10... | collective-permute-start | bytes 786440 | tf_op jit(solution)/shard_map/ppermute | solution.py:233
  13.2 6.9 %collective-permute-start.1 = (bf16[256,512]{1,0:T(8,128)(2,1)S(1)}, bf16[256,512]{1,0:T(8,128)(2,1)S(1)}, u32[]{:S(2)}, u32[]{:S(2)}) collective-permute-start(bf16[256,512]{1,0:T(8,128)(2,1)S(1)} %collective-permute-done.refs_0_), channel_id=1, source_target_pairs={{0,2},{1,3},{2,0},{3,1},{4,6},{5,7},{6,4},{7,5},{8,10},{9,11},{10,... | collective-permute-start | bytes 786440 | tf_op jit(solution)/shard_map/ppermute | solution.py:244
  14.5 6.2 %collective-permute-start.4 = (bf16[256,512]{1,0:T(8,128)(2,1)S(1)}, bf16[256,512]{1,0:T(8,128)(2,1)S(1)}, u32[]{:S(2)}, u32[]{:S(2)}) collective-permute-start(bf16[256,512]{1,0:T(8,128)(2,1)S(1)} %collective-permute-done.refs_0_), channel_id=1, source_target_pairs={{0,16},{8,24},{16,0},{24,8},{1,17},{9,25},{17,1},{25,9},{2,18},{10... | collective-permute-start | bytes 786440 | tf_op jit(solution)/shard_map/ppermute | solution.py:237
  15.8 7.1 %collective-permute-start.3 = (bf16[256,512]{1,0:T(8,128)(2,1)S(1)}, bf16[256,512]{1,0:T(8,128)(2,1)S(1)}, u32[]{:S(2)}, u32[]{:S(2)}) collective-permute-start(bf16[256,512]{1,0:T(8,128)(2,1)S(1)} %get-tuple-element.15), channel_id=1, source_target_pairs={{0,8},{8,0},{16,24},{24,16},{1,9},{9,1},{17,25},{25,17},{2,10},{10... | collective-permute-start | bytes 786440 | tf_op jit(solution)/shard_map/ppermute | solution.py:233
  20.8 5.3 %collective-permute-start.5 = (bf16[256,512]{1,0:T(8,128)(2,1)S(1)}, bf16[256,512]{1,0:T(8,128)(2,1)S(1)}, u32[]{:S(2)}, u32[]{:S(2)}) collective-permute-start(bf16[256,512]{1,0:T(8,128)(2,1)S(1)} %copy_after.2), channel_id=1, source_target_pairs={{0,2},{1,3},{2,0},{3,1},{4,6},{5,7},{6,4},{7,5},{8,10},{9,11},{10,... | collective-permute-start | bytes 786440 | tf_op jit(solution)/shard_map/ppermute | solution.py:245
  21.3 9.5 %collective-permute-start.10 = (bf16[256,512]{1,0:T(8,128)(2,1)S(1)}, bf16[256,512]{1,0:T(8,128)(2,1)S(1)}, u32[]{:S(2)}, u32[]{:S(2)}) collective-permute-start(bf16[256,512]{1,0:T(8,128)(2,1)S(1)} %collective-permute-done.2.refs_0_.refs_2_), channel_id=1, source_target_pairs={{0,16},{8,24},{16,0},{24,8},{1,17},{9,25},{17,1},{25,9},{2,18},{10... | collective-permute-start | bytes 786440 | tf_op jit(solution)/shard_map/ppermute | solution.py:237
  22.9 9.7 %collective-permute-start.11 = (bf16[256,512]{1,0:T(8,128)(2,1)S(1)}, bf16[256,512]{1,0:T(8,128)(2,1)S(1)}, u32[]{:S(2)}, u32[]{:S(2)}) collective-permute-start(bf16[256,512]{1,0:T(8,128)(2,1)S(1)} %copy_after.3), channel_id=1, source_target_pairs={{0,16},{8,24},{16,0},{24,8},{1,17},{9,25},{17,1},{25,9},{2,18},{10... | collective-permute-start | bytes 786440 | tf_op jit(solution)/shard_map/ppermute | solution.py:238
  29.6 8.1 %copy-start = (f32[2,128,512]{2,1,0:T(8,128)S(1)}, f32[2,128,512]{2,1,0:T(8,128)}, u32[]{:S(2)}) copy-start(f32[2,128,512]{2,1,0:T(8,128)} %get-tuple-element.17) | copy-start | bytes 1572868
  29.6 8.1 %collective-permute-start.7 = (bf16[2,128,512]{2,1,0:T(8,128)(2,1)S(1)}, bf16[2,128,512]{2,1,0:T(8,128)(2,1)S(1)}, u32[]{:S(2)}, u32[]{:S(2)}) collective-permute-start(bf16[2,128,512]{2,1,0:T(8,128)(2,1)S(1)} %get-tuple-element.18), channel_id=1, source_target_pairs={{0,2},{1,3},{2,0},{3,1},{4,6},{5,7},{6,4},{7,5},{8,10},{9,11},{10,... | collective-permute-start | bytes 786440 | tf_op jit(solution)/shard_map/ppermute | solution.py:217
  35.5 8.4 %collective-permute-start.12 = (bf16[2,128,512]{2,1,0:T(8,128)(2,1)S(1)}, bf16[2,128,512]{2,1,0:T(8,128)(2,1)S(1)}, u32[]{:S(2)}, u32[]{:S(2)}) collective-permute-start(bf16[2,128,512]{2,1,0:T(8,128)(2,1)S(1)} %get-tuple-element.20), channel_id=1, source_target_pairs={{0,2},{1,3},{2,0},{3,1},{4,6},{5,7},{6,4},{7,5},{8,10},{9,11},{10,... | collective-permute-start | bytes 786440 | tf_op jit(solution)/shard_map/ppermute | solution.py:217
  37.8 12.9 %collective-permute-start.8 = (bf16[1,128,512]{2,1,0:T(8,128)(2,1)S(1)}, bf16[1,128,512]{2,1,0:T(8,128)(2,1)S(1)}, u32[]{:S(2)}, u32[]{:S(2)}) collective-permute-start(bf16[1,128,512]{2,1,0:T(8,128)(2,1)S(1)} %slice.81), channel_id=1, source_target_pairs={{0,4},{1,5},{2,6},{3,7},{4,0},{5,1},{6,2},{7,3},{8,12},{9,13},{10,... | collective-permute-start | bytes 393224 | tf_op jit(solution)/shard_map/ppermute | solution.py:217
  44.1 7.2 %collective-permute-start.13 = (bf16[64,512]{1,0:T(8,128)(2,1)S(1)}, bf16[64,512]{1,0:T(8,128)(2,1)S(1)}, u32[]{:S(2)}, u32[]{:S(2)}) collective-permute-start(bf16[64,512]{1,0:T(8,128)(2,1)S(1)} %get-tuple-element.23), channel_id=1, source_target_pairs={{0,4},{1,5},{2,6},{3,7},{4,0},{5,1},{6,2},{7,3},{8,12},{9,13},{10,... | collective-permute-start | bytes 196616 | tf_op jit(solution)/shard_map/ppermute | solution.py:214
  45.6 11.0 %collective-permute-start.14 = (f32[128,512]{1,0:T(8,128)S(1)}, f32[128,512]{1,0:T(8,128)S(1)}, u32[]{:S(2)}, u32[]{:S(2)}) collective-permute-start(f32[128,512]{1,0:T(8,128)S(1)} %slice_bitcast_fusion), channel_id=1, source_target_pairs={{0,1},{1,0},{2,3},{3,2},{4,5},{5,4},{6,7},{7,6},{8,9},{9,8},{10,11... | collective-permute-start | bytes 786440 | tf_op jit(solution)/shard_map/ppermute | solution.py:213
  50.5 6.1 %collective-permute-start.15 = (bf16[64,512]{1,0:T(8,128)(2,1)S(1)}, bf16[64,512]{1,0:T(8,128)(2,1)S(1)}, u32[]{:S(2)}, u32[]{:S(2)}) collective-permute-start(bf16[64,512]{1,0:T(8,128)(2,1)S(1)} %get-tuple-element.24), channel_id=1, source_target_pairs={{0,5},{1,4},{2,7},{3,6},{4,1},{5,0},{6,3},{7,2},{8,13},{9,12},{10,... | collective-permute-start | bytes 196616 | tf_op jit(solution)/shard_map/ppermute | solution.py:215
  50.8 1.4 %collective-permute-start.9 = (bf16[64,512]{1,0:T(8,128)(2,1)S(1)}, bf16[64,512]{1,0:T(8,128)(2,1)S(1)}, u32[]{:S(2)}, u32[]{:S(2)}) collective-permute-start(bf16[64,512]{1,0:T(8,128)(2,1)S(1)} %get-tuple-element.26), channel_id=1, source_target_pairs={{0,1},{1,0},{2,3},{3,2},{4,5},{5,4},{6,7},{7,6},{8,9},{9,8},{10,11... | collective-permute-start | bytes 196616 | tf_op jit(solution)/shard_map/ppermute | solution.py:220

commit v5 on v4

--- a/solution.py
+++ b/solution.py
@@ -82,7 +82,7 @@
     )(in_vmem(part), *after)
 
 
-def piece(step, secs, chips, bits, scalars, halo, swapped, pack1, psi, left0, right0):
+def piece(step, secs, chips, bits, scalars, halo, swapped, pack1, pack0, psi):
     def relative(q):
         return sum((q >> k & 1) << bit for k, bit in enumerate(bits))
 
@@ -90,12 +90,12 @@
     parked = step == 0
     slots, height, count = len(halo), size // chips, chips // 2
     rows = size // 2
-    near = [part for block in halo for part in block] + [pack1]
-    far = [psi, left0, right0]
+    near = [part for block in halo for part in block] + [pack1, pack0]
+    far = [psi]
 
     def body(place, *refs):
-        halves, pack, refs = refs[: 2 * slots], refs[2 * slots], refs[2 * slots + 1 :]
-        psi_ref, left_ref, right_ref, stay, gone, own, left, right, inner, kept, sem = refs
+        halves, pack, own_pack, refs = refs[: 2 * slots], refs[2 * slots], refs[2 * slots + 1], refs[2 * slots + 2 :]
+        psi_ref, stay, gone, own, inner, kept, sem = refs
         core, odd, i, z = place[0], place[1], place[2], place[3]
         sector = step * odd + (1 - step) * (1 - odd)
         flags = pack[pl.ds(4 * size, 16), pl.ds(0, 128)].astype(jnp.float32)
@@ -119,23 +119,15 @@
             @pl.when(slot_of[term] >= slots)
             def _(term=term):
                 own_copy(term, slot_of[term] - slots).start()
-        left_copy = pltpu.make_async_copy(left_ref.at[0, sector], left, sem.at[2])
-        right_copy = pltpu.make_async_copy(right_ref.at[0, sector], right, sem.at[3])
-        left_copy.start()
-        right_copy.start()
-
         order = [relative(q) for q in [*range(1, chips, 2), *range(0, chips, 2)]]
         for term in (1, 0):
-            if term == 0:
-                left_copy.wait()
-
             def left_rows(group, column, term=term):
                 def at(r, k):
                     start = (z ^ r) * height + (core ^ k) * (height // 2)
-                    start = start if term == 0 else start + sector * size
+                    start = start + sector * size
                     block = pl.ds(pl.multiple_of(start, height // 2), height // 2)
                     columns = pl.ds(pl.multiple_of(column * rows, 128), rows)
-                    return left[block, columns] if term == 0 else pack[block, columns]
+                    return (own_pack, pack)[term][block, columns]
 
                 return jnp.concatenate([at(r, k) for r in order[group * count : (group + 1) * count] for k in range(2)])
 
@@ -159,13 +151,12 @@
                 own_copy(term, 0).wait()
                 first_product([lambda n=n: own[term, pl.ds(n * rows, rows)] for n in range(2)], [0, 1])
 
-        right_copy.wait()
         stay_copy = pltpu.make_async_copy(kept, stay, sem.at[4]) if parked else None
         for group in (1, 0):
             total = sum(
                 lax.dot_general(
                     inner[term, pl.ds(group * rows, rows)],
-                    right[...] if term == 0 else pack[pl.ds(pl.multiple_of((2 + sector) * size, size), size)],
+                    (own_pack, pack)[term][pl.ds(pl.multiple_of((2 + sector) * size, size), size)],
                     (((1,), (1,)), ((), ())),
                     preferred_element_type=jnp.float32,
                 )
@@ -194,8 +185,6 @@
         out_specs=[ANY_SPEC if parked else VMEM_SPEC] + [VMEM_SPEC] * (len(outs) - 1),
         scratch_shapes=[
             pltpu.VMEM((2, size, size), jnp.bfloat16),
-            pltpu.VMEM((size, size), jnp.bfloat16),
-            pltpu.VMEM((size, size), jnp.bfloat16),
             pltpu.VMEM((2, size, size), jnp.bfloat16),
             pltpu.VMEM((count, height, size), jnp.float32),
             pltpu.SemaphoreType.DMA((5,)),
@@ -250,7 +239,7 @@
         halo = (near_first, near_second, far_first) if step == 0 else (near_second, far_first, far_second)
         swapped = (True, False, True) if step == 0 else (False, True, False)
         bits = list(range((terms // 2).bit_length() - 1))
-        blocks = piece(step, secs, terms // 2, bits, scalars, halo, swapped, pack1, psi, left_ops, right_ops)
+        blocks = piece(step, secs, terms // 2, bits, scalars, halo, swapped, pack1, pack0, psi)
         mine, got = sum_over_chips(*blocks, bits, terms, step == 1)
         outs.append(jnp.where(core == 0, jnp.stack([mine, got]), jnp.stack([got, mine])))
     return jnp.where(odd == 1, jnp.stack(outs), jnp.stack(outs[::-1]))

time: 56.9 us -> 56.7 us (level)
  starting transfers between devices: 23.6 us -> 26.7 us
  waiting for transfers between devices: 22.4 us -> 20.3 us
  Pallas kernels: 8.85 us -> 7.75 us
    ppermute x3, starting transfers between devices: 5.46 us -> 7.2 us  [sum_over_chips(): total = stay + lax.ppermute(gone, 'term', pairs).astype(jnp.float32)]
    ppermute x1, starting transfers between devices: 0.16 us -> 1.46 us  [sum_over_chips(): lax.ppermute(gone[0, half:], 'term', across).astype(jnp.float32)]
    pallas_call x2, Pallas kernels: 6.43 us -> 5.33 us  [piece(): call(body, 'piece', out_shape=outs, in_specs=[SMEM_SPEC] + [VMEM_SPEC] *...]
    ppermute x3, waiting for transfers between devices: 4.14 us -> 3.09 us  [sum_over_chips(): total = stay + lax.ppermute(gone, 'term', pairs).astype(jnp.float32)]
    ppermute x1, starting transfers between devices: 1.48 us -> 2.33 us  [sum_over_chips(): lax.ppermute(gone[0, :half], 'term', pairs).astype(jnp.float32)]
    ppermute x1, starting transfers between devices: 4.95 us -> 4.15 us  [sum_over_chips(): swapped = lax.ppermute(stay[0], 'term', cores)[half:]]
    ppermute x1, waiting for transfers between devices: 4.44 us -> 3.8 us  [sum_over_chips(): lax.ppermute(gone[0, half:], 'term', across).astype(jnp.float32)]
  transfers between devices with their start and end apart: 16 -> 16, of which waited for: 10 -> 10; matrix products, arithmetic and copies ran while one was open for 0% -> 0% of each run, Pallas kernels for 11% -> 9%
where the time goes in v5:
time: 56.7 us; the launch traced here: 57.4 us
  starting transfers between devices  26.7 us (47%)
  waiting for transfers between devices  20.3 us (36%)
  Pallas kernels  7.75 us (14%)
  between operations  1.44 us (3%)
  other arithmetic  0.98 us (2%)
    ppermute x3, waiting for transfers between devices, local(): near = [lax.ppermute(part, 'sec', pairs) for part in parts]  8.81 us
    ppermute x3, starting transfers between devices, sum_over_chips(): total = stay + lax.ppermute(gone, 'term', pairs).astype(jnp.float32)  7.2 us
    pallas_call x2, Pallas kernels, piece(): call(body, 'piece', out_shape=outs, in_specs=[SMEM_SPEC] + [VMEM_SPEC] *...  5.33 us
    ppermute x1, starting transfers between devices, sum_over_chips(): swapped = lax.ppermute(stay[0], 'term', cores)[half:]  4.15 us
    ppermute x3, starting transfers between devices, local(): near = [lax.ppermute(part, 'sec', pairs) for part in parts]  3.9 us
    ppermute x1, waiting for transfers between devices, sum_over_chips(): lax.ppermute(gone[0, half:], 'term', across).astype(jnp.float32)  3.8 us
    ppermute x3, waiting for transfers between devices, sum_over_chips(): total = stay + lax.ppermute(gone, 'term', pairs).astype(jnp.float32)  3.09 us
    ppermute x1, starting transfers between devices, local(): far.append(lax.ppermute(copy_after(near[2], far[0]), 'sec', turn))  2.85 us
  transfers between devices with their start and end apart: 16, of which 10 were waited for; matrix products, arithmetic and copies ran while one was open for 0% of the time, Pallas kernels for 9%

profile of v5, /device:TPU:1, one launch (start us, length us, event | category | flops | bytes accessed | tf_op | source)
XLA Modules:
  0.0 57.4 jit_solution(13712046453016822591)
XLA Ops:
  1.4 2.4 %cut.1 = (bf16[256,512]{1,0:T(8,128)(2,1)S(1)}, bf16[256,512]{1,0:T(8,128)(2,1)S(1)}, bf16[256,512]{1,0:T(8,128)(2,1)S(1)}, bf16[2064,512]{1,0:T(8,128)(2,1)S(1)}) custom-call(s32[6]{0:T(128)S(1)} %stack.57.place_ref.place, bf16[2,2,512,512]{3,2,1,0:T(8,128)(2,1)} %refs_8_.3, bf16[1,2,512,512]{3,2,1,0:T(8,128)(2,1)} %left_ref.1, ...), custom_call_target="tpu_custom_call" | custom-call | flops 1000 | bytes 1000 | tf_op jit(solution)/shard_map/cut/pallas_call | solution.py:57
  3.9 2.7 %collective-permute-start = (bf16[256,512]{1,0:T(8,128)(2,1)S(1)}, bf16[256,512]{1,0:T(8,128)(2,1)S(1)}, u32[]{:S(2)}, u32[]{:S(2)}) collective-permute-start(bf16[256,512]{1,0:T(8,128)(2,1)S(1)} %get-tuple-element.13), channel_id=1, source_target_pairs={{0,8},{8,0},{16,24},{24,16},{1,9},{9,1},{17,25},{25,17},{2,10},{10... | collective-permute-start | bytes 786440 | tf_op jit(solution)/shard_map/ppermute | solution.py:222
  6.6 6.6 %collective-permute-done.refs_0_ = bf16[256,512]{1,0:T(8,128)(2,1)S(1)} collective-permute-done((bf16[256,512]{1,0:T(8,128)(2,1)S(1)}, bf16[256,512]{1,0:T(8,128)(2,1)S(1)}, u32[]{:S(2)}, u32[]{:S(2)}) %collective-permute-start) | collective-permute-done | bytes 262176 | tf_op jit(solution)/shard_map/ppermute | solution.py:222
  13.2 1.4 %collective-permute-start.1 = (bf16[256,512]{1,0:T(8,128)(2,1)S(1)}, bf16[256,512]{1,0:T(8,128)(2,1)S(1)}, u32[]{:S(2)}, u32[]{:S(2)}) collective-permute-start(bf16[256,512]{1,0:T(8,128)(2,1)S(1)} %collective-permute-done.refs_0_), channel_id=1, source_target_pairs={{0,2},{1,3},{2,0},{3,1},{4,6},{5,7},{6,4},{7,5},{8,10},{9,11},{10,... | collective-permute-start | bytes 786440 | tf_op jit(solution)/shard_map/ppermute | solution.py:233
  14.5 1.2 %collective-permute-start.4 = (bf16[256,512]{1,0:T(8,128)(2,1)S(1)}, bf16[256,512]{1,0:T(8,128)(2,1)S(1)}, u32[]{:S(2)}, u32[]{:S(2)}) collective-permute-start(bf16[256,512]{1,0:T(8,128)(2,1)S(1)} %collective-permute-done.refs_0_), channel_id=1, source_target_pairs={{0,16},{8,24},{16,0},{24,8},{1,17},{9,25},{17,1},{25,9},{2,18},{10... | collective-permute-start | bytes 786440 | tf_op jit(solution)/shard_map/ppermute | solution.py:226
  15.8 1.2 %collective-permute-start.3 = (bf16[256,512]{1,0:T(8,128)(2,1)S(1)}, bf16[256,512]{1,0:T(8,128)(2,1)S(1)}, u32[]{:S(2)}, u32[]{:S(2)}) collective-permute-start(bf16[256,512]{1,0:T(8,128)(2,1)S(1)} %get-tuple-element.15), channel_id=1, source_target_pairs={{0,8},{8,0},{16,24},{24,16},{1,9},{9,1},{17,25},{25,17},{2,10},{10... | collective-permute-start | bytes 786440 | tf_op jit(solution)/shard_map/ppermute | solution.py:222
  17.0 1.8 %collective-permute-done.2.refs_0_.refs_2_ = bf16[256,512]{1,0:T(8,128)(2,1)S(1)} collective-permute-done((bf16[256,512]{1,0:T(8,128)(2,1)S(1)}, bf16[256,512]{1,0:T(8,128)(2,1)S(1)}, u32[]{:S(2)}, u32[]{:S(2)}) %collective-permute-start.2) | collective-permute-done | bytes 262176 | tf_op jit(solution)/shard_map/ppermute | solution.py:222
  18.8 1.3 %collective-permute-done.1.refs_1_ = bf16[256,512]{1,0:T(8,128)(2,1)S(1)} collective-permute-done((bf16[256,512]{1,0:T(8,128)(2,1)S(1)}, bf16[256,512]{1,0:T(8,128)(2,1)S(1)}, u32[]{:S(2)}, u32[]{:S(2)}) %collective-permute-start.1) | collective-permute-done | bytes 262176 | tf_op jit(solution)/shard_map/ppermute | solution.py:233
  20.0 0.7 %collective-permute-done.4.part_ref.refs_4_.refs_0_.refs_2_ = bf16[256,512]{1,0:T(8,128)(2,1)S(1)} collective-permute-done((bf16[256,512]{1,0:T(8,128)(2,1)S(1)}, bf16[256,512]{1,0:T(8,128)(2,1)S(1)}, u32[]{:S(2)}, u32[]{:S(2)}) %collective-permute-start.4) | collective-permute-done | bytes 262176 | tf_op jit(solution)/shard_map/ppermute | solution.py:226
  21.3 1.1 %collective-permute-start.10 = (bf16[256,512]{1,0:T(8,128)(2,1)S(1)}, bf16[256,512]{1,0:T(8,128)(2,1)S(1)}, u32[]{:S(2)}, u32[]{:S(2)}) collective-permute-start(bf16[256,512]{1,0:T(8,128)(2,1)S(1)} %collective-permute-done.2.refs_0_.refs_2_), channel_id=1, source_target_pairs={{0,16},{8,24},{16,0},{24,8},{1,17},{9,25},{17,1},{25,9},{2,18},{10... | collective-permute-start | bytes 786440 | tf_op jit(solution)/shard_map/ppermute | solution.py:226
  22.9 2.8 %collective-permute-start.11 = (bf16[256,512]{1,0:T(8,128)(2,1)S(1)}, bf16[256,512]{1,0:T(8,128)(2,1)S(1)}, u32[]{:S(2)}, u32[]{:S(2)}) collective-permute-start(bf16[256,512]{1,0:T(8,128)(2,1)S(1)} %copy_after.3), channel_id=1, source_target_pairs={{0,16},{8,24},{16,0},{24,8},{1,17},{9,25},{17,1},{25,9},{2,18},{10... | collective-permute-start | bytes 786440 | tf_op jit(solution)/shard_map/ppermute | solution.py:227
  26.1 2.9 %piece.2 = (f32[2,128,512]{2,1,0:T(8,128)}, bf16[2,128,512]{2,1,0:T(8,128)(2,1)S(1)}) custom-call(s32[6]{0:T(128)S(1)} %stack.57.place_ref.place, bf16[256,512]{1,0:T(8,128)(2,1)S(1)} %collective-permute-done.refs_0_, bf16[256,512]{1,0:T(8,128)(2,1)S(1)} %collective-permute-done.1.refs_1_, bf16[256,512]{1,0:T(8,128)(2,1)S(1)} %collective-permute-done.2.refs_0_.refs_2_, ...), custom_call_target="tpu_custom_call" | custom-call | flops 1000 | bytes 1000 | tf_op jit(solution)/shard_map/piece/pallas_call | solution.py:180
  29.0 2.1 %collective-permute-start.7 = (bf16[2,128,512]{2,1,0:T(8,128)(2,1)S(1)}, bf16[2,128,512]{2,1,0:T(8,128)(2,1)S(1)}, u32[]{:S(2)}, u32[]{:S(2)}) collective-permute-start(bf16[2,128,512]{2,1,0:T(8,128)(2,1)S(1)} %get-tuple-element.18), channel_id=1, source_target_pairs={{0,2},{1,3},{2,0},{3,1},{4,6},{5,7},{6,4},{7,5},{8,10},{9,11},{10,... | collective-permute-start | bytes 786440 | tf_op jit(solution)/shard_map/ppermute | solution.py:206
  31.2 1.4 %collective-permute-done.11.refs_5_ = bf16[256,512]{1,0:T(8,128)(2,1)S(1)} collective-permute-done((bf16[256,512]{1,0:T(8,128)(2,1)S(1)}, bf16[256,512]{1,0:T(8,128)(2,1)S(1)}, u32[]{:S(2)}, u32[]{:S(2)}) %collective-permute-start.11) | collective-permute-done | bytes 262176 | tf_op jit(solution)/shard_map/ppermute | solution.py:227
  32.6 2.4 %piece.3 = (f32[2,128,512]{2,1,0:T(8,128)S(1)}, bf16[2,128,512]{2,1,0:T(8,128)(2,1)S(1)}) custom-call(s32[6]{0:T(128)S(1)} %stack.57.place_ref.place, bf16[256,512]{1,0:T(8,128)(2,1)S(1)} %collective-permute-done.2.refs_0_.refs_2_, bf16[256,512]{1,0:T(8,128)(2,1)S(1)} %collective-permute-done.3.refs_3_.part_ref.refs_1_, ...), custom_call_target="tpu_custom_call" | custom-call | flops 1000 | bytes 1000 | tf_op jit(solution)/shard_map/piece/pallas_call | solution.py:180
  35.0 2.7 %collective-permute-start.12 = (bf16[2,128,512]{2,1,0:T(8,128)(2,1)S(1)}, bf16[2,128,512]{2,1,0:T(8,128)(2,1)S(1)}, u32[]{:S(2)}, u32[]{:S(2)}) collective-permute-start(bf16[2,128,512]{2,1,0:T(8,128)(2,1)S(1)} %get-tuple-element.20), channel_id=1, source_target_pairs={{0,2},{1,3},{2,0},{3,1},{4,6},{5,7},{6,4},{7,5},{8,10},{9,11},{10,... | collective-permute-start | bytes 786440 | tf_op jit(solution)/shard_map/ppermute | solution.py:206
  37.8 2.4 %collective-permute-start.8 = (bf16[1,128,512]{2,1,0:T(8,128)(2,1)S(1)}, bf16[1,128,512]{2,1,0:T(8,128)(2,1)S(1)}, u32[]{:S(2)}, u32[]{:S(2)}) collective-permute-start(bf16[1,128,512]{2,1,0:T(8,128)(2,1)S(1)} %slice.81), channel_id=1, source_target_pairs={{0,4},{1,5},{2,6},{3,7},{4,0},{5,1},{6,2},{7,3},{8,12},{9,13},{10,... | collective-permute-start | bytes 393224 | tf_op jit(solution)/shard_map/ppermute | solution.py:206
  40.2 3.1 %collective-permute-done.12 = bf16[2,128,512]{2,1,0:T(8,128)(2,1)S(1)} collective-permute-done((bf16[2,128,512]{2,1,0:T(8,128)(2,1)S(1)}, bf16[2,128,512]{2,1,0:T(8,128)(2,1)S(1)}, u32[]{:S(2)}, u32[]{:S(2)}) %collective-permute-start.12) | collective-permute-done | bytes 262176 | tf_op jit(solution)/shard_map/ppermute | solution.py:206
  43.4 2.3 %collective-permute-start.13 = (bf16[64,512]{1,0:T(8,128)(2,1)S(1)}, bf16[64,512]{1,0:T(8,128)(2,1)S(1)}, u32[]{:S(2)}, u32[]{:S(2)}) collective-permute-start(bf16[64,512]{1,0:T(8,128)(2,1)S(1)} %get-tuple-element.23), channel_id=1, source_target_pairs={{0,4},{1,5},{2,6},{3,7},{4,0},{5,1},{6,2},{7,3},{8,12},{9,13},{10,... | collective-permute-start | bytes 196616 | tf_op jit(solution)/shard_map/ppermute | solution.py:203
  45.7 4.1 %collective-permute-start.14 = (f32[128,512]{1,0:T(8,128)S(1)}, f32[128,512]{1,0:T(8,128)S(1)}, u32[]{:S(2)}, u32[]{:S(2)}) collective-permute-start(f32[128,512]{1,0:T(8,128)S(1)} %slice_bitcast_fusion), channel_id=1, source_target_pairs={{0,1},{1,0},{2,3},{3,2},{4,5},{5,4},{6,7},{7,6},{8,9},{9,8},{10,11... | collective-permute-start | bytes 786440 | tf_op jit(solution)/shard_map/ppermute | solution.py:202
  49.9 1.5 %collective-permute-start.15 = (bf16[64,512]{1,0:T(8,128)(2,1)S(1)}, bf16[64,512]{1,0:T(8,128)(2,1)S(1)}, u32[]{:S(2)}, u32[]{:S(2)}) collective-permute-start(bf16[64,512]{1,0:T(8,128)(2,1)S(1)} %get-tuple-element.24), channel_id=1, source_target_pairs={{0,5},{1,4},{2,7},{3,6},{4,1},{5,0},{6,3},{7,2},{8,13},{9,12},{10,... | collective-permute-start | bytes 196616 | tf_op jit(solution)/shard_map/ppermute | solution.py:204
  51.9 0.9 %collective-permute-done.9 = bf16[64,512]{1,0:T(8,128)(2,1)S(1)} collective-permute-done((bf16[64,512]{1,0:T(8,128)(2,1)S(1)}, bf16[64,512]{1,0:T(8,128)(2,1)S(1)}, u32[]{:S(2)}, u32[]{:S(2)}) %collective-permute-start.9) | collective-permute-done | bytes 65568 | tf_op jit(solution)/shard_map/ppermute | solution.py:209
  52.8 3.8 %collective-permute-done.15 = bf16[64,512]{1,0:T(8,128)(2,1)S(1)} collective-permute-done((bf16[64,512]{1,0:T(8,128)(2,1)S(1)}, bf16[64,512]{1,0:T(8,128)(2,1)S(1)}, u32[]{:S(2)}, u32[]{:S(2)}) %collective-permute-start.15) | collective-permute-done | bytes 65568 | tf_op jit(solution)/shard_map/ppermute | solution.py:204
  56.7 0.7 %maximum_select_fusion = bf16[2,2,64,512]{3,2,1,0:T(8,128)(2,1)} fusion(bf16[1,2,64,512]{3,2,1,0:T(8,128)(2,1)S(1)} %maximum_select_fusion.2, bf16[1,2,64,512]{3,2,1,0:T(8,128)(2,1)S(1)} %maximum_select_fusion.1, pred[]{:T(512)S(6)} %eq.10), kind=kLoop, calls=%fused_computation.6 | loop fusion | flops 393216 | bytes 524289 | tf_op jit(solution)/shard_map/jit(_where)/select_n | solution.py:245
  (28 shorter events, 2.5 us)
Async XLA Ops:
  3.8 22.3 %collective-permute-start.6 = (bf16[2064,512]{1,0:T(8,128)(2,1)S(1)}, bf16[2064,512]{1,0:T(8,128)(2,1)S(1)}, u32[]{:S(2)}, u32[]{:S(2)}) collective-permute-start(bf16[2064,512]{1,0:T(8,128)(2,1)S(1)} %get-tuple-element.16.refs_7_), channel_id=1, source_target_pairs={{0,1},{1,0},{2,3},{3,2},{4,5},{5,4},{6,7},{7,6},{8,9},{9,8},{10,11... | collective-permute-start | bytes 6340616 | tf_op jit(solution)/shard_map/ppermute | solution.py:223
  3.9 9.3 %collective-permute-start = (bf16[256,512]{1,0:T(8,128)(2,1)S(1)}, bf16[256,512]{1,0:T(8,128)(2,1)S(1)}, u32[]{:S(2)}, u32[]{:S(2)}) collective-permute-start(bf16[256,512]{1,0:T(8,128)(2,1)S(1)} %get-tuple-element.13), channel_id=1, source_target_pairs={{0,8},{8,0},{16,24},{24,16},{1,9},{9,1},{17,25},{25,17},{2,10},{10... | collective-permute-start | bytes 786440 | tf_op jit(solution)/shard_map/ppermute | solution.py:222
  6.6 12.2 %collective-permute-start.2 = (bf16[256,512]{1,0:T(8,128)(2,1)S(1)}, bf16[256,512]{1,0:T(8,128)(2,1)S(1)}, u32[]{:S(2)}, u32[]{:S(2)}) collective-permute-start(bf16[256,512]{1,0:T(8,128)(2,1)S(1)} %get-tuple-element.14), channel_id=1, source_target_pairs={{0,8},{8,0},{16,24},{24,16},{1,9},{9,1},{17,25},{25,17},{2,10},{10... | collective-permute-start | bytes 786440 | tf_op jit(solution)/shard_map/ppermute | solution.py:222
  13.2 6.9 %collective-permute-start.1 = (bf16[256,512]{1,0:T(8,128)(2,1)S(1)}, bf16[256,512]{1,0:T(8,128)(2,1)S(1)}, u32[]{:S(2)}, u32[]{:S(2)}) collective-permute-start(bf16[256,512]{1,0:T(8,128)(2,1)S(1)} %collective-permute-done.refs_0_), channel_id=1, source_target_pairs={{0,2},{1,3},{2,0},{3,1},{4,6},{5,7},{6,4},{7,5},{8,10},{9,11},{10,... | collective-permute-start | bytes 786440 | tf_op jit(solution)/shard_map/ppermute | solution.py:233
  14.5 6.2 %collective-permute-start.4 = (bf16[256,512]{1,0:T(8,128)(2,1)S(1)}, bf16[256,512]{1,0:T(8,128)(2,1)S(1)}, u32[]{:S(2)}, u32[]{:S(2)}) collective-permute-start(bf16[256,512]{1,0:T(8,128)(2,1)S(1)} %collective-permute-done.refs_0_), channel_id=1, source_target_pairs={{0,16},{8,24},{16,0},{24,8},{1,17},{9,25},{17,1},{25,9},{2,18},{10... | collective-permute-start | bytes 786440 | tf_op jit(solution)/shard_map/ppermute | solution.py:226
  15.8 7.1 %collective-permute-start.3 = (bf16[256,512]{1,0:T(8,128)(2,1)S(1)}, bf16[256,512]{1,0:T(8,128)(2,1)S(1)}, u32[]{:S(2)}, u32[]{:S(2)}) collective-permute-start(bf16[256,512]{1,0:T(8,128)(2,1)S(1)} %get-tuple-element.15), channel_id=1, source_target_pairs={{0,8},{8,0},{16,24},{24,16},{1,9},{9,1},{17,25},{25,17},{2,10},{10... | collective-permute-start | bytes 786440 | tf_op jit(solution)/shard_map/ppermute | solution.py:222
  20.8 5.3 %collective-permute-start.5 = (bf16[256,512]{1,0:T(8,128)(2,1)S(1)}, bf16[256,512]{1,0:T(8,128)(2,1)S(1)}, u32[]{:S(2)}, u32[]{:S(2)}) collective-permute-start(bf16[256,512]{1,0:T(8,128)(2,1)S(1)} %copy_after.2), channel_id=1, source_target_pairs={{0,2},{1,3},{2,0},{3,1},{4,6},{5,7},{6,4},{7,5},{8,10},{9,11},{10,... | collective-permute-start | bytes 786440 | tf_op jit(solution)/shard_map/ppermute | solution.py:234
  21.3 9.8 %collective-permute-start.10 = (bf16[256,512]{1,0:T(8,128)(2,1)S(1)}, bf16[256,512]{1,0:T(8,128)(2,1)S(1)}, u32[]{:S(2)}, u32[]{:S(2)}) collective-permute-start(bf16[256,512]{1,0:T(8,128)(2,1)S(1)} %collective-permute-done.2.refs_0_.refs_2_), channel_id=1, source_target_pairs={{0,16},{8,24},{16,0},{24,8},{1,17},{9,25},{17,1},{25,9},{2,18},{10... | collective-permute-start | bytes 786440 | tf_op jit(solution)/shard_map/ppermute | solution.py:226
  22.9 9.7 %collective-permute-start.11 = (bf16[256,512]{1,0:T(8,128)(2,1)S(1)}, bf16[256,512]{1,0:T(8,128)(2,1)S(1)}, u32[]{:S(2)}, u32[]{:S(2)}) collective-permute-start(bf16[256,512]{1,0:T(8,128)(2,1)S(1)} %copy_after.3), channel_id=1, source_target_pairs={{0,16},{8,24},{16,0},{24,8},{1,17},{9,25},{17,1},{25,9},{2,18},{10... | collective-permute-start | bytes 786440 | tf_op jit(solution)/shard_map/ppermute | solution.py:227
  29.0 8.7 %copy-start = (f32[2,128,512]{2,1,0:T(8,128)S(1)}, f32[2,128,512]{2,1,0:T(8,128)}, u32[]{:S(2)}) copy-start(f32[2,128,512]{2,1,0:T(8,128)} %get-tuple-element.17) | copy-start | bytes 1572868
  29.0 8.6 %collective-permute-start.7 = (bf16[2,128,512]{2,1,0:T(8,128)(2,1)S(1)}, bf16[2,128,512]{2,1,0:T(8,128)(2,1)S(1)}, u32[]{:S(2)}, u32[]{:S(2)}) collective-permute-start(bf16[2,128,512]{2,1,0:T(8,128)(2,1)S(1)} %get-tuple-element.18), channel_id=1, source_target_pairs={{0,2},{1,3},{2,0},{3,1},{4,6},{5,7},{6,4},{7,5},{8,10},{9,11},{10,... | collective-permute-start | bytes 786440 | tf_op jit(solution)/shard_map/ppermute | solution.py:206
  35.0 8.3 %collective-permute-start.12 = (bf16[2,128,512]{2,1,0:T(8,128)(2,1)S(1)}, bf16[2,128,512]{2,1,0:T(8,128)(2,1)S(1)}, u32[]{:S(2)}, u32[]{:S(2)}) collective-permute-start(bf16[2,128,512]{2,1,0:T(8,128)(2,1)S(1)} %get-tuple-element.20), channel_id=1, source_target_pairs={{0,2},{1,3},{2,0},{3,1},{4,6},{5,7},{6,4},{7,5},{8,10},{9,11},{10,... | collective-permute-start | bytes 786440 | tf_op jit(solution)/shard_map/ppermute | solution.py:206
  37.8 13.5 %collective-permute-start.8 = (bf16[1,128,512]{2,1,0:T(8,128)(2,1)S(1)}, bf16[1,128,512]{2,1,0:T(8,128)(2,1)S(1)}, u32[]{:S(2)}, u32[]{:S(2)}) collective-permute-start(bf16[1,128,512]{2,1,0:T(8,128)(2,1)S(1)} %slice.81), channel_id=1, source_target_pairs={{0,4},{1,5},{2,6},{3,7},{4,0},{5,1},{6,2},{7,3},{8,12},{9,13},{10,... | collective-permute-start | bytes 393224 | tf_op jit(solution)/shard_map/ppermute | solution.py:206
  43.4 8.5 %collective-permute-start.13 = (bf16[64,512]{1,0:T(8,128)(2,1)S(1)}, bf16[64,512]{1,0:T(8,128)(2,1)S(1)}, u32[]{:S(2)}, u32[]{:S(2)}) collective-permute-start(bf16[64,512]{1,0:T(8,128)(2,1)S(1)} %get-tuple-element.23), channel_id=1, source_target_pairs={{0,4},{1,5},{2,6},{3,7},{4,0},{5,1},{6,2},{7,3},{8,12},{9,13},{10,... | collective-permute-start | bytes 196616 | tf_op jit(solution)/shard_map/ppermute | solution.py:203
  45.7 10.9 %collective-permute-start.14 = (f32[128,512]{1,0:T(8,128)S(1)}, f32[128,512]{1,0:T(8,128)S(1)}, u32[]{:S(2)}, u32[]{:S(2)}) collective-permute-start(f32[128,512]{1,0:T(8,128)S(1)} %slice_bitcast_fusion), channel_id=1, source_target_pairs={{0,1},{1,0},{2,3},{3,2},{4,5},{5,4},{6,7},{7,6},{8,9},{9,8},{10,11... | collective-permute-start | bytes 786440 | tf_op jit(solution)/shard_map/ppermute | solution.py:202
  49.9 6.7 %collective-permute-start.15 = (bf16[64,512]{1,0:T(8,128)(2,1)S(1)}, bf16[64,512]{1,0:T(8,128)(2,1)S(1)}, u32[]{:S(2)}, u32[]{:S(2)}) collective-permute-start(bf16[64,512]{1,0:T(8,128)(2,1)S(1)} %get-tuple-element.24), channel_id=1, source_target_pairs={{0,5},{1,4},{2,7},{3,6},{4,1},{5,0},{6,3},{7,2},{8,13},{9,12},{10,... | collective-permute-start | bytes 196616 | tf_op jit(solution)/shard_map/ppermute | solution.py:204
  51.4 1.4 %collective-permute-start.9 = (bf16[64,512]{1,0:T(8,128)(2,1)S(1)}, bf16[64,512]{1,0:T(8,128)(2,1)S(1)}, u32[]{:S(2)}, u32[]{:S(2)}) collective-permute-start(bf16[64,512]{1,0:T(8,128)(2,1)S(1)} %get-tuple-element.26), channel_id=1, source_target_pairs={{0,1},{1,0},{2,3},{3,2},{4,5},{5,4},{6,7},{7,6},{8,9},{9,8},{10,11... | collective-permute-start | bytes 196616 | tf_op jit(solution)/shard_map/ppermute | solution.py:209

commit v6 on v5

--- a/solution.py
+++ b/solution.py
@@ -35,16 +35,16 @@
     rows = size // 2
 
     def body(place_ref, psi_ref, left_ref, right_ref, *refs):
-        parts, pack, sem = refs[:3], refs[3], refs[4]
+        parts, pack, sem = refs[:4], refs[4], refs[5]
         core, odd, half = place_ref[0], place_ref[1], place_ref[3] % 2
         copies = [
             pltpu.make_async_copy(psi_ref.at[sector, core, pl.ds(start * rows, rows)], part, sem.at[n])
-            for n, (part, sector, start) in enumerate(zip(parts, (odd, 1 - odd, 1 - odd), (half, 0, 1), strict=True))
+            for n, (part, sector, start) in enumerate(zip(parts, (odd, 1 - odd, 1 - odd, odd), (half, 0, 1, 1 - half), strict=True))
         ]
         for k, ref in enumerate((left_ref, right_ref)):
             for s in range(2):
                 at = pl.ds((2 * k + s) * size, size)
-                copies.append(pltpu.make_async_copy(ref.at[0, s], pack.at[at], sem.at[3 + 2 * k + s]))
+                copies.append(pltpu.make_async_copy(ref.at[0, s], pack.at[at], sem.at[4 + 2 * k + s]))
         for copy in copies:
             copy.start()
         number = lax.broadcasted_iota(jnp.int32, (16, size), 0)
@@ -53,14 +53,14 @@
         for copy in copies:
             copy.wait()
 
-    out = [pltpu.VMEM((rows, size), psi.dtype)] * 3 + [pltpu.VMEM((4 * size + 16, size), psi.dtype)]
+    out = [pltpu.VMEM((rows, size), psi.dtype)] * 4 + [pltpu.VMEM((4 * size + 16, size), psi.dtype)]
     *parts, pack = call(
         body,
         "cut",
         out_shape=out,
         in_specs=[SMEM_SPEC] + [ANY_SPEC] * 3,
-        out_specs=[VMEM_SPEC] * 4,
-        scratch_shapes=[pltpu.SemaphoreType.DMA((7,))],
+        out_specs=[VMEM_SPEC] * 5,
+        scratch_shapes=[pltpu.SemaphoreType.DMA((8,))],
     )(place, in_hbm(psi), in_hbm(left), in_hbm(right))
     return parts, pack
 
@@ -82,20 +82,19 @@
     )(in_vmem(part), *after)
 
 
-def piece(step, secs, chips, bits, scalars, halo, swapped, pack1, pack0, psi):
+def piece(step, secs, chips, bits, scalars, sources, swapped, pack1, pack0):
     def relative(q):
         return sum((q >> k & 1) << bit for k, bit in enumerate(bits))
 
-    size = psi.shape[-1]
+    size = pack1.shape[-1]
     parked = step == 0
-    slots, height, count = len(halo), size // chips, chips // 2
+    slots, height, count = len(sources), size // chips, chips // 2
     rows = size // 2
-    near = [part for block in halo for part in block] + [pack1, pack0]
-    far = [psi]
+    near = [part for block in sources for part in block] + [pack1, pack0]
 
     def body(place, *refs):
         halves, pack, own_pack, refs = refs[: 2 * slots], refs[2 * slots], refs[2 * slots + 1], refs[2 * slots + 2 :]
-        psi_ref, stay, gone, own, inner, kept, sem = refs
+        stay, gone, inner, kept, sem = refs
         core, odd, i, z = place[0], place[1], place[2], place[3]
         sector = step * odd + (1 - step) * (1 - odd)
         flags = pack[pl.ds(4 * size, 16), pl.ds(0, 128)].astype(jnp.float32)
@@ -104,21 +103,11 @@
         for shift, live in ((place[4], place[5]), (shift1, live1)):
             rel = sector - shift
             at = step - (2 * odd - 1) * shift
-            if step == 0:
-                slot = jnp.where(at == 2, 2, at + 2)
-            else:
-                slot = jnp.where(at >= 2, at - 1, at + 1)
-            slot_of.append(jnp.where((rel == 0) | (rel == 1), slots + rel, slot))
+            came = jnp.where(at == 2, 2, at + 2) if step == 0 else jnp.where(at >= 2, at - 1, at + 1)
+            slot_of.append(jnp.where((at == 0) | (at == 1), at + 3, came))
             there = ((rel >= 0) | (i > 0)) & ((rel <= 1) | (i < secs - 1))
             weight_of.append(jnp.where(there, live, 0).astype(jnp.float32))
 
-        def own_copy(term, index):
-            return pltpu.make_async_copy(psi_ref.at[index, core], own.at[term], sem.at[term])
-
-        for term in (1, 0):
-            @pl.when(slot_of[term] >= slots)
-            def _(term=term):
-                own_copy(term, slot_of[term] - slots).start()
         order = [relative(q) for q in [*range(1, chips, 2), *range(0, chips, 2)]]
         for term in (1, 0):
             def left_rows(group, column, term=term):
@@ -131,11 +120,11 @@
 
                 return jnp.concatenate([at(r, k) for r in order[group * count : (group + 1) * count] for k in range(2)])
 
-            def first_product(sources, columns, term=term, left_rows=left_rows):
+            def first_product(reads, columns, term=term, left_rows=left_rows):
                 for group in range(2):
                     product = sum(
-                        jnp.dot(left_rows(group, column), source(), preferred_element_type=jnp.float32)
-                        for source, column in zip(sources, columns)
+                        jnp.dot(left_rows(group, column), read(), preferred_element_type=jnp.float32)
+                        for read, column in zip(reads, columns, strict=True)
                     )
                     inner[term, pl.ds(group * rows, rows)] = product.astype(jnp.bfloat16)
 
@@ -143,15 +132,9 @@
                 @pl.when(slot_of[term] == k)
                 def _(k=k):
                     parity = z % 2 if swapped[k] else 0
-                    sources = [lambda n=n: halves[2 * k + n][...] for n in range(2)]
-                    first_product(sources, [parity, 1 - parity])
-
-            @pl.when(slot_of[term] >= slots)
-            def _(term=term):
-                own_copy(term, 0).wait()
-                first_product([lambda n=n: own[term, pl.ds(n * rows, rows)] for n in range(2)], [0, 1])
-
-        stay_copy = pltpu.make_async_copy(kept, stay, sem.at[4]) if parked else None
+                    first_product([lambda n=n: halves[2 * k + n][...] for n in range(2)], [parity, 1 - parity])
+
+        stay_copy = pltpu.make_async_copy(kept, stay, sem) if parked else None
         for group in (1, 0):
             total = sum(
                 lax.dot_general(
@@ -181,15 +164,14 @@
         body,
         "piece",
         out_shape=outs,
-        in_specs=[SMEM_SPEC] + [VMEM_SPEC] * len(near) + [ANY_SPEC] * len(far),
+        in_specs=[SMEM_SPEC] + [VMEM_SPEC] * len(near),
         out_specs=[ANY_SPEC if parked else VMEM_SPEC] + [VMEM_SPEC] * (len(outs) - 1),
         scratch_shapes=[
             pltpu.VMEM((2, size, size), jnp.bfloat16),
-            pltpu.VMEM((2, size, size), jnp.bfloat16),
             pltpu.VMEM((count, height, size), jnp.float32),
-            pltpu.SemaphoreType.DMA((5,)),
+            pltpu.SemaphoreType.DMA,
         ],
-    )(*scalars, *[in_vmem(x) for x in near], *[in_hbm(x) for x in far])
+    )(*scalars, *[in_vmem(x) for x in near])
 
 
 def sum_over_chips(stay, gone, bits, terms, direct):
@@ -218,7 +200,7 @@
     pairs = [(d, d ^ 1) for d in range(secs)]
 
     place = jnp.stack([core, odd, i, z, shift[0], live[0]]).astype(jnp.int32)
-    parts, pack0 = cut(place, psi, left_ops, right_ops)
+    (*parts, rest), pack0 = cut(place, psi, left_ops, right_ops)
     near = [lax.ppermute(part, "sec", pairs) for part in parts]
     pack1 = lax.ppermute(pack0, "term", cores)
     if secs == 4:
@@ -236,10 +218,11 @@
     scalars = (place,)
     outs = []
     for step in range(2):
-        halo = (near_first, near_second, far_first) if step == 0 else (near_second, far_first, far_second)
-        swapped = (True, False, True) if step == 0 else (False, True, False)
+        came = (near_first, near_second, far_first) if step == 0 else (near_second, far_first, far_second)
+        sources = (*came, parts[1:], (parts[0], rest))
+        swapped = (True, False, True, False, True) if step == 0 else (False, True, False, False, True)
         bits = list(range((terms // 2).bit_length() - 1))
-        blocks = piece(step, secs, terms // 2, bits, scalars, halo, swapped, pack1, pack0, psi)
+        blocks = piece(step, secs, terms // 2, bits, scalars, sources, swapped, pack1, pack0)
         mine, got = sum_over_chips(*blocks, bits, terms, step == 1)
         outs.append(jnp.where(core == 0, jnp.stack([mine, got]), jnp.stack([got, mine])))
     return jnp.where(odd == 1, jnp.stack(outs), jnp.stack(outs[::-1]))

time: 56.7 us -> 56.7 us (level); the launches traced: 57.4 us -> 56.6 us
  starting transfers between devices: 26.7 us -> 23.1 us
  waiting for transfers between devices: 20.3 us -> 23 us
    ppermute x3, starting transfers between devices: 7.2 us -> 5.14 us  [sum_over_chips(): total = stay + lax.ppermute(gone, 'term', pairs).astype(jnp.float32)]
    ppermute x1, starting transfers between devices: 2.33 us -> 0.66 us  [sum_over_chips(): lax.ppermute(gone[0, :half], 'term', pairs).astype(jnp.float32)]
    ppermute x3, waiting for transfers between devices: 3.09 us -> 4.73 us  [sum_over_chips(): total = stay + lax.ppermute(gone, 'term', pairs).astype(jnp.float32)]
    ppermute x1, waiting for transfers between devices: 1.42 us -> 2.46 us  [local(): far.append(lax.ppermute(copy_after(near[2], far[0]), 'sec', turn))]
where the time goes in v6:
time: 56.7 us; the launch traced here: 56.6 us
  starting transfers between devices  23.1 us (41%)
  waiting for transfers between devices  23 us (41%)
  Pallas kernels  7.8 us (14%)
  between operations  1.44 us (3%)
  other arithmetic  0.98 us (2%)
    ppermute x3, waiting for transfers between devices, local(): near = [lax.ppermute(part, 'sec', pairs) for part in parts]  8.81 us
    pallas_call x2, Pallas kernels, piece(): call(body, 'piece', out_shape=outs, in_specs=[SMEM_SPEC] + [VMEM_SPEC] *...  5.29 us
    ppermute x3, starting transfers between devices, sum_over_chips(): total = stay + lax.ppermute(gone, 'term', pairs).astype(jnp.float32)  5.14 us
    ppermute x3, waiting for transfers between devices, sum_over_chips(): total = stay + lax.ppermute(gone, 'term', pairs).astype(jnp.float32)  4.73 us
    ppermute x1, starting transfers between devices, sum_over_chips(): swapped = lax.ppermute(stay[0], 'term', cores)[half:]  4.34 us
    ppermute x3, starting transfers between devices, local(): near = [lax.ppermute(part, 'sec', pairs) for part in parts]  3.9 us
    ppermute x1, waiting for transfers between devices, sum_over_chips(): lax.ppermute(gone[0, half:], 'term', across).astype(jnp.float32)  3.8 us
    ppermute x1, starting transfers between devices, local(): far.append(lax.ppermute(copy_after(near[2], far[0]), 'sec', turn))  2.85 us
  transfers between devices with their start and end apart: 16, of which 10 were waited for; matrix products, arithmetic and copies ran while one was open for 0% of the time, Pallas kernels for 9%

profile of v6, /device:TPU:1, one launch (start us, length us, event | category | flops | bytes accessed | tf_op | source)
XLA Modules:
  0.0 56.6 jit_solution(2302136775809749002)
XLA Ops:
  1.4 2.5 %cut.1 = (bf16[256,512]{1,0:T(8,128)(2,1)S(1)}, bf16[256,512]{1,0:T(8,128)(2,1)S(1)}, bf16[256,512]{1,0:T(8,128)(2,1)S(1)}, bf16[256,512]{1,0:T(8,128)(2,1)S(1)}, bf16[2064,512]{1,0:T(8,128)(2,1)S(1)}) custom-call(s32[6]{0:T(128)S(1)} %stack.57.place_ref.place, bf16[2,2,512,512]{3,2,1,0:T(8,128)(2,1)} %psi_ref.1, bf16[1,2,512,512]{3,2,1,0:T(8,128)(2,1)} %left_ref.1, ...), custom_call_target="tpu_custom_call" | custom-call | flops 1000 | bytes 1000 | tf_op jit(solution)/shard_map/cut/pallas_call | solution.py:57
  4.0 2.7 %collective-permute-start = (bf16[256,512]{1,0:T(8,128)(2,1)S(1)}, bf16[256,512]{1,0:T(8,128)(2,1)S(1)}, u32[]{:S(2)}, u32[]{:S(2)}) collective-permute-start(bf16[256,512]{1,0:T(8,128)(2,1)S(1)} %get-tuple-element.14.refs_8_), channel_id=1, source_target_pairs={{0,8},{8,0},{16,24},{24,16},{1,9},{9,1},{17,25},{25,17},{2,10},{10... | collective-permute-start | bytes 786440 | tf_op jit(solution)/shard_map/ppermute | solution.py:204
  6.7 6.6 %collective-permute-done.refs_0_ = bf16[256,512]{1,0:T(8,128)(2,1)S(1)} collective-permute-done((bf16[256,512]{1,0:T(8,128)(2,1)S(1)}, bf16[256,512]{1,0:T(8,128)(2,1)S(1)}, u32[]{:S(2)}, u32[]{:S(2)}) %collective-permute-start) | collective-permute-done | bytes 262176 | tf_op jit(solution)/shard_map/ppermute | solution.py:204
  13.2 1.4 %collective-permute-start.1 = (bf16[256,512]{1,0:T(8,128)(2,1)S(1)}, bf16[256,512]{1,0:T(8,128)(2,1)S(1)}, u32[]{:S(2)}, u32[]{:S(2)}) collective-permute-start(bf16[256,512]{1,0:T(8,128)(2,1)S(1)} %collective-permute-done.refs_0_), channel_id=1, source_target_pairs={{0,2},{1,3},{2,0},{3,1},{4,6},{5,7},{6,4},{7,5},{8,10},{9,11},{10,... | collective-permute-start | bytes 786440 | tf_op jit(solution)/shard_map/ppermute | solution.py:215
  14.6 1.2 %collective-permute-start.4 = (bf16[256,512]{1,0:T(8,128)(2,1)S(1)}, bf16[256,512]{1,0:T(8,128)(2,1)S(1)}, u32[]{:S(2)}, u32[]{:S(2)}) collective-permute-start(bf16[256,512]{1,0:T(8,128)(2,1)S(1)} %collective-permute-done.refs_0_), channel_id=1, source_target_pairs={{0,16},{8,24},{16,0},{24,8},{1,17},{9,25},{17,1},{25,9},{2,18},{10... | collective-permute-start | bytes 786440 | tf_op jit(solution)/shard_map/ppermute | solution.py:208
  15.8 1.2 %collective-permute-start.3 = (bf16[256,512]{1,0:T(8,128)(2,1)S(1)}, bf16[256,512]{1,0:T(8,128)(2,1)S(1)}, u32[]{:S(2)}, u32[]{:S(2)}) collective-permute-start(bf16[256,512]{1,0:T(8,128)(2,1)S(1)} %get-tuple-element.16.refs_7_), channel_id=1, source_target_pairs={{0,8},{8,0},{16,24},{24,16},{1,9},{9,1},{17,25},{25,17},{2,10},{10... | collective-permute-start | bytes 786440 | tf_op jit(solution)/shard_map/ppermute | solution.py:204
  17.1 1.8 %collective-permute-done.2.refs_0_.refs_2_ = bf16[256,512]{1,0:T(8,128)(2,1)S(1)} collective-permute-done((bf16[256,512]{1,0:T(8,128)(2,1)S(1)}, bf16[256,512]{1,0:T(8,128)(2,1)S(1)}, u32[]{:S(2)}, u32[]{:S(2)}) %collective-permute-start.2) | collective-permute-done | bytes 262176 | tf_op jit(solution)/shard_map/ppermute | solution.py:204
  18.9 1.3 %collective-permute-done.1.refs_1_ = bf16[256,512]{1,0:T(8,128)(2,1)S(1)} collective-permute-done((bf16[256,512]{1,0:T(8,128)(2,1)S(1)}, bf16[256,512]{1,0:T(8,128)(2,1)S(1)}, u32[]{:S(2)}, u32[]{:S(2)}) %collective-permute-start.1) | collective-permute-done | bytes 262176 | tf_op jit(solution)/shard_map/ppermute | solution.py:215
  20.1 0.7 %collective-permute-done.4.part_ref.refs_4_.refs_0_.refs_2_ = bf16[256,512]{1,0:T(8,128)(2,1)S(1)} collective-permute-done((bf16[256,512]{1,0:T(8,128)(2,1)S(1)}, bf16[256,512]{1,0:T(8,128)(2,1)S(1)}, u32[]{:S(2)}, u32[]{:S(2)}) %collective-permute-start.4) | collective-permute-done | bytes 262176 | tf_op jit(solution)/shard_map/ppermute | solution.py:208
  21.4 1.1 %collective-permute-start.10 = (bf16[256,512]{1,0:T(8,128)(2,1)S(1)}, bf16[256,512]{1,0:T(8,128)(2,1)S(1)}, u32[]{:S(2)}, u32[]{:S(2)}) collective-permute-start(bf16[256,512]{1,0:T(8,128)(2,1)S(1)} %collective-permute-done.2.refs_0_.refs_2_), channel_id=1, source_target_pairs={{0,16},{8,24},{16,0},{24,8},{1,17},{9,25},{17,1},{25,9},{2,18},{10... | collective-permute-start | bytes 786440 | tf_op jit(solution)/shard_map/ppermute | solution.py:208
  22.9 2.8 %collective-permute-start.11 = (bf16[256,512]{1,0:T(8,128)(2,1)S(1)}, bf16[256,512]{1,0:T(8,128)(2,1)S(1)}, u32[]{:S(2)}, u32[]{:S(2)}) collective-permute-start(bf16[256,512]{1,0:T(8,128)(2,1)S(1)} %copy_after.3), channel_id=1, source_target_pairs={{0,16},{8,24},{16,0},{24,8},{1,17},{9,25},{17,1},{25,9},{2,18},{10... | collective-permute-start | bytes 786440 | tf_op jit(solution)/shard_map/ppermute | solution.py:209
  26.2 2.9 %piece.2 = (f32[2,128,512]{2,1,0:T(8,128)}, bf16[2,128,512]{2,1,0:T(8,128)(2,1)S(1)}) custom-call(s32[6]{0:T(128)S(1)} %stack.57.place_ref.place, bf16[256,512]{1,0:T(8,128)(2,1)S(1)} %collective-permute-done.refs_0_, bf16[256,512]{1,0:T(8,128)(2,1)S(1)} %collective-permute-done.1.refs_1_, bf16[256,512]{1,0:T(8,128)(2,1)S(1)} %collective-permute-done.2.refs_0_.refs_2_, ...), custom_call_target="tpu_custom_call" | custom-call | flops 1000 | bytes 1000 | tf_op jit(solution)/shard_map/piece/pallas_call | solution.py:163
  29.1 1.1 %collective-permute-start.7 = (bf16[2,128,512]{2,1,0:T(8,128)(2,1)S(1)}, bf16[2,128,512]{2,1,0:T(8,128)(2,1)S(1)}, u32[]{:S(2)}, u32[]{:S(2)}) collective-permute-start(bf16[2,128,512]{2,1,0:T(8,128)(2,1)S(1)} %get-tuple-element.20), channel_id=1, source_target_pairs={{0,2},{1,3},{2,0},{3,1},{4,6},{5,7},{6,4},{7,5},{8,10},{9,11},{10,... | collective-permute-start | bytes 786440 | tf_op jit(solution)/shard_map/ppermute | solution.py:188
  30.2 2.5 %collective-permute-done.11.refs_5_ = bf16[256,512]{1,0:T(8,128)(2,1)S(1)} collective-permute-done((bf16[256,512]{1,0:T(8,128)(2,1)S(1)}, bf16[256,512]{1,0:T(8,128)(2,1)S(1)}, u32[]{:S(2)}, u32[]{:S(2)}) %collective-permute-start.11) | collective-permute-done | bytes 262176 | tf_op jit(solution)/shard_map/ppermute | solution.py:209
  32.7 2.4 %piece.3 = (f32[2,128,512]{2,1,0:T(8,128)S(1)}, bf16[2,128,512]{2,1,0:T(8,128)(2,1)S(1)}) custom-call(s32[6]{0:T(128)S(1)} %stack.57.place_ref.place, bf16[256,512]{1,0:T(8,128)(2,1)S(1)} %collective-permute-done.2.refs_0_.refs_2_, bf16[256,512]{1,0:T(8,128)(2,1)S(1)} %collective-permute-done.3.refs_3_.part_ref.refs_1_, ...), custom_call_target="tpu_custom_call" | custom-call | flops 1000 | bytes 1000 | tf_op jit(solution)/shard_map/piece/pallas_call | solution.py:163
  35.0 1.7 %collective-permute-start.12 = (bf16[2,128,512]{2,1,0:T(8,128)(2,1)S(1)}, bf16[2,128,512]{2,1,0:T(8,128)(2,1)S(1)}, u32[]{:S(2)}, u32[]{:S(2)}) collective-permute-start(bf16[2,128,512]{2,1,0:T(8,128)(2,1)S(1)} %get-tuple-element.22), channel_id=1, source_target_pairs={{0,2},{1,3},{2,0},{3,1},{4,6},{5,7},{6,4},{7,5},{8,10},{9,11},{10,... | collective-permute-start | bytes 786440 | tf_op jit(solution)/shard_map/ppermute | solution.py:188
  36.8 2.4 %collective-permute-start.8 = (bf16[1,128,512]{2,1,0:T(8,128)(2,1)S(1)}, bf16[1,128,512]{2,1,0:T(8,128)(2,1)S(1)}, u32[]{:S(2)}, u32[]{:S(2)}) collective-permute-start(bf16[1,128,512]{2,1,0:T(8,128)(2,1)S(1)} %slice.81), channel_id=1, source_target_pairs={{0,4},{1,5},{2,6},{3,7},{4,0},{5,1},{6,2},{7,3},{8,12},{9,13},{10,... | collective-permute-start | bytes 393224 | tf_op jit(solution)/shard_map/ppermute | solution.py:188
  39.2 4.7 %collective-permute-done.12 = bf16[2,128,512]{2,1,0:T(8,128)(2,1)S(1)} collective-permute-done((bf16[2,128,512]{2,1,0:T(8,128)(2,1)S(1)}, bf16[2,128,512]{2,1,0:T(8,128)(2,1)S(1)}, u32[]{:S(2)}, u32[]{:S(2)}) %collective-permute-start.12) | collective-permute-done | bytes 262176 | tf_op jit(solution)/shard_map/ppermute | solution.py:188
  44.0 0.7 %collective-permute-start.13 = (bf16[64,512]{1,0:T(8,128)(2,1)S(1)}, bf16[64,512]{1,0:T(8,128)(2,1)S(1)}, u32[]{:S(2)}, u32[]{:S(2)}) collective-permute-start(bf16[64,512]{1,0:T(8,128)(2,1)S(1)} %get-tuple-element.25), channel_id=1, source_target_pairs={{0,4},{1,5},{2,6},{3,7},{4,0},{5,1},{6,2},{7,3},{8,12},{9,13},{10,... | collective-permute-start | bytes 196616 | tf_op jit(solution)/shard_map/ppermute | solution.py:185
  44.7 4.3 %collective-permute-start.14 = (f32[128,512]{1,0:T(8,128)S(1)}, f32[128,512]{1,0:T(8,128)S(1)}, u32[]{:S(2)}, u32[]{:S(2)}) collective-permute-start(f32[128,512]{1,0:T(8,128)S(1)} %slice_bitcast_fusion), channel_id=1, source_target_pairs={{0,1},{1,0},{2,3},{3,2},{4,5},{5,4},{6,7},{7,6},{8,9},{9,8},{10,11... | collective-permute-start | bytes 786440 | tf_op jit(solution)/shard_map/ppermute | solution.py:184
  49.1 1.4 %collective-permute-start.15 = (bf16[64,512]{1,0:T(8,128)(2,1)S(1)}, bf16[64,512]{1,0:T(8,128)(2,1)S(1)}, u32[]{:S(2)}, u32[]{:S(2)}) collective-permute-start(bf16[64,512]{1,0:T(8,128)(2,1)S(1)} %get-tuple-element.26), channel_id=1, source_target_pairs={{0,5},{1,4},{2,7},{3,6},{4,1},{5,0},{6,3},{7,2},{8,13},{9,12},{10,... | collective-permute-start | bytes 196616 | tf_op jit(solution)/shard_map/ppermute | solution.py:186
  51.1 0.9 %collective-permute-done.9 = bf16[64,512]{1,0:T(8,128)(2,1)S(1)} collective-permute-done((bf16[64,512]{1,0:T(8,128)(2,1)S(1)}, bf16[64,512]{1,0:T(8,128)(2,1)S(1)}, u32[]{:S(2)}, u32[]{:S(2)}) %collective-permute-start.9) | collective-permute-done | bytes 65568 | tf_op jit(solution)/shard_map/ppermute | solution.py:191
  52.0 3.8 %collective-permute-done.15 = bf16[64,512]{1,0:T(8,128)(2,1)S(1)} collective-permute-done((bf16[64,512]{1,0:T(8,128)(2,1)S(1)}, bf16[64,512]{1,0:T(8,128)(2,1)S(1)}, u32[]{:S(2)}, u32[]{:S(2)}) %collective-permute-start.15) | collective-permute-done | bytes 65568 | tf_op jit(solution)/shard_map/ppermute | solution.py:186
  55.8 0.7 %maximum_select_fusion = bf16[2,2,64,512]{3,2,1,0:T(8,128)(2,1)} fusion(bf16[1,2,64,512]{3,2,1,0:T(8,128)(2,1)S(1)} %maximum_select_fusion.2, bf16[1,2,64,512]{3,2,1,0:T(8,128)(2,1)S(1)} %maximum_select_fusion.1, pred[]{:T(512)S(6)} %eq.10), kind=kLoop, calls=%fused_computation.6 | loop fusion | flops 393216 | bytes 524289 | tf_op jit(solution)/shard_map/jit(_where)/select_n | solution.py:228
  (28 shorter events, 2.5 us)
Async XLA Ops:
  3.9 22.3 %collective-permute-start.6 = (bf16[2064,512]{1,0:T(8,128)(2,1)S(1)}, bf16[2064,512]{1,0:T(8,128)(2,1)S(1)}, u32[]{:S(2)}, u32[]{:S(2)}) collective-permute-start(bf16[2064,512]{1,0:T(8,128)(2,1)S(1)} %get-tuple-element.18.refs_11_), channel_id=1, source_target_pairs={{0,1},{1,0},{2,3},{3,2},{4,5},{5,4},{6,7},{7,6},{8,9},{9,8},{10,11... | collective-permute-start | bytes 6340616 | tf_op jit(solution)/shard_map/ppermute | solution.py:205
  4.0 9.3 %collective-permute-start = (bf16[256,512]{1,0:T(8,128)(2,1)S(1)}, bf16[256,512]{1,0:T(8,128)(2,1)S(1)}, u32[]{:S(2)}, u32[]{:S(2)}) collective-permute-start(bf16[256,512]{1,0:T(8,128)(2,1)S(1)} %get-tuple-element.14.refs_8_), channel_id=1, source_target_pairs={{0,8},{8,0},{16,24},{24,16},{1,9},{9,1},{17,25},{25,17},{2,10},{10... | collective-permute-start | bytes 786440 | tf_op jit(solution)/shard_map/ppermute | solution.py:204
  6.7 12.2 %collective-permute-start.2 = (bf16[256,512]{1,0:T(8,128)(2,1)S(1)}, bf16[256,512]{1,0:T(8,128)(2,1)S(1)}, u32[]{:S(2)}, u32[]{:S(2)}) collective-permute-start(bf16[256,512]{1,0:T(8,128)(2,1)S(1)} %get-tuple-element.15.refs_6_), channel_id=1, source_target_pairs={{0,8},{8,0},{16,24},{24,16},{1,9},{9,1},{17,25},{25,17},{2,10},{10... | collective-permute-start | bytes 786440 | tf_op jit(solution)/shard_map/ppermute | solution.py:204
  13.2 6.9 %collective-permute-start.1 = (bf16[256,512]{1,0:T(8,128)(2,1)S(1)}, bf16[256,512]{1,0:T(8,128)(2,1)S(1)}, u32[]{:S(2)}, u32[]{:S(2)}) collective-permute-start(bf16[256,512]{1,0:T(8,128)(2,1)S(1)} %collective-permute-done.refs_0_), channel_id=1, source_target_pairs={{0,2},{1,3},{2,0},{3,1},{4,6},{5,7},{6,4},{7,5},{8,10},{9,11},{10,... | collective-permute-start | bytes 786440 | tf_op jit(solution)/shard_map/ppermute | solution.py:215
  14.6 6.2 %collective-permute-start.4 = (bf16[256,512]{1,0:T(8,128)(2,1)S(1)}, bf16[256,512]{1,0:T(8,128)(2,1)S(1)}, u32[]{:S(2)}, u32[]{:S(2)}) collective-permute-start(bf16[256,512]{1,0:T(8,128)(2,1)S(1)} %collective-permute-done.refs_0_), channel_id=1, source_target_pairs={{0,16},{8,24},{16,0},{24,8},{1,17},{9,25},{17,1},{25,9},{2,18},{10... | collective-permute-start | bytes 786440 | tf_op jit(solution)/shard_map/ppermute | solution.py:208
  15.8 7.1 %collective-permute-start.3 = (bf16[256,512]{1,0:T(8,128)(2,1)S(1)}, bf16[256,512]{1,0:T(8,128)(2,1)S(1)}, u32[]{:S(2)}, u32[]{:S(2)}) collective-permute-start(bf16[256,512]{1,0:T(8,128)(2,1)S(1)} %get-tuple-element.16.refs_7_), channel_id=1, source_target_pairs={{0,8},{8,0},{16,24},{24,16},{1,9},{9,1},{17,25},{25,17},{2,10},{10... | collective-permute-start | bytes 786440 | tf_op jit(solution)/shard_map/ppermute | solution.py:204
  20.9 5.3 %collective-permute-start.5 = (bf16[256,512]{1,0:T(8,128)(2,1)S(1)}, bf16[256,512]{1,0:T(8,128)(2,1)S(1)}, u32[]{:S(2)}, u32[]{:S(2)}) collective-permute-start(bf16[256,512]{1,0:T(8,128)(2,1)S(1)} %copy_after.2), channel_id=1, source_target_pairs={{0,2},{1,3},{2,0},{3,1},{4,6},{5,7},{6,4},{7,5},{8,10},{9,11},{10,... | collective-permute-start | bytes 786440 | tf_op jit(solution)/shard_map/ppermute | solution.py:216
  21.4 8.8 %collective-permute-start.10 = (bf16[256,512]{1,0:T(8,128)(2,1)S(1)}, bf16[256,512]{1,0:T(8,128)(2,1)S(1)}, u32[]{:S(2)}, u32[]{:S(2)}) collective-permute-start(bf16[256,512]{1,0:T(8,128)(2,1)S(1)} %collective-permute-done.2.refs_0_.refs_2_), channel_id=1, source_target_pairs={{0,16},{8,24},{16,0},{24,8},{1,17},{9,25},{17,1},{25,9},{2,18},{10... | collective-permute-start | bytes 786440 | tf_op jit(solution)/shard_map/ppermute | solution.py:208
  22.9 9.7 %collective-permute-start.11 = (bf16[256,512]{1,0:T(8,128)(2,1)S(1)}, bf16[256,512]{1,0:T(8,128)(2,1)S(1)}, u32[]{:S(2)}, u32[]{:S(2)}) collective-permute-start(bf16[256,512]{1,0:T(8,128)(2,1)S(1)} %copy_after.3), channel_id=1, source_target_pairs={{0,16},{8,24},{16,0},{24,8},{1,17},{9,25},{17,1},{25,9},{2,18},{10... | collective-permute-start | bytes 786440 | tf_op jit(solution)/shard_map/ppermute | solution.py:209
  29.1 7.6 %copy-start = (f32[2,128,512]{2,1,0:T(8,128)S(1)}, f32[2,128,512]{2,1,0:T(8,128)}, u32[]{:S(2)}) copy-start(f32[2,128,512]{2,1,0:T(8,128)} %get-tuple-element.19) | copy-start | bytes 1572868
  29.1 7.6 %collective-permute-start.7 = (bf16[2,128,512]{2,1,0:T(8,128)(2,1)S(1)}, bf16[2,128,512]{2,1,0:T(8,128)(2,1)S(1)}, u32[]{:S(2)}, u32[]{:S(2)}) collective-permute-start(bf16[2,128,512]{2,1,0:T(8,128)(2,1)S(1)} %get-tuple-element.20), channel_id=1, source_target_pairs={{0,2},{1,3},{2,0},{3,1},{4,6},{5,7},{6,4},{7,5},{8,10},{9,11},{10,... | collective-permute-start | bytes 786440 | tf_op jit(solution)/shard_map/ppermute | solution.py:188
  35.0 8.9 %collective-permute-start.12 = (bf16[2,128,512]{2,1,0:T(8,128)(2,1)S(1)}, bf16[2,128,512]{2,1,0:T(8,128)(2,1)S(1)}, u32[]{:S(2)}, u32[]{:S(2)}) collective-permute-start(bf16[2,128,512]{2,1,0:T(8,128)(2,1)S(1)} %get-tuple-element.22), channel_id=1, source_target_pairs={{0,2},{1,3},{2,0},{3,1},{4,6},{5,7},{6,4},{7,5},{8,10},{9,11},{10,... | collective-permute-start | bytes 786440 | tf_op jit(solution)/shard_map/ppermute | solution.py:188
  36.8 13.7 %collective-permute-start.8 = (bf16[1,128,512]{2,1,0:T(8,128)(2,1)S(1)}, bf16[1,128,512]{2,1,0:T(8,128)(2,1)S(1)}, u32[]{:S(2)}, u32[]{:S(2)}) collective-permute-start(bf16[1,128,512]{2,1,0:T(8,128)(2,1)S(1)} %slice.81), channel_id=1, source_target_pairs={{0,4},{1,5},{2,6},{3,7},{4,0},{5,1},{6,2},{7,3},{8,12},{9,13},{10,... | collective-permute-start | bytes 393224 | tf_op jit(solution)/shard_map/ppermute | solution.py:188
  44.0 7.0 %collective-permute-start.13 = (bf16[64,512]{1,0:T(8,128)(2,1)S(1)}, bf16[64,512]{1,0:T(8,128)(2,1)S(1)}, u32[]{:S(2)}, u32[]{:S(2)}) collective-permute-start(bf16[64,512]{1,0:T(8,128)(2,1)S(1)} %get-tuple-element.25), channel_id=1, source_target_pairs={{0,4},{1,5},{2,6},{3,7},{4,0},{5,1},{6,2},{7,3},{8,12},{9,13},{10,... | collective-permute-start | bytes 196616 | tf_op jit(solution)/shard_map/ppermute | solution.py:185
  44.7 11.1 %collective-permute-start.14 = (f32[128,512]{1,0:T(8,128)S(1)}, f32[128,512]{1,0:T(8,128)S(1)}, u32[]{:S(2)}, u32[]{:S(2)}) collective-permute-start(f32[128,512]{1,0:T(8,128)S(1)} %slice_bitcast_fusion), channel_id=1, source_target_pairs={{0,1},{1,0},{2,3},{3,2},{4,5},{5,4},{6,7},{7,6},{8,9},{9,8},{10,11... | collective-permute-start | bytes 786440 | tf_op jit(solution)/shard_map/ppermute | solution.py:184
  49.1 6.7 %collective-permute-start.15 = (bf16[64,512]{1,0:T(8,128)(2,1)S(1)}, bf16[64,512]{1,0:T(8,128)(2,1)S(1)}, u32[]{:S(2)}, u32[]{:S(2)}) collective-permute-start(bf16[64,512]{1,0:T(8,128)(2,1)S(1)} %get-tuple-element.26), channel_id=1, source_target_pairs={{0,5},{1,4},{2,7},{3,6},{4,1},{5,0},{6,3},{7,2},{8,13},{9,12},{10,... | collective-permute-start | bytes 196616 | tf_op jit(solution)/shard_map/ppermute | solution.py:186
  50.5 1.4 %collective-permute-start.9 = (bf16[64,512]{1,0:T(8,128)(2,1)S(1)}, bf16[64,512]{1,0:T(8,128)(2,1)S(1)}, u32[]{:S(2)}, u32[]{:S(2)}) collective-permute-start(bf16[64,512]{1,0:T(8,128)(2,1)S(1)} %get-tuple-element.28), channel_id=1, source_target_pairs={{0,1},{1,0},{2,3},{3,2},{4,5},{5,4},{6,7},{7,6},{8,9},{9,8},{10,11... | collective-permute-start | bytes 196616 | tf_op jit(solution)/shard_map/ppermute | solution.py:191

commit v7 on v6

--- a/solution.py
+++ b/solution.py
@@ -213,7 +213,7 @@
         far = [lax.ppermute(part, "sec", nexts) for part in parts]
     planes = [(d, d ^ 2) for d in range(terms)]
     near_first, near_second = (near[0], lax.ppermute(near[0], "term", planes)), near[1:]
-    far_first, far_second = (far[0], lax.ppermute(copy_after(far[0], near[1], near_first[1]), "term", planes)), far[1:]
+    far_first, far_second = (far[0], lax.ppermute(copy_after(far[0], near[1]), "term", planes)), far[1:]
 
     scalars = (place,)
     outs = []

time: 56.7 us -> 55.7 us (0.982)
  starting transfers between devices: 23.1 us -> 21 us
  waiting for transfers between devices: 23 us -> 24 us
    ppermute x1, waiting for transfers between devices: 2.46 us -> 0.21 us  [local(): far.append(lax.ppermute(copy_after(near[2], far[0]), 'sec', turn))]
    ppermute x1, waiting for transfers between devices: 0.36 us -> 2.61 us  [local(): lax.ppermute(copy_after(far[0], near[1]), 'term', planes)]
    ppermute x3, waiting for transfers between devices: 8.81 us -> 10.4 us  [local(): near = [lax.ppermute(part, 'sec', pairs) for part in parts]]
    ppermute x3, waiting for transfers between devices: 4.73 us -> 6.25 us  [sum_over_chips(): total = stay + lax.ppermute(gone, 'term', pairs).astype(jnp.float32)]
    ppermute x1, starting transfers between devices: 2.85 us -> 1.38 us  [local(): far.append(lax.ppermute(copy_after(near[2], far[0]), 'sec', turn))]
    ppermute x1, waiting for transfers between devices: 3.8 us -> 2.4 us  [sum_over_chips(): lax.ppermute(gone[0, half:], 'term', across).astype(jnp.float32)]
    ppermute x1, starting transfers between devices: 4.34 us -> 3.02 us  [sum_over_chips(): swapped = lax.ppermute(stay[0], 'term', cores)[half:]]
    ppermute x1, waiting for transfers between devices: 1.27 us -> 0.01 us  [local(): lax.ppermute(near[0], 'term', planes)]
  transfers between devices with their start and end apart: 16 -> 16, of which waited for: 10 -> 10; matrix products, arithmetic and copies ran while one was open for 0% -> 1% of each run, Pallas kernels for 9% -> 10%
where the time goes in v7:
time: 55.7 us; the launch traced here: 55.4 us
  waiting for transfers between devices  24 us (43%)
  starting transfers between devices  21 us (38%)
  Pallas kernels  7.8 us (14%)
  between operations  1.44 us (3%)
  other arithmetic  0.98 us (2%)
    ppermute x3, waiting for transfers between devices, local(): near = [lax.ppermute(part, 'sec', pairs) for part in parts]  10.4 us
    ppermute x3, waiting for transfers between devices, sum_over_chips(): total = stay + lax.ppermute(gone, 'term', pairs).astype(jnp.float32)  6.25 us
    pallas_call x2, Pallas kernels, piece(): call(body, 'piece', out_shape=outs, in_specs=[SMEM_SPEC] + [VMEM_SPEC] *...  5.29 us
    ppermute x3, starting transfers between devices, sum_over_chips(): total = stay + lax.ppermute(gone, 'term', pairs).astype(jnp.float32)  4.73 us
    ppermute x3, starting transfers between devices, local(): near = [lax.ppermute(part, 'sec', pairs) for part in parts]  3.9 us
    ppermute x1, starting transfers between devices, sum_over_chips(): swapped = lax.ppermute(stay[0], 'term', cores)[half:]  3.02 us
    ppermute x1, waiting for transfers between devices, local(): lax.ppermute(copy_after(far[0], near[1]), 'term', planes)  2.61 us
    ppermute x2, starting transfers between devices, local(): far = [lax.ppermute(part, 'sec', turn) for part in near[:2]]  2.55 us
  transfers between devices with their start and end apart: 16, of which 10 were waited for; matrix products, arithmetic and copies ran while one was open for 1% of the time, Pallas kernels for 10%

profile of v7, /device:TPU:1, one launch (start us, length us, event | category | flops | bytes accessed | tf_op | source)
XLA Modules:
  0.0 55.4 jit_solution(6639547864378131367)
XLA Ops:
  1.4 2.5 %cut.1 = (bf16[256,512]{1,0:T(8,128)(2,1)S(1)}, bf16[256,512]{1,0:T(8,128)(2,1)S(1)}, bf16[256,512]{1,0:T(8,128)(2,1)S(1)}, bf16[256,512]{1,0:T(8,128)(2,1)S(1)}, bf16[2064,512]{1,0:T(8,128)(2,1)S(1)}) custom-call(s32[6]{0:T(128)S(1)} %stack.57.place_ref.place, bf16[2,2,512,512]{3,2,1,0:T(8,128)(2,1)} %psi_ref.1, bf16[1,2,512,512]{3,2,1,0:T(8,128)(2,1)} %left_ref.1, ...), custom_call_target="tpu_custom_call" | custom-call | flops 1000 | bytes 1000 | tf_op jit(solution)/shard_map/cut/pallas_call | solution.py:57
  4.0 2.7 %collective-permute-start = (bf16[256,512]{1,0:T(8,128)(2,1)S(1)}, bf16[256,512]{1,0:T(8,128)(2,1)S(1)}, u32[]{:S(2)}, u32[]{:S(2)}) collective-permute-start(bf16[256,512]{1,0:T(8,128)(2,1)S(1)} %get-tuple-element.14.refs_8_), channel_id=1, source_target_pairs={{0,8},{8,0},{16,24},{24,16},{1,9},{9,1},{17,25},{25,17},{2,10},{10... | collective-permute-start | bytes 786440 | tf_op jit(solution)/shard_map/ppermute | solution.py:204
  6.7 6.6 %collective-permute-done.refs_0_ = bf16[256,512]{1,0:T(8,128)(2,1)S(1)} collective-permute-done((bf16[256,512]{1,0:T(8,128)(2,1)S(1)}, bf16[256,512]{1,0:T(8,128)(2,1)S(1)}, u32[]{:S(2)}, u32[]{:S(2)}) %collective-permute-start) | collective-permute-done | bytes 262176 | tf_op jit(solution)/shard_map/ppermute | solution.py:204
  13.2 1.3 %collective-permute-start.4 = (bf16[256,512]{1,0:T(8,128)(2,1)S(1)}, bf16[256,512]{1,0:T(8,128)(2,1)S(1)}, u32[]{:S(2)}, u32[]{:S(2)}) collective-permute-start(bf16[256,512]{1,0:T(8,128)(2,1)S(1)} %collective-permute-done.refs_0_), channel_id=1, source_target_pairs={{0,16},{8,24},{16,0},{24,8},{1,17},{9,25},{17,1},{25,9},{2,18},{10... | collective-permute-start | bytes 786440 | tf_op jit(solution)/shard_map/ppermute | solution.py:208
  14.6 1.2 %collective-permute-start.3 = (bf16[256,512]{1,0:T(8,128)(2,1)S(1)}, bf16[256,512]{1,0:T(8,128)(2,1)S(1)}, u32[]{:S(2)}, u32[]{:S(2)}) collective-permute-start(bf16[256,512]{1,0:T(8,128)(2,1)S(1)} %get-tuple-element.16.refs_7_), channel_id=1, source_target_pairs={{0,8},{8,0},{16,24},{24,16},{1,9},{9,1},{17,25},{25,17},{2,10},{10... | collective-permute-start | bytes 786440 | tf_op jit(solution)/shard_map/ppermute | solution.py:204
  15.8 1.3 %collective-permute-start.1 = (bf16[256,512]{1,0:T(8,128)(2,1)S(1)}, bf16[256,512]{1,0:T(8,128)(2,1)S(1)}, u32[]{:S(2)}, u32[]{:S(2)}) collective-permute-start(bf16[256,512]{1,0:T(8,128)(2,1)S(1)} %collective-permute-done.refs_0_), channel_id=1, source_target_pairs={{0,2},{1,3},{2,0},{3,1},{4,6},{5,7},{6,4},{7,5},{8,10},{9,11},{10,... | collective-permute-start | bytes 786440 | tf_op jit(solution)/shard_map/ppermute | solution.py:215
  17.1 1.8 %collective-permute-done.2.refs_0_.refs_2_ = bf16[256,512]{1,0:T(8,128)(2,1)S(1)} collective-permute-done((bf16[256,512]{1,0:T(8,128)(2,1)S(1)}, bf16[256,512]{1,0:T(8,128)(2,1)S(1)}, u32[]{:S(2)}, u32[]{:S(2)}) %collective-permute-start.2) | collective-permute-done | bytes 262176 | tf_op jit(solution)/shard_map/ppermute | solution.py:204
  18.9 1.3 %collective-permute-done.4.part_ref.refs_4_.refs_0_.refs_2_ = bf16[256,512]{1,0:T(8,128)(2,1)S(1)} collective-permute-done((bf16[256,512]{1,0:T(8,128)(2,1)S(1)}, bf16[256,512]{1,0:T(8,128)(2,1)S(1)}, u32[]{:S(2)}, u32[]{:S(2)}) %collective-permute-start.4) | collective-permute-done | bytes 262176 | tf_op jit(solution)/shard_map/ppermute | solution.py:208
  20.2 1.0 %collective-permute-start.5 = (bf16[256,512]{1,0:T(8,128)(2,1)S(1)}, bf16[256,512]{1,0:T(8,128)(2,1)S(1)}, u32[]{:S(2)}, u32[]{:S(2)}) collective-permute-start(bf16[256,512]{1,0:T(8,128)(2,1)S(1)} %copy_after.2), channel_id=1, source_target_pairs={{0,2},{1,3},{2,0},{3,1},{4,6},{5,7},{6,4},{7,5},{8,10},{9,11},{10,... | collective-permute-start | bytes 786440 | tf_op jit(solution)/shard_map/ppermute | solution.py:216
  21.2 1.2 %collective-permute-start.10 = (bf16[256,512]{1,0:T(8,128)(2,1)S(1)}, bf16[256,512]{1,0:T(8,128)(2,1)S(1)}, u32[]{:S(2)}, u32[]{:S(2)}) collective-permute-start(bf16[256,512]{1,0:T(8,128)(2,1)S(1)} %collective-permute-done.2.refs_0_.refs_2_), channel_id=1, source_target_pairs={{0,16},{8,24},{16,0},{24,8},{1,17},{9,25},{17,1},{25,9},{2,18},{10... | collective-permute-start | bytes 786440 | tf_op jit(solution)/shard_map/ppermute | solution.py:208
  22.5 2.0 %collective-permute-done.3.refs_3_.part_ref.refs_1_ = bf16[256,512]{1,0:T(8,128)(2,1)S(1)} collective-permute-done((bf16[256,512]{1,0:T(8,128)(2,1)S(1)}, bf16[256,512]{1,0:T(8,128)(2,1)S(1)}, u32[]{:S(2)}, u32[]{:S(2)}) %collective-permute-start.3) | collective-permute-done | bytes 262176 | tf_op jit(solution)/shard_map/ppermute | solution.py:204
  24.5 1.4 %collective-permute-start.11 = (bf16[256,512]{1,0:T(8,128)(2,1)S(1)}, bf16[256,512]{1,0:T(8,128)(2,1)S(1)}, u32[]{:S(2)}, u32[]{:S(2)}) collective-permute-start(bf16[256,512]{1,0:T(8,128)(2,1)S(1)} %copy_after.3), channel_id=1, source_target_pairs={{0,16},{8,24},{16,0},{24,8},{1,17},{9,25},{17,1},{25,9},{2,18},{10... | collective-permute-start | bytes 786440 | tf_op jit(solution)/shard_map/ppermute | solution.py:209
  25.9 2.6 %collective-permute-done.5.refs_5_.refs_3_ = bf16[256,512]{1,0:T(8,128)(2,1)S(1)} collective-permute-done((bf16[256,512]{1,0:T(8,128)(2,1)S(1)}, bf16[256,512]{1,0:T(8,128)(2,1)S(1)}, u32[]{:S(2)}, u32[]{:S(2)}) %collective-permute-start.5) | collective-permute-done | bytes 262176 | tf_op jit(solution)/shard_map/ppermute | solution.py:216
  28.5 2.9 %piece.2 = (f32[2,128,512]{2,1,0:T(8,128)}, bf16[2,128,512]{2,1,0:T(8,128)(2,1)S(1)}) custom-call(s32[6]{0:T(128)S(1)} %stack.57.place_ref.place, bf16[256,512]{1,0:T(8,128)(2,1)S(1)} %collective-permute-done.refs_0_, bf16[256,512]{1,0:T(8,128)(2,1)S(1)} %collective-permute-done.1.refs_1_, bf16[256,512]{1,0:T(8,128)(2,1)S(1)} %collective-permute-done.2.refs_0_.refs_2_, ...), custom_call_target="tpu_custom_call" | custom-call | flops 1000 | bytes 1000 | tf_op jit(solution)/shard_map/piece/pallas_call | solution.py:163
  31.4 1.2 %collective-permute-start.7 = (bf16[2,128,512]{2,1,0:T(8,128)(2,1)S(1)}, bf16[2,128,512]{2,1,0:T(8,128)(2,1)S(1)}, u32[]{:S(2)}, u32[]{:S(2)}) collective-permute-start(bf16[2,128,512]{2,1,0:T(8,128)(2,1)S(1)} %get-tuple-element.20), channel_id=1, source_target_pairs={{0,2},{1,3},{2,0},{3,1},{4,6},{5,7},{6,4},{7,5},{8,10},{9,11},{10,... | collective-permute-start | bytes 786440 | tf_op jit(solution)/shard_map/ppermute | solution.py:188
  32.8 2.4 %piece.3 = (f32[2,128,512]{2,1,0:T(8,128)S(1)}, bf16[2,128,512]{2,1,0:T(8,128)(2,1)S(1)}) custom-call(s32[6]{0:T(128)S(1)} %stack.57.place_ref.place, bf16[256,512]{1,0:T(8,128)(2,1)S(1)} %collective-permute-done.2.refs_0_.refs_2_, bf16[256,512]{1,0:T(8,128)(2,1)S(1)} %collective-permute-done.3.refs_3_.part_ref.refs_1_, ...), custom_call_target="tpu_custom_call" | custom-call | flops 1000 | bytes 1000 | tf_op jit(solution)/shard_map/piece/pallas_call | solution.py:163
  35.2 1.6 %collective-permute-start.12 = (bf16[2,128,512]{2,1,0:T(8,128)(2,1)S(1)}, bf16[2,128,512]{2,1,0:T(8,128)(2,1)S(1)}, u32[]{:S(2)}, u32[]{:S(2)}) collective-permute-start(bf16[2,128,512]{2,1,0:T(8,128)(2,1)S(1)} %get-tuple-element.22), channel_id=1, source_target_pairs={{0,2},{1,3},{2,0},{3,1},{4,6},{5,7},{6,4},{7,5},{8,10},{9,11},{10,... | collective-permute-start | bytes 786440 | tf_op jit(solution)/shard_map/ppermute | solution.py:188
  36.8 0.9 %collective-permute-done.7 = bf16[2,128,512]{2,1,0:T(8,128)(2,1)S(1)} collective-permute-done((bf16[2,128,512]{2,1,0:T(8,128)(2,1)S(1)}, bf16[2,128,512]{2,1,0:T(8,128)(2,1)S(1)}, u32[]{:S(2)}, u32[]{:S(2)}) %collective-permute-start.7) | collective-permute-done | bytes 262176 | tf_op jit(solution)/shard_map/ppermute | solution.py:188
  37.8 2.0 %collective-permute-start.8 = (bf16[1,128,512]{2,1,0:T(8,128)(2,1)S(1)}, bf16[1,128,512]{2,1,0:T(8,128)(2,1)S(1)}, u32[]{:S(2)}, u32[]{:S(2)}) collective-permute-start(bf16[1,128,512]{2,1,0:T(8,128)(2,1)S(1)} %slice.81), channel_id=1, source_target_pairs={{0,4},{1,5},{2,6},{3,7},{4,0},{5,1},{6,2},{7,3},{8,12},{9,13},{10,... | collective-permute-start | bytes 393224 | tf_op jit(solution)/shard_map/ppermute | solution.py:188
  39.8 5.3 %collective-permute-done.12 = bf16[2,128,512]{2,1,0:T(8,128)(2,1)S(1)} collective-permute-done((bf16[2,128,512]{2,1,0:T(8,128)(2,1)S(1)}, bf16[2,128,512]{2,1,0:T(8,128)(2,1)S(1)}, u32[]{:S(2)}, u32[]{:S(2)}) %collective-permute-start.12) | collective-permute-done | bytes 262176 | tf_op jit(solution)/shard_map/ppermute | solution.py:188
  45.2 1.6 %collective-permute-start.13 = (bf16[64,512]{1,0:T(8,128)(2,1)S(1)}, bf16[64,512]{1,0:T(8,128)(2,1)S(1)}, u32[]{:S(2)}, u32[]{:S(2)}) collective-permute-start(bf16[64,512]{1,0:T(8,128)(2,1)S(1)} %get-tuple-element.25), channel_id=1, source_target_pairs={{0,4},{1,5},{2,6},{3,7},{4,0},{5,1},{6,2},{7,3},{8,12},{9,13},{10,... | collective-permute-start | bytes 196616 | tf_op jit(solution)/shard_map/ppermute | solution.py:185
  46.9 3.0 %collective-permute-start.14 = (f32[128,512]{1,0:T(8,128)S(1)}, f32[128,512]{1,0:T(8,128)S(1)}, u32[]{:S(2)}, u32[]{:S(2)}) collective-permute-start(f32[128,512]{1,0:T(8,128)S(1)} %slice_bitcast_fusion), channel_id=1, source_target_pairs={{0,1},{1,0},{2,3},{3,2},{4,5},{5,4},{6,7},{7,6},{8,9},{9,8},{10,11... | collective-permute-start | bytes 786440 | tf_op jit(solution)/shard_map/ppermute | solution.py:184
  51.4 0.9 %collective-permute-done.9 = bf16[64,512]{1,0:T(8,128)(2,1)S(1)} collective-permute-done((bf16[64,512]{1,0:T(8,128)(2,1)S(1)}, bf16[64,512]{1,0:T(8,128)(2,1)S(1)}, u32[]{:S(2)}, u32[]{:S(2)}) %collective-permute-start.9) | collective-permute-done | bytes 65568 | tf_op jit(solution)/shard_map/ppermute | solution.py:191
  52.2 2.4 %collective-permute-done.15 = bf16[64,512]{1,0:T(8,128)(2,1)S(1)} collective-permute-done((bf16[64,512]{1,0:T(8,128)(2,1)S(1)}, bf16[64,512]{1,0:T(8,128)(2,1)S(1)}, u32[]{:S(2)}, u32[]{:S(2)}) %collective-permute-start.15) | collective-permute-done | bytes 65568 | tf_op jit(solution)/shard_map/ppermute | solution.py:186
  (28 shorter events, 2.9 us)
Async XLA Ops:
  3.9 24.6 %collective-permute-start.6 = (bf16[2064,512]{1,0:T(8,128)(2,1)S(1)}, bf16[2064,512]{1,0:T(8,128)(2,1)S(1)}, u32[]{:S(2)}, u32[]{:S(2)}) collective-permute-start(bf16[2064,512]{1,0:T(8,128)(2,1)S(1)} %get-tuple-element.18.refs_11_), channel_id=1, source_target_pairs={{0,1},{1,0},{2,3},{3,2},{4,5},{5,4},{6,7},{7,6},{8,9},{9,8},{10,11... | collective-permute-start | bytes 6340616 | tf_op jit(solution)/shard_map/ppermute | solution.py:205
  4.0 9.3 %collective-permute-start = (bf16[256,512]{1,0:T(8,128)(2,1)S(1)}, bf16[256,512]{1,0:T(8,128)(2,1)S(1)}, u32[]{:S(2)}, u32[]{:S(2)}) collective-permute-start(bf16[256,512]{1,0:T(8,128)(2,1)S(1)} %get-tuple-element.14.refs_8_), channel_id=1, source_target_pairs={{0,8},{8,0},{16,24},{24,16},{1,9},{9,1},{17,25},{25,17},{2,10},{10... | collective-permute-start | bytes 786440 | tf_op jit(solution)/shard_map/ppermute | solution.py:204
  6.7 12.2 %collective-permute-start.2 = (bf16[256,512]{1,0:T(8,128)(2,1)S(1)}, bf16[256,512]{1,0:T(8,128)(2,1)S(1)}, u32[]{:S(2)}, u32[]{:S(2)}) collective-permute-start(bf16[256,512]{1,0:T(8,128)(2,1)S(1)} %get-tuple-element.15.refs_6_), channel_id=1, source_target_pairs={{0,8},{8,0},{16,24},{24,16},{1,9},{9,1},{17,25},{25,17},{2,10},{10... | collective-permute-start | bytes 786440 | tf_op jit(solution)/shard_map/ppermute | solution.py:204
  13.2 6.9 %collective-permute-start.4 = (bf16[256,512]{1,0:T(8,128)(2,1)S(1)}, bf16[256,512]{1,0:T(8,128)(2,1)S(1)}, u32[]{:S(2)}, u32[]{:S(2)}) collective-permute-start(bf16[256,512]{1,0:T(8,128)(2,1)S(1)} %collective-permute-done.refs_0_), channel_id=1, source_target_pairs={{0,16},{8,24},{16,0},{24,8},{1,17},{9,25},{17,1},{25,9},{2,18},{10... | collective-permute-start | bytes 786440 | tf_op jit(solution)/shard_map/ppermute | solution.py:208
  14.6 9.9 %collective-permute-start.3 = (bf16[256,512]{1,0:T(8,128)(2,1)S(1)}, bf16[256,512]{1,0:T(8,128)(2,1)S(1)}, u32[]{:S(2)}, u32[]{:S(2)}) collective-permute-start(bf16[256,512]{1,0:T(8,128)(2,1)S(1)} %get-tuple-element.16.refs_7_), channel_id=1, source_target_pairs={{0,8},{8,0},{16,24},{24,16},{1,9},{9,1},{17,25},{25,17},{2,10},{10... | collective-permute-start | bytes 786440 | tf_op jit(solution)/shard_map/ppermute | solution.py:204
  15.8 10.1 %collective-permute-start.1 = (bf16[256,512]{1,0:T(8,128)(2,1)S(1)}, bf16[256,512]{1,0:T(8,128)(2,1)S(1)}, u32[]{:S(2)}, u32[]{:S(2)}) collective-permute-start(bf16[256,512]{1,0:T(8,128)(2,1)S(1)} %collective-permute-done.refs_0_), channel_id=1, source_target_pairs={{0,2},{1,3},{2,0},{3,1},{4,6},{5,7},{6,4},{7,5},{8,10},{9,11},{10,... | collective-permute-start | bytes 786440 | tf_op jit(solution)/shard_map/ppermute | solution.py:215
  20.2 8.3 %collective-permute-start.5 = (bf16[256,512]{1,0:T(8,128)(2,1)S(1)}, bf16[256,512]{1,0:T(8,128)(2,1)S(1)}, u32[]{:S(2)}, u32[]{:S(2)}) collective-permute-start(bf16[256,512]{1,0:T(8,128)(2,1)S(1)} %copy_after.2), channel_id=1, source_target_pairs={{0,2},{1,3},{2,0},{3,1},{4,6},{5,7},{6,4},{7,5},{8,10},{9,11},{10,... | collective-permute-start | bytes 786440 | tf_op jit(solution)/shard_map/ppermute | solution.py:216
  21.2 11.4 %collective-permute-start.10 = (bf16[256,512]{1,0:T(8,128)(2,1)S(1)}, bf16[256,512]{1,0:T(8,128)(2,1)S(1)}, u32[]{:S(2)}, u32[]{:S(2)}) collective-permute-start(bf16[256,512]{1,0:T(8,128)(2,1)S(1)} %collective-permute-done.2.refs_0_.refs_2_), channel_id=1, source_target_pairs={{0,16},{8,24},{16,0},{24,8},{1,17},{9,25},{17,1},{25,9},{2,18},{10... | collective-permute-start | bytes 786440 | tf_op jit(solution)/shard_map/ppermute | solution.py:208
  24.5 8.3 %collective-permute-start.11 = (bf16[256,512]{1,0:T(8,128)(2,1)S(1)}, bf16[256,512]{1,0:T(8,128)(2,1)S(1)}, u32[]{:S(2)}, u32[]{:S(2)}) collective-permute-start(bf16[256,512]{1,0:T(8,128)(2,1)S(1)} %copy_after.3), channel_id=1, source_target_pairs={{0,16},{8,24},{16,0},{24,8},{1,17},{9,25},{17,1},{25,9},{2,18},{10... | collective-permute-start | bytes 786440 | tf_op jit(solution)/shard_map/ppermute | solution.py:209
  31.4 6.3 %copy-start = (f32[2,128,512]{2,1,0:T(8,128)S(1)}, f32[2,128,512]{2,1,0:T(8,128)}, u32[]{:S(2)}) copy-start(f32[2,128,512]{2,1,0:T(8,128)} %get-tuple-element.19) | copy-start | bytes 1572868
  31.4 6.3 %collective-permute-start.7 = (bf16[2,128,512]{2,1,0:T(8,128)(2,1)S(1)}, bf16[2,128,512]{2,1,0:T(8,128)(2,1)S(1)}, u32[]{:S(2)}, u32[]{:S(2)}) collective-permute-start(bf16[2,128,512]{2,1,0:T(8,128)(2,1)S(1)} %get-tuple-element.20), channel_id=1, source_target_pairs={{0,2},{1,3},{2,0},{3,1},{4,6},{5,7},{6,4},{7,5},{8,10},{9,11},{10,... | collective-permute-start | bytes 786440 | tf_op jit(solution)/shard_map/ppermute | solution.py:188
  35.2 9.9 %collective-permute-start.12 = (bf16[2,128,512]{2,1,0:T(8,128)(2,1)S(1)}, bf16[2,128,512]{2,1,0:T(8,128)(2,1)S(1)}, u32[]{:S(2)}, u32[]{:S(2)}) collective-permute-start(bf16[2,128,512]{2,1,0:T(8,128)(2,1)S(1)} %get-tuple-element.22), channel_id=1, source_target_pairs={{0,2},{1,3},{2,0},{3,1},{4,6},{5,7},{6,4},{7,5},{8,10},{9,11},{10,... | collective-permute-start | bytes 786440 | tf_op jit(solution)/shard_map/ppermute | solution.py:188
  37.8 12.9 %collective-permute-start.8 = (bf16[1,128,512]{2,1,0:T(8,128)(2,1)S(1)}, bf16[1,128,512]{2,1,0:T(8,128)(2,1)S(1)}, u32[]{:S(2)}, u32[]{:S(2)}) collective-permute-start(bf16[1,128,512]{2,1,0:T(8,128)(2,1)S(1)} %slice.81), channel_id=1, source_target_pairs={{0,4},{1,5},{2,6},{3,7},{4,0},{5,1},{6,2},{7,3},{8,12},{9,13},{10,... | collective-permute-start | bytes 393224 | tf_op jit(solution)/shard_map/ppermute | solution.py:188
  45.2 6.1 %collective-permute-start.13 = (bf16[64,512]{1,0:T(8,128)(2,1)S(1)}, bf16[64,512]{1,0:T(8,128)(2,1)S(1)}, u32[]{:S(2)}, u32[]{:S(2)}) collective-permute-start(bf16[64,512]{1,0:T(8,128)(2,1)S(1)} %get-tuple-element.25), channel_id=1, source_target_pairs={{0,4},{1,5},{2,6},{3,7},{4,0},{5,1},{6,2},{7,3},{8,12},{9,13},{10,... | collective-permute-start | bytes 196616 | tf_op jit(solution)/shard_map/ppermute | solution.py:185
  46.9 7.8 %collective-permute-start.14 = (f32[128,512]{1,0:T(8,128)S(1)}, f32[128,512]{1,0:T(8,128)S(1)}, u32[]{:S(2)}, u32[]{:S(2)}) collective-permute-start(f32[128,512]{1,0:T(8,128)S(1)} %slice_bitcast_fusion), channel_id=1, source_target_pairs={{0,1},{1,0},{2,3},{3,2},{4,5},{5,4},{6,7},{7,6},{8,9},{9,8},{10,11... | collective-permute-start | bytes 786440 | tf_op jit(solution)/shard_map/ppermute | solution.py:184
  49.9 4.7 %collective-permute-start.15 = (bf16[64,512]{1,0:T(8,128)(2,1)S(1)}, bf16[64,512]{1,0:T(8,128)(2,1)S(1)}, u32[]{:S(2)}, u32[]{:S(2)}) collective-permute-start(bf16[64,512]{1,0:T(8,128)(2,1)S(1)} %get-tuple-element.26), channel_id=1, source_target_pairs={{0,5},{1,4},{2,7},{3,6},{4,1},{5,0},{6,3},{7,2},{8,13},{9,12},{10,... | collective-permute-start | bytes 196616 | tf_op jit(solution)/shard_map/ppermute | solution.py:186
  50.8 1.4 %collective-permute-start.9 = (bf16[64,512]{1,0:T(8,128)(2,1)S(1)}, bf16[64,512]{1,0:T(8,128)(2,1)S(1)}, u32[]{:S(2)}, u32[]{:S(2)}) collective-permute-start(bf16[64,512]{1,0:T(8,128)(2,1)S(1)} %get-tuple-element.28), channel_id=1, source_target_pairs={{0,1},{1,0},{2,3},{3,2},{4,5},{5,4},{6,7},{7,6},{8,9},{9,8},{10,11... | collective-permute-start | bytes 196616 | tf_op jit(solution)/shard_map/ppermute | solution.py:191

commit v8 on v7

--- a/solution.py
+++ b/solution.py
@@ -182,8 +182,8 @@
         if direct and n == len(bits) - 1:
             across = [(d, d ^ (2 << bit) ^ 1) for d in range(terms)]
             swapped = lax.ppermute(stay[0], "term", cores)[half:]
+            others = swapped + lax.ppermute(gone[0, half:], "term", across).astype(jnp.float32)
             mine = stay[0, :half] + lax.ppermute(gone[0, :half], "term", pairs).astype(jnp.float32)
-            others = swapped + lax.ppermute(gone[0, half:], "term", across).astype(jnp.float32)
             return mine.astype(jnp.bfloat16), others.astype(jnp.bfloat16)
         total = stay + lax.ppermute(gone, "term", pairs).astype(jnp.float32)
         stay, gone = total[::2], total[1::2].astype(jnp.bfloat16)
@@ -213,7 +213,7 @@
         far = [lax.ppermute(part, "sec", nexts) for part in parts]
     planes = [(d, d ^ 2) for d in range(terms)]
     near_first, near_second = (near[0], lax.ppermute(near[0], "term", planes)), near[1:]
-    far_first, far_second = (far[0], lax.ppermute(copy_after(far[0], near[1]), "term", planes)), far[1:]
+    far_first, far_second = (far[0], lax.ppermute(copy_after(far[0], near[1], pack1), "term", planes)), far[1:]
 
     scalars = (place,)
     outs = []

time: 55.7 us -> 55.7 us (level)
  no operation moved by 1% of the time
where the time goes in v8:
time: 55.7 us; the launch traced here: 55.4 us
  waiting for transfers between devices  24 us (43%)
  starting transfers between devices  21.1 us (38%)
  Pallas kernels  7.81 us (14%)
  between operations  1.44 us (3%)
  other arithmetic  0.98 us (2%)
    ppermute x3, waiting for transfers between devices, local(): near = [lax.ppermute(part, 'sec', pairs) for part in parts]  10.4 us
    ppermute x3, waiting for transfers between devices, sum_over_chips(): total = stay + lax.ppermute(gone, 'term', pairs).astype(jnp.float32)  6.22 us
    pallas_call x2, Pallas kernels, piece(): call(body, 'piece', out_shape=outs, in_specs=[SMEM_SPEC] + [VMEM_SPEC] *...  5.29 us
    ppermute x3, starting transfers between devices, sum_over_chips(): total = stay + lax.ppermute(gone, 'term', pairs).astype(jnp.float32)  4.77 us
    ppermute x3, starting transfers between devices, local(): near = [lax.ppermute(part, 'sec', pairs) for part in parts]  3.9 us
    ppermute x1, starting transfers between devices, sum_over_chips(): swapped = lax.ppermute(stay[0], 'term', cores)[half:]  3.02 us
    ppermute x1, waiting for transfers between devices, local(): lax.ppermute(copy_after(far[0], near[1], pack1), 'term', planes)  2.6 us
    ppermute x2, starting transfers between devices, local(): far = [lax.ppermute(part, 'sec', turn) for part in near[:2]]  2.55 us
  transfers between devices with their start and end apart: 16, of which 10 were waited for; matrix products, arithmetic and copies ran while one was open for 1% of the time, Pallas kernels for 10%

profile of v8, /device:TPU:1, one launch (start us, length us, event | category | flops | bytes accessed | tf_op | source)
XLA Modules:
  0.0 55.4 jit_solution(14968962315791954344)
XLA Ops:
  1.4 2.5 %cut.1 = (bf16[256,512]{1,0:T(8,128)(2,1)S(1)}, bf16[256,512]{1,0:T(8,128)(2,1)S(1)}, bf16[256,512]{1,0:T(8,128)(2,1)S(1)}, bf16[256,512]{1,0:T(8,128)(2,1)S(1)}, bf16[2064,512]{1,0:T(8,128)(2,1)S(1)}) custom-call(s32[6]{0:T(128)S(1)} %stack.57.place_ref.place, bf16[2,2,512,512]{3,2,1,0:T(8,128)(2,1)} %psi_ref.1, bf16[1,2,512,512]{3,2,1,0:T(8,128)(2,1)} %left_ref.1, ...), custom_call_target="tpu_custom_call" | custom-call | flops 1000 | bytes 1000 | tf_op jit(solution)/shard_map/cut/pallas_call | solution.py:57
  4.0 2.7 %collective-permute-start = (bf16[256,512]{1,0:T(8,128)(2,1)S(1)}, bf16[256,512]{1,0:T(8,128)(2,1)S(1)}, u32[]{:S(2)}, u32[]{:S(2)}) collective-permute-start(bf16[256,512]{1,0:T(8,128)(2,1)S(1)} %get-tuple-element.14.refs_8_), channel_id=1, source_target_pairs={{0,8},{8,0},{16,24},{24,16},{1,9},{9,1},{17,25},{25,17},{2,10},{10... | collective-permute-start | bytes 786440 | tf_op jit(solution)/shard_map/ppermute | solution.py:204
  6.7 6.6 %collective-permute-done.refs_0_ = bf16[256,512]{1,0:T(8,128)(2,1)S(1)} collective-permute-done((bf16[256,512]{1,0:T(8,128)(2,1)S(1)}, bf16[256,512]{1,0:T(8,128)(2,1)S(1)}, u32[]{:S(2)}, u32[]{:S(2)}) %collective-permute-start) | collective-permute-done | bytes 262176 | tf_op jit(solution)/shard_map/ppermute | solution.py:204
  13.2 1.3 %collective-permute-start.4 = (bf16[256,512]{1,0:T(8,128)(2,1)S(1)}, bf16[256,512]{1,0:T(8,128)(2,1)S(1)}, u32[]{:S(2)}, u32[]{:S(2)}) collective-permute-start(bf16[256,512]{1,0:T(8,128)(2,1)S(1)} %collective-permute-done.refs_0_), channel_id=1, source_target_pairs={{0,16},{8,24},{16,0},{24,8},{1,17},{9,25},{17,1},{25,9},{2,18},{10... | collective-permute-start | bytes 786440 | tf_op jit(solution)/shard_map/ppermute | solution.py:208
  14.6 1.2 %collective-permute-start.3 = (bf16[256,512]{1,0:T(8,128)(2,1)S(1)}, bf16[256,512]{1,0:T(8,128)(2,1)S(1)}, u32[]{:S(2)}, u32[]{:S(2)}) collective-permute-start(bf16[256,512]{1,0:T(8,128)(2,1)S(1)} %get-tuple-element.16.refs_7_), channel_id=1, source_target_pairs={{0,8},{8,0},{16,24},{24,16},{1,9},{9,1},{17,25},{25,17},{2,10},{10... | collective-permute-start | bytes 786440 | tf_op jit(solution)/shard_map/ppermute | solution.py:204
  15.8 1.3 %collective-permute-start.1 = (bf16[256,512]{1,0:T(8,128)(2,1)S(1)}, bf16[256,512]{1,0:T(8,128)(2,1)S(1)}, u32[]{:S(2)}, u32[]{:S(2)}) collective-permute-start(bf16[256,512]{1,0:T(8,128)(2,1)S(1)} %collective-permute-done.refs_0_), channel_id=1, source_target_pairs={{0,2},{1,3},{2,0},{3,1},{4,6},{5,7},{6,4},{7,5},{8,10},{9,11},{10,... | collective-permute-start | bytes 786440 | tf_op jit(solution)/shard_map/ppermute | solution.py:215
  17.1 1.8 %collective-permute-done.2.refs_0_.refs_2_ = bf16[256,512]{1,0:T(8,128)(2,1)S(1)} collective-permute-done((bf16[256,512]{1,0:T(8,128)(2,1)S(1)}, bf16[256,512]{1,0:T(8,128)(2,1)S(1)}, u32[]{:S(2)}, u32[]{:S(2)}) %collective-permute-start.2) | collective-permute-done | bytes 262176 | tf_op jit(solution)/shard_map/ppermute | solution.py:204
  18.9 1.3 %collective-permute-done.4.part_ref.refs_4_.refs_0_.refs_2_ = bf16[256,512]{1,0:T(8,128)(2,1)S(1)} collective-permute-done((bf16[256,512]{1,0:T(8,128)(2,1)S(1)}, bf16[256,512]{1,0:T(8,128)(2,1)S(1)}, u32[]{:S(2)}, u32[]{:S(2)}) %collective-permute-start.4) | collective-permute-done | bytes 262176 | tf_op jit(solution)/shard_map/ppermute | solution.py:208
  20.2 1.0 %collective-permute-start.6 = (bf16[256,512]{1,0:T(8,128)(2,1)S(1)}, bf16[256,512]{1,0:T(8,128)(2,1)S(1)}, u32[]{:S(2)}, u32[]{:S(2)}) collective-permute-start(bf16[256,512]{1,0:T(8,128)(2,1)S(1)} %copy_after.2), channel_id=1, source_target_pairs={{0,2},{1,3},{2,0},{3,1},{4,6},{5,7},{6,4},{7,5},{8,10},{9,11},{10,... | collective-permute-start | bytes 786440 | tf_op jit(solution)/shard_map/ppermute | solution.py:216
  21.2 1.2 %collective-permute-start.10 = (bf16[256,512]{1,0:T(8,128)(2,1)S(1)}, bf16[256,512]{1,0:T(8,128)(2,1)S(1)}, u32[]{:S(2)}, u32[]{:S(2)}) collective-permute-start(bf16[256,512]{1,0:T(8,128)(2,1)S(1)} %collective-permute-done.2.refs_0_.refs_2_), channel_id=1, source_target_pairs={{0,16},{8,24},{16,0},{24,8},{1,17},{9,25},{17,1},{25,9},{2,18},{10... | collective-permute-start | bytes 786440 | tf_op jit(solution)/shard_map/ppermute | solution.py:208
  22.5 2.0 %collective-permute-done.3.refs_3_.part_ref.refs_1_ = bf16[256,512]{1,0:T(8,128)(2,1)S(1)} collective-permute-done((bf16[256,512]{1,0:T(8,128)(2,1)S(1)}, bf16[256,512]{1,0:T(8,128)(2,1)S(1)}, u32[]{:S(2)}, u32[]{:S(2)}) %collective-permute-start.3) | collective-permute-done | bytes 262176 | tf_op jit(solution)/shard_map/ppermute | solution.py:204
  24.5 1.4 %collective-permute-start.11 = (bf16[256,512]{1,0:T(8,128)(2,1)S(1)}, bf16[256,512]{1,0:T(8,128)(2,1)S(1)}, u32[]{:S(2)}, u32[]{:S(2)}) collective-permute-start(bf16[256,512]{1,0:T(8,128)(2,1)S(1)} %copy_after.3), channel_id=1, source_target_pairs={{0,16},{8,24},{16,0},{24,8},{1,17},{9,25},{17,1},{25,9},{2,18},{10... | collective-permute-start | bytes 786440 | tf_op jit(solution)/shard_map/ppermute | solution.py:209
  25.9 2.6 %collective-permute-done.6.refs_5_.refs_3_ = bf16[256,512]{1,0:T(8,128)(2,1)S(1)} collective-permute-done((bf16[256,512]{1,0:T(8,128)(2,1)S(1)}, bf16[256,512]{1,0:T(8,128)(2,1)S(1)}, u32[]{:S(2)}, u32[]{:S(2)}) %collective-permute-start.6) | collective-permute-done | bytes 262176 | tf_op jit(solution)/shard_map/ppermute | solution.py:216
  28.5 2.9 %piece.2 = (f32[2,128,512]{2,1,0:T(8,128)}, bf16[2,128,512]{2,1,0:T(8,128)(2,1)S(1)}) custom-call(s32[6]{0:T(128)S(1)} %stack.57.place_ref.place, bf16[256,512]{1,0:T(8,128)(2,1)S(1)} %collective-permute-done.refs_0_, bf16[256,512]{1,0:T(8,128)(2,1)S(1)} %collective-permute-done.1.refs_1_, bf16[256,512]{1,0:T(8,128)(2,1)S(1)} %collective-permute-done.2.refs_0_.refs_2_, ...), custom_call_target="tpu_custom_call" | custom-call | flops 1000 | bytes 1000 | tf_op jit(solution)/shard_map/piece/pallas_call | solution.py:163
  31.4 1.2 %collective-permute-start.7 = (bf16[2,128,512]{2,1,0:T(8,128)(2,1)S(1)}, bf16[2,128,512]{2,1,0:T(8,128)(2,1)S(1)}, u32[]{:S(2)}, u32[]{:S(2)}) collective-permute-start(bf16[2,128,512]{2,1,0:T(8,128)(2,1)S(1)} %get-tuple-element.20), channel_id=1, source_target_pairs={{0,2},{1,3},{2,0},{3,1},{4,6},{5,7},{6,4},{7,5},{8,10},{9,11},{10,... | collective-permute-start | bytes 786440 | tf_op jit(solution)/shard_map/ppermute | solution.py:188
  32.8 2.4 %piece.3 = (f32[2,128,512]{2,1,0:T(8,128)S(1)}, bf16[2,128,512]{2,1,0:T(8,128)(2,1)S(1)}) custom-call(s32[6]{0:T(128)S(1)} %stack.57.place_ref.place, bf16[256,512]{1,0:T(8,128)(2,1)S(1)} %collective-permute-done.2.refs_0_.refs_2_, bf16[256,512]{1,0:T(8,128)(2,1)S(1)} %collective-permute-done.3.refs_3_.part_ref.refs_1_, ...), custom_call_target="tpu_custom_call" | custom-call | flops 1000 | bytes 1000 | tf_op jit(solution)/shard_map/piece/pallas_call | solution.py:163
  35.2 1.6 %collective-permute-start.12 = (bf16[2,128,512]{2,1,0:T(8,128)(2,1)S(1)}, bf16[2,128,512]{2,1,0:T(8,128)(2,1)S(1)}, u32[]{:S(2)}, u32[]{:S(2)}) collective-permute-start(bf16[2,128,512]{2,1,0:T(8,128)(2,1)S(1)} %get-tuple-element.22), channel_id=1, source_target_pairs={{0,2},{1,3},{2,0},{3,1},{4,6},{5,7},{6,4},{7,5},{8,10},{9,11},{10,... | collective-permute-start | bytes 786440 | tf_op jit(solution)/shard_map/ppermute | solution.py:188
  36.8 0.9 %collective-permute-done.7 = bf16[2,128,512]{2,1,0:T(8,128)(2,1)S(1)} collective-permute-done((bf16[2,128,512]{2,1,0:T(8,128)(2,1)S(1)}, bf16[2,128,512]{2,1,0:T(8,128)(2,1)S(1)}, u32[]{:S(2)}, u32[]{:S(2)}) %collective-permute-start.7) | collective-permute-done | bytes 262176 | tf_op jit(solution)/shard_map/ppermute | solution.py:188
  37.8 2.0 %collective-permute-start.8 = (bf16[1,128,512]{2,1,0:T(8,128)(2,1)S(1)}, bf16[1,128,512]{2,1,0:T(8,128)(2,1)S(1)}, u32[]{:S(2)}, u32[]{:S(2)}) collective-permute-start(bf16[1,128,512]{2,1,0:T(8,128)(2,1)S(1)} %slice.81), channel_id=1, source_target_pairs={{0,4},{1,5},{2,6},{3,7},{4,0},{5,1},{6,2},{7,3},{8,12},{9,13},{10,... | collective-permute-start | bytes 393224 | tf_op jit(solution)/shard_map/ppermute | solution.py:188
  39.8 5.3 %collective-permute-done.12 = bf16[2,128,512]{2,1,0:T(8,128)(2,1)S(1)} collective-permute-done((bf16[2,128,512]{2,1,0:T(8,128)(2,1)S(1)}, bf16[2,128,512]{2,1,0:T(8,128)(2,1)S(1)}, u32[]{:S(2)}, u32[]{:S(2)}) %collective-permute-start.12) | collective-permute-done | bytes 262176 | tf_op jit(solution)/shard_map/ppermute | solution.py:188
  45.2 1.6 %collective-permute-start.13 = (bf16[64,512]{1,0:T(8,128)(2,1)S(1)}, bf16[64,512]{1,0:T(8,128)(2,1)S(1)}, u32[]{:S(2)}, u32[]{:S(2)}) collective-permute-start(bf16[64,512]{1,0:T(8,128)(2,1)S(1)} %get-tuple-element.25), channel_id=1, source_target_pairs={{0,4},{1,5},{2,6},{3,7},{4,0},{5,1},{6,2},{7,3},{8,12},{9,13},{10,... | collective-permute-start | bytes 196616 | tf_op jit(solution)/shard_map/ppermute | solution.py:186
  46.9 3.0 %collective-permute-start.14 = (f32[128,512]{1,0:T(8,128)S(1)}, f32[128,512]{1,0:T(8,128)S(1)}, u32[]{:S(2)}, u32[]{:S(2)}) collective-permute-start(f32[128,512]{1,0:T(8,128)S(1)} %slice_bitcast_fusion), channel_id=1, source_target_pairs={{0,1},{1,0},{2,3},{3,2},{4,5},{5,4},{6,7},{7,6},{8,9},{9,8},{10,11... | collective-permute-start | bytes 786440 | tf_op jit(solution)/shard_map/ppermute | solution.py:184
  51.4 0.9 %collective-permute-done.9 = bf16[64,512]{1,0:T(8,128)(2,1)S(1)} collective-permute-done((bf16[64,512]{1,0:T(8,128)(2,1)S(1)}, bf16[64,512]{1,0:T(8,128)(2,1)S(1)}, u32[]{:S(2)}, u32[]{:S(2)}) %collective-permute-start.9) | collective-permute-done | bytes 65568 | tf_op jit(solution)/shard_map/ppermute | solution.py:191
  52.3 2.4 %collective-permute-done.15 = bf16[64,512]{1,0:T(8,128)(2,1)S(1)} collective-permute-done((bf16[64,512]{1,0:T(8,128)(2,1)S(1)}, bf16[64,512]{1,0:T(8,128)(2,1)S(1)}, u32[]{:S(2)}, u32[]{:S(2)}) %collective-permute-start.15) | collective-permute-done | bytes 65568 | tf_op jit(solution)/shard_map/ppermute | solution.py:185
  (28 shorter events, 2.9 us)
Async XLA Ops:
  3.9 16.3 %collective-permute-start.5 = (bf16[2064,512]{1,0:T(8,128)(2,1)S(1)}, bf16[2064,512]{1,0:T(8,128)(2,1)S(1)}, u32[]{:S(2)}, u32[]{:S(2)}) collective-permute-start(bf16[2064,512]{1,0:T(8,128)(2,1)S(1)} %get-tuple-element.17.refs_11_), channel_id=1, source_target_pairs={{0,1},{1,0},{2,3},{3,2},{4,5},{5,4},{6,7},{7,6},{8,9},{9,8},{10,11... | collective-permute-start | bytes 6340616 | tf_op jit(solution)/shard_map/ppermute | solution.py:205
  4.0 9.3 %collective-permute-start = (bf16[256,512]{1,0:T(8,128)(2,1)S(1)}, bf16[256,512]{1,0:T(8,128)(2,1)S(1)}, u32[]{:S(2)}, u32[]{:S(2)}) collective-permute-start(bf16[256,512]{1,0:T(8,128)(2,1)S(1)} %get-tuple-element.14.refs_8_), channel_id=1, source_target_pairs={{0,8},{8,0},{16,24},{24,16},{1,9},{9,1},{17,25},{25,17},{2,10},{10... | collective-permute-start | bytes 786440 | tf_op jit(solution)/shard_map/ppermute | solution.py:204
  6.7 12.2 %collective-permute-start.2 = (bf16[256,512]{1,0:T(8,128)(2,1)S(1)}, bf16[256,512]{1,0:T(8,128)(2,1)S(1)}, u32[]{:S(2)}, u32[]{:S(2)}) collective-permute-start(bf16[256,512]{1,0:T(8,128)(2,1)S(1)} %get-tuple-element.15.refs_6_), channel_id=1, source_target_pairs={{0,8},{8,0},{16,24},{24,16},{1,9},{9,1},{17,25},{25,17},{2,10},{10... | collective-permute-start | bytes 786440 | tf_op jit(solution)/shard_map/ppermute | solution.py:204
  13.2 6.9 %collective-permute-start.4 = (bf16[256,512]{1,0:T(8,128)(2,1)S(1)}, bf16[256,512]{1,0:T(8,128)(2,1)S(1)}, u32[]{:S(2)}, u32[]{:S(2)}) collective-permute-start(bf16[256,512]{1,0:T(8,128)(2,1)S(1)} %collective-permute-done.refs_0_), channel_id=1, source_target_pairs={{0,16},{8,24},{16,0},{24,8},{1,17},{9,25},{17,1},{25,9},{2,18},{10... | collective-permute-start | bytes 786440 | tf_op jit(solution)/shard_map/ppermute | solution.py:208
  14.6 9.9 %collective-permute-start.3 = (bf16[256,512]{1,0:T(8,128)(2,1)S(1)}, bf16[256,512]{1,0:T(8,128)(2,1)S(1)}, u32[]{:S(2)}, u32[]{:S(2)}) collective-permute-start(bf16[256,512]{1,0:T(8,128)(2,1)S(1)} %get-tuple-element.16.refs_7_), channel_id=1, source_target_pairs={{0,8},{8,0},{16,24},{24,16},{1,9},{9,1},{17,25},{25,17},{2,10},{10... | collective-permute-start | bytes 786440 | tf_op jit(solution)/shard_map/ppermute | solution.py:204
  15.8 10.1 %collective-permute-start.1 = (bf16[256,512]{1,0:T(8,128)(2,1)S(1)}, bf16[256,512]{1,0:T(8,128)(2,1)S(1)}, u32[]{:S(2)}, u32[]{:S(2)}) collective-permute-start(bf16[256,512]{1,0:T(8,128)(2,1)S(1)} %collective-permute-done.refs_0_), channel_id=1, source_target_pairs={{0,2},{1,3},{2,0},{3,1},{4,6},{5,7},{6,4},{7,5},{8,10},{9,11},{10,... | collective-permute-start | bytes 786440 | tf_op jit(solution)/shard_map/ppermute | solution.py:215
  20.2 8.3 %collective-permute-start.6 = (bf16[256,512]{1,0:T(8,128)(2,1)S(1)}, bf16[256,512]{1,0:T(8,128)(2,1)S(1)}, u32[]{:S(2)}, u32[]{:S(2)}) collective-permute-start(bf16[256,512]{1,0:T(8,128)(2,1)S(1)} %copy_after.2), channel_id=1, source_target_pairs={{0,2},{1,3},{2,0},{3,1},{4,6},{5,7},{6,4},{7,5},{8,10},{9,11},{10,... | collective-permute-start | bytes 786440 | tf_op jit(solution)/shard_map/ppermute | solution.py:216
  21.2 11.4 %collective-permute-start.10 = (bf16[256,512]{1,0:T(8,128)(2,1)S(1)}, bf16[256,512]{1,0:T(8,128)(2,1)S(1)}, u32[]{:S(2)}, u32[]{:S(2)}) collective-permute-start(bf16[256,512]{1,0:T(8,128)(2,1)S(1)} %collective-permute-done.2.refs_0_.refs_2_), channel_id=1, source_target_pairs={{0,16},{8,24},{16,0},{24,8},{1,17},{9,25},{17,1},{25,9},{2,18},{10... | collective-permute-start | bytes 786440 | tf_op jit(solution)/shard_map/ppermute | solution.py:208
  24.5 8.3 %collective-permute-start.11 = (bf16[256,512]{1,0:T(8,128)(2,1)S(1)}, bf16[256,512]{1,0:T(8,128)(2,1)S(1)}, u32[]{:S(2)}, u32[]{:S(2)}) collective-permute-start(bf16[256,512]{1,0:T(8,128)(2,1)S(1)} %copy_after.3), channel_id=1, source_target_pairs={{0,16},{8,24},{16,0},{24,8},{1,17},{9,25},{17,1},{25,9},{2,18},{10... | collective-permute-start | bytes 786440 | tf_op jit(solution)/shard_map/ppermute | solution.py:209
  31.4 6.3 %copy-start = (f32[2,128,512]{2,1,0:T(8,128)S(1)}, f32[2,128,512]{2,1,0:T(8,128)}, u32[]{:S(2)}) copy-start(f32[2,128,512]{2,1,0:T(8,128)} %get-tuple-element.19) | copy-start | bytes 1572868
  31.4 6.3 %collective-permute-start.7 = (bf16[2,128,512]{2,1,0:T(8,128)(2,1)S(1)}, bf16[2,128,512]{2,1,0:T(8,128)(2,1)S(1)}, u32[]{:S(2)}, u32[]{:S(2)}) collective-permute-start(bf16[2,128,512]{2,1,0:T(8,128)(2,1)S(1)} %get-tuple-element.20), channel_id=1, source_target_pairs={{0,2},{1,3},{2,0},{3,1},{4,6},{5,7},{6,4},{7,5},{8,10},{9,11},{10,... | collective-permute-start | bytes 786440 | tf_op jit(solution)/shard_map/ppermute | solution.py:188
  35.2 9.9 %collective-permute-start.12 = (bf16[2,128,512]{2,1,0:T(8,128)(2,1)S(1)}, bf16[2,128,512]{2,1,0:T(8,128)(2,1)S(1)}, u32[]{:S(2)}, u32[]{:S(2)}) collective-permute-start(bf16[2,128,512]{2,1,0:T(8,128)(2,1)S(1)} %get-tuple-element.22), channel_id=1, source_target_pairs={{0,2},{1,3},{2,0},{3,1},{4,6},{5,7},{6,4},{7,5},{8,10},{9,11},{10,... | collective-permute-start | bytes 786440 | tf_op jit(solution)/shard_map/ppermute | solution.py:188
  37.8 13.0 %collective-permute-start.8 = (bf16[1,128,512]{2,1,0:T(8,128)(2,1)S(1)}, bf16[1,128,512]{2,1,0:T(8,128)(2,1)S(1)}, u32[]{:S(2)}, u32[]{:S(2)}) collective-permute-start(bf16[1,128,512]{2,1,0:T(8,128)(2,1)S(1)} %slice.81), channel_id=1, source_target_pairs={{0,4},{1,5},{2,6},{3,7},{4,0},{5,1},{6,2},{7,3},{8,12},{9,13},{10,... | collective-permute-start | bytes 393224 | tf_op jit(solution)/shard_map/ppermute | solution.py:188
  45.2 6.1 %collective-permute-start.13 = (bf16[64,512]{1,0:T(8,128)(2,1)S(1)}, bf16[64,512]{1,0:T(8,128)(2,1)S(1)}, u32[]{:S(2)}, u32[]{:S(2)}) collective-permute-start(bf16[64,512]{1,0:T(8,128)(2,1)S(1)} %get-tuple-element.25), channel_id=1, source_target_pairs={{0,4},{1,5},{2,6},{3,7},{4,0},{5,1},{6,2},{7,3},{8,12},{9,13},{10,... | collective-permute-start | bytes 196616 | tf_op jit(solution)/shard_map/ppermute | solution.py:186
  46.9 7.8 %collective-permute-start.14 = (f32[128,512]{1,0:T(8,128)S(1)}, f32[128,512]{1,0:T(8,128)S(1)}, u32[]{:S(2)}, u32[]{:S(2)}) collective-permute-start(f32[128,512]{1,0:T(8,128)S(1)} %slice_bitcast_fusion), channel_id=1, source_target_pairs={{0,1},{1,0},{2,3},{3,2},{4,5},{5,4},{6,7},{7,6},{8,9},{9,8},{10,11... | collective-permute-start | bytes 786440 | tf_op jit(solution)/shard_map/ppermute | solution.py:184
  49.9 4.7 %collective-permute-start.15 = (bf16[64,512]{1,0:T(8,128)(2,1)S(1)}, bf16[64,512]{1,0:T(8,128)(2,1)S(1)}, u32[]{:S(2)}, u32[]{:S(2)}) collective-permute-start(bf16[64,512]{1,0:T(8,128)(2,1)S(1)} %get-tuple-element.26), channel_id=1, source_target_pairs={{0,5},{1,4},{2,7},{3,6},{4,1},{5,0},{6,3},{7,2},{8,13},{9,12},{10,... | collective-permute-start | bytes 196616 | tf_op jit(solution)/shard_map/ppermute | solution.py:185
  50.8 1.4 %collective-permute-start.9 = (bf16[64,512]{1,0:T(8,128)(2,1)S(1)}, bf16[64,512]{1,0:T(8,128)(2,1)S(1)}, u32[]{:S(2)}, u32[]{:S(2)}) collective-permute-start(bf16[64,512]{1,0:T(8,128)(2,1)S(1)} %get-tuple-element.28), channel_id=1, source_target_pairs={{0,1},{1,0},{2,3},{3,2},{4,5},{5,4},{6,7},{7,6},{8,9},{9,8},{10,11... | collective-permute-start | bytes 196616 | tf_op jit(solution)/shard_map/ppermute | solution.py:191
